TPU v7x, 256 devices: a whole 4x4x8 slice. The times are simulated.
256 devices in a mesh: seq: 64 (over z, y, core), head: 4 (over x).
Axes of the slice: x: 4, y: 4, z: 8, core: 2. Of those that a mesh axis runs over, the one named last changes fastest.
Arguments:
- query: bfloat16 [256, 5120], P(('seq', 'head')), may hold values from -48 to 48
- query_tangent: bfloat16 [256, 5120], P(('seq', 'head')), may hold values from -6 to 6
- keys: bfloat16 [16384, 5120], P('seq', 'head'), may hold values from -4 to 4
- values: bfloat16 [16384, 5120], P('seq', 'head'), may hold values from -18 to 18
- key_tangent: bfloat16 [16384, 5120], P('seq', 'head'), may hold values from -6 to 6
- value_tangent: bfloat16 [16384, 5120], P('seq', 'head'), may hold values from -6 to 6
Outputs:
- attended: float32 [256, 5120], P('seq', 'head')
- attended_tangent: float32 [256, 5120], P('seq', 'head')
- lse: float32 [40, 256], P('head', 'seq')
- lse_tangent: float32 [40, 256], P('head', 'seq')
All inputs are finite; a program needn't handle non-finite values.
Results may differ from a plain program's by a relative error of at most 0.012.
Values may be sent and summed in bfloat16 or wider, within the bound.
No kernel may reach another device: no remote copies, remote signals or barrier semaphores. Data moves between devices by JAX's collectives and lax.ppermute only.
A program may use at most 320 MiB of HBM per device.

v0:
```python
import math

import jax
import jax.numpy as jnp
from jax import lax
from jax.sharding import PartitionSpec as P

HD = 128


def block_terms(
    window, window_tangent, key_block, value_block, key_tangent_block, value_tangent_block
):
    factor = 1.0 / math.sqrt(HD)
    scores = jnp.dot(window, key_block.T, preferred_element_type=jnp.float32) * factor
    score_tangent = (
        jnp.dot(window_tangent, key_block.T, preferred_element_type=jnp.float32)
        + jnp.dot(window, key_tangent_block.T, preferred_element_type=jnp.float32)
    ) * factor
    block_max = jnp.max(scores, axis=1)
    weights = jnp.exp(scores - block_max[:, None])
    rounded = weights.astype(jnp.bfloat16)
    product = weights * score_tangent
    tangent_weights = product.astype(jnp.bfloat16)
    block_total = jnp.sum(weights, axis=1)
    block_slope = jnp.sum(product, axis=1)
    block_out = jnp.dot(rounded, value_block, preferred_element_type=jnp.float32)
    block_out_tangent = jnp.dot(
        tangent_weights, value_block, preferred_element_type=jnp.float32
    ) + jnp.dot(rounded, value_tangent_block, preferred_element_type=jnp.float32)
    return (block_out, block_out_tangent, block_total, block_slope, block_max)


def per_device(query, query_tangent, keys, values, key_tangent, value_tangent):
    window, window_tangent = (
        lax.all_to_all(query, "head", split_axis=1, concat_axis=0, tiled=True),
        lax.all_to_all(query_tangent, "head", split_axis=1, concat_axis=0, tiled=True),
    )
    window, window_tangent = (
        lax.all_gather(window, "seq", axis=0, tiled=True),
        lax.all_gather(window_tangent, "seq", axis=0, tiled=True),
    )
    head_count = keys.shape[1] // HD
    window_rows = window.shape[0]

    def head_terms(head_index):
        column_start = head_index * HD

        def column_slice(array):
            return lax.dynamic_slice_in_dim(array, column_start, HD, 1)

        return block_terms(
            column_slice(window),
            column_slice(window_tangent),
            column_slice(keys),
            column_slice(values),
            column_slice(key_tangent),
            column_slice(value_tangent),
        )

    outs, outs_tangent, totals, slopes, maxima = lax.map(
        head_terms, jnp.arange(head_count, dtype=jnp.int32)
    )
    parts = lax.axis_size("seq")
    row_count = window_rows // parts
    top_all = lax.pmax(maxima, "seq")
    scaling = jnp.exp(maxima - top_all)
    summed_out, summed_tangent, total, slope = (
        lax.psum_scatter(outs * scaling[:, :, None], "seq", scatter_dimension=1, tiled=True),
        lax.psum_scatter(
            outs_tangent * scaling[:, :, None], "seq", scatter_dimension=1, tiled=True
        ),
        lax.psum_scatter(totals * scaling, "seq", scatter_dimension=1, tiled=True),
        lax.psum_scatter(slopes * scaling, "seq", scatter_dimension=1, tiled=True),
    )
    top = lax.dynamic_slice_in_dim(top_all, lax.axis_index("seq") * row_count, row_count, 1)
    attended = summed_out / total[:, :, None]
    lse_tangent = slope / total
    attended_tangent = summed_tangent / total[:, :, None] - lse_tangent[:, :, None] * attended
    lse = top + jnp.log(total)
    attended = jnp.transpose(attended, (1, 0, 2)).reshape(row_count, head_count * HD)
    attended_tangent = jnp.transpose(attended_tangent, (1, 0, 2)).reshape(
        row_count, head_count * HD
    )
    return (attended, attended_tangent, lse, lse_tangent)


def solution(mesh):
    return jax.shard_map(
        per_device,
        mesh=mesh,
        in_specs=(
            P(("seq", "head"), None),
            P(("seq", "head"), None),
            P("seq", "head"),
            P("seq", "head"),
            P("seq", "head"),
            P("seq", "head"),
        ),
        out_specs=(P("seq", "head"), P("seq", "head"), P("head", "seq"), P("head", "seq")),
        check_vma=False,
    )
```

profile of v0, /device:TPU:2, one launch (start us, length us, event | category | flops | bytes accessed | tf_op | source)
XLA Modules:
  0.0 722.3 jit_solution(2870182374197520212)
XLA Ops:
  7.7 1.4 reduce.1
  9.7 5.5 all-to-all-start.1
  15.2 1.4 reduce
  17.3 1.8 all-to-all-done.1
  19.1 4.7 all-to-all-start
  23.8 53.3 %all-gather.1 = bf16[1,256,1280]{2,0,1:T(2,128)(2,1)S(1)} all-gather(bf16[1,4,1280]{2,0,1:T(2,128)(2,1)S(1)} %bitcast.57), channel_id=3, replica_groups=mesh['seq'=64,'head'=4] {'seq'}, dimensions={1}, use_global_device_ids=true | all-gather | bytes 665600 | tf_op jit(solution)/shard_map/all_gather | solution.py:41
  77.2 49.5 %all-gather = bf16[1,256,1280]{2,0,1:T(2,128)(2,1)S(1)} all-gather(bf16[1,4,1280]{2,0,1:T(2,128)(2,1)S(1)} %bitcast.58), channel_id=2, replica_groups=mesh['seq'=64,'head'=4] {'seq'}, dimensions={1}, use_global_device_ids=true | all-gather | bytes 665600 | tf_op jit(solution)/shard_map/all_gather | solution.py:40
  126.8 85.3 %while.18 = (s32[]{:T(128)}, f32[10,256,128]{2,1,0:T(8,128)S(1)}, f32[10,256,128]{2,1,0:T(8,128)}, f32[10,256]{1,0:T(8,128)S(1)}, f32[10,256]{1,0:T(8,128)S(1)},...) while((s32[]{:T(128)}, f32[10,256,128]{2,1,0:T(8,128)S(1)}, ...), condition=%wide.region_4.5_spmd, body=%wide.region_0.4_spmd.sunk | while | flops 101612800 | bytes 3228911 | solution.py:61
  128.1 1.1 fusion.56
  130.2 1.1 fusion.59
  131.3 1.1 fusion.60
  132.3 1.7 fusion.61
  134.1 1.1 fusion.57
  136.6 1.1 fusion.56
  138.7 1.1 fusion.59
  139.8 1.1 fusion.60
  140.8 1.7 fusion.61
  142.6 1.1 fusion.57
  145.1 1.1 fusion.56
  147.2 1.1 fusion.59
  148.3 1.1 fusion.60
  149.4 1.7 fusion.61
  151.1 1.1 fusion.57
  153.7 1.1 fusion.56
  154.7 1.0 fusion.58
  155.8 1.1 fusion.59
  156.9 1.1 fusion.60
  157.9 1.7 fusion.61
  159.7 1.1 fusion.57
  162.2 1.1 fusion.56
  164.3 1.1 fusion.59
  165.4 1.1 fusion.60
  166.5 1.7 fusion.61
  168.2 1.1 fusion.57
  170.7 1.1 fusion.56
  172.8 1.1 fusion.59
  173.9 1.1 fusion.60
  175.0 1.7 fusion.61
  176.7 1.1 fusion.57
  179.3 1.1 fusion.56
  181.4 1.1 fusion.59
  182.4 1.1 fusion.60
  183.5 1.7 fusion.61
  185.3 1.1 fusion.57
  187.8 1.1 fusion.56
  189.9 1.1 fusion.59
  191.0 1.1 fusion.60
  192.1 1.7 fusion.61
  193.8 1.1 fusion.57
  196.3 1.1 fusion.56
  197.4 1.0 fusion.58
  198.4 1.1 fusion.59
  199.5 1.1 fusion.60
  200.6 1.7 fusion.61
  202.3 1.1 fusion.57
  204.9 1.1 fusion.56
  207.0 1.1 fusion.59
  208.0 1.1 fusion.60
  209.1 1.7 fusion.61
  210.8 1.1 fusion.57
  212.1 248.8 %pmax.7 = f32[10,256]{1,0:T(8,128)S(1)} all-reduce(f32[10,256]{1,0:T(8,128)S(1)} %get-tuple-element.76), channel_id=1, replica_groups=mesh['seq'=64,'head'=4] {'seq'}, use_global_device_ids=true, to_apply=%region_5.6 | all-reduce | flops 2560 | bytes 20480 | tf_op jit(solution)/shard_map/pmax | solution.py:66
  460.9 3.3 broadcast_multiply_fusion
  466.3 246.6 %all-reduce.4 = (f32[10,256]{0,1:T(8,128)S(1)}, f32[10,256]{0,1:T(8,128)S(1)}) all-reduce(f32[10,256]{0,1:T(8,128)S(1)} %copy.40, f32[10,256]{0,1:T(8,128)S(1)} %copy.42), channel_id=5, replica_groups=mesh['seq'=64,'head'=4] {'seq'}, use_global_device_ids=true, to_apply=%region_7.8.clone | all-reduce | flops 5120 | bytes 40960
  713.9 1.5 fusion.27
  (89 shorter events, 20.4 us)
Async XLA Ops:
  9.7 9.4 %all-to-all-start.1 = ((bf16[4,2,640]{2,1,0:T(2,128)(2,1)}), bf16[4,2,640]{2,1,0:T(2,128)(2,1)S(1)}, u32[]{:S(2)}, u32[]{:S(2)}) async-start(bf16[4,2,640]{2,1,0:T(2,128)(2,1)} %reshape.46), calls=%async_computation.1 | async-start | bytes 20480 | tf_op jit(solution)/shard_map/all_to_all | solution.py:37
  19.1 58.1 %all-to-all-start = ((bf16[4,2,640]{2,1,0:T(2,128)(2,1)}), bf16[4,2,640]{2,1,0:T(2,128)(2,1)S(1)}, u32[]{:S(2)}, u32[]{:S(2)}) async-start(bf16[4,2,640]{2,1,0:T(2,128)(2,1)} %reshape.44), calls=%async_computation | async-start | bytes 20480 | tf_op jit(solution)/shard_map/all_to_all | solution.py:36
  23.8 690.2 %all-reduce.8.cloned.1.call-start = ((), (), s32[]{:S(2)}) async-start(), calls=%async_computation.2 | async-start | bytes 5242880
  464.2 0.7 copy-start.1
  713.0 2.5 copy-start
Sparse Core Ops, SparseCore 0:
  464.3 187.7 all-reduce.7
where the time goes:
time: 726 us; the launch traced here: 722 us
  blocking collectives  598 us (82%)
  matrix products  70.3 us (10%)
  between operations  14.8 us (2%)
  local copies, waits for them, and re-layouts  11.3 us (2%)
  starting transfers between devices  10.2 us (1%)
  other arithmetic  8.46 us (1%)
    pmax x1, blocking collectives, per_device(): top_all = lax.pmax(maxima, 'seq')  249 us
    unnamed x1, blocking collectives  247 us
    all_gather x1, blocking collectives, per_device(): lax.all_gather(window_tangent, 'seq', axis=0, tiled=True)  53.3 us
    all_gather x1, blocking collectives, per_device(): lax.all_gather(window, 'seq', axis=0, tiled=True)  49.5 us
    dot_general x10, matrix products, block_terms(): jnp.dot(rounded, value_tangent_block, preferred_element_type=jnp.float32)  17.3 us
  transfers between devices with their start and end apart: 3, of which 1 were waited for; matrix products, arithmetic and copies ran while one was open for 1% of the time, Pallas kernels for 0%

commit v1 on v0

v1 whole, which is shorter than its diff:
```python
import math

import jax
import jax.numpy as jnp
from jax import lax
from jax.experimental import pallas as pl
from jax.experimental.pallas import tpu as pltpu
from jax.sharding import Mesh, PartitionSpec as P

HD = 128
PAIR = 2
LANES = 128
LSE_PARTS = (0, 16, 32)
LT_PARTS = (48, 64, 80)

NT = (((1,), (1,)), ((), ()))


def split3(x):
    hi = x.astype(jnp.bfloat16).astype(jnp.float32)
    mid = (x - hi).astype(jnp.bfloat16).astype(jnp.float32)
    return hi, mid, x - hi - mid


def attend_kernel(
    owners, q_ref, k0, v0, kt0, vt0, k1, v1, kt1, vt1, msg_ref, lse_ref, lt_ref
):
    pair = pl.program_id(0)
    rows = q_ref.shape[1]
    per_owner = rows // owners
    lane = lax.broadcasted_iota(jnp.int32, (rows, LANES), 1)

    @pl.when(pair == 0)
    def _():
        lse_ref[...] = jnp.zeros_like(lse_ref)
        lt_ref[...] = jnp.zeros_like(lt_ref)

    factor = 1.0 / math.sqrt(HD)
    tiles = []
    for i in range(PAIR):
        cols = slice(i * HD, (i + 1) * HD)
        q = q_ref[0, :, cols]
        qt = q_ref[1, :, cols]

        def nt(a, b):
            return lax.dot_general(a, b, NT, preferred_element_type=jnp.float32)

        def nn(a, b):
            return jnp.dot(a, b, preferred_element_type=jnp.float32)

        blocks = [
            (k[:, cols], v[:, cols], kt[:, cols], vt[:, cols])
            for k, v, kt, vt in ((k0, v0, kt0, vt0), (k1, v1, kt1, vt1))
        ]
        scores = [nt(q, k) * factor for k, v, kt, vt in blocks]
        tangents = [(nt(qt, k) + nt(q, kt)) * factor for k, v, kt, vt in blocks]
        top = jnp.max(jnp.maximum(scores[0], scores[1]), axis=1, keepdims=True)
        weights = [jnp.exp(s - top) for s in scores]
        products = [w * t for w, t in zip(weights, tangents)]
        total = jnp.sum(weights[0] + weights[1], axis=1, keepdims=True)
        slope = jnp.sum(products[0] + products[1], axis=1, keepdims=True)
        out = jnp.zeros((rows, HD), jnp.float32)
        out_tangent = jnp.zeros((rows, HD), jnp.float32)
        for w, p, (k, v, kt, vt) in zip(weights, products, blocks):
            rounded = w.astype(jnp.bfloat16)
            out += nn(rounded, v)
            out_tangent += nn(p.astype(jnp.bfloat16), v) + nn(rounded, vt)
        inverse = 1.0 / total
        lt = slope * inverse
        out = out * inverse
        out_tangent = out_tangent * inverse - lt * out
        head = pair * PAIR + i
        lse_ref[...] = jnp.where(lane == head, top + jnp.log(total), lse_ref[...])
        lt_ref[...] = jnp.where(lane == head, lt, lt_ref[...])
        tiles += [
            out.reshape(owners, per_owner, HD),
            out_tangent.reshape(owners, per_owner, HD),
        ]
    tile = jnp.concatenate(tiles, axis=1)
    span = tile.shape[1]
    msg_ref[:, pl.ds(pl.multiple_of(pair * span, span), span), :] = tile.astype(jnp.bfloat16)

    @pl.when(pair == pl.num_programs(0) - 1)
    def _():
        stats = jnp.zeros((rows, LANES), jnp.float32)
        for ref, offsets in ((lse_ref, LSE_PARTS), (lt_ref, LT_PARTS)):
            for part, offset in zip(split3(ref[...]), offsets):
                stats += pltpu.roll(part, offset, 1) if offset else part
        stats = stats.reshape(owners, per_owner, LANES)
        stats = jnp.concatenate([stats, stats], axis=1)
        start = span * pl.num_programs(0)
        msg_ref[:, pl.ds(pl.multiple_of(start, 16), 2 * per_owner), :] = stats.astype(jnp.bfloat16)


def attend(window, own, other, owners):
    arrays, rows, width = window.shape
    keys = own[0].shape[0]
    per_owner = rows // owners
    heads = width // HD
    message_rows = (heads + 1) * 2 * per_owner
    block = PAIR * HD
    kv_spec = pl.BlockSpec((keys, block), lambda i: (0, i))
    return pl.pallas_call(
        lambda *refs: attend_kernel(owners, *refs),
        grid=(heads // PAIR,),
        out_shape=jax.ShapeDtypeStruct((owners, message_rows, HD), jnp.bfloat16),
        in_specs=[pl.BlockSpec((arrays, rows, block), lambda i: (0, 0, i))] + [kv_spec] * 8,
        out_specs=pl.BlockSpec((owners, message_rows, HD), lambda i: (0, 0, 0)),
        scratch_shapes=[pltpu.VMEM((rows, LANES), jnp.float32)] * 2,
        compiler_params=pltpu.CompilerParams(vmem_limit_bytes=24 * 1024 * 1024),
        cost_estimate=pl.CostEstimate(
            flops=12 * rows * 2 * keys * width,
            bytes_accessed=16 * keys * width,
            transcendentals=rows * 2 * keys * heads,
        ),
    )(window, *own, *other)


def merge_kernel(heads, msg_ref, out_ref, out_tangent_ref, lse_ref, lt_ref):
    owners = msg_ref.shape[0]
    half = out_ref.shape[0]
    span = 2 * half
    stats = msg_ref[:, heads * span : (heads + 1) * span, :].astype(jnp.float32)

    def gather_parts(offsets):
        total = None
        for offset in offsets[::-1]:
            part = pltpu.roll(stats, LANES - offset, 2) if offset else stats
            total = part if total is None else total + part
        return total

    lse_parts = gather_parts(LSE_PARTS)
    lt_parts = gather_parts(LT_PARTS)
    top = jnp.max(lse_parts, axis=0)
    weights = jnp.exp(lse_parts - top)
    total = jnp.sum(weights, axis=0)
    weights = weights * (1.0 / total)
    lse = top + jnp.log(total)
    lt = jnp.sum(weights * lt_parts, axis=0)
    shifts = weights * (lt_parts - lt)
    for head in range(heads):
        rows = slice(head * span, (head + 1) * span)
        values = msg_ref[:, rows, :].astype(jnp.float32)
        merged = jnp.sum(values * weights[:, :, head : head + 1], axis=0)
        moved = jnp.sum(values * shifts[:, :, head : head + 1], axis=0)
        cols = slice(head * HD, (head + 1) * HD)
        out_ref[:, cols] = merged[:half]
        out_tangent_ref[:, cols] = merged[half:] + moved[:half]
    lse_ref[...] = lse[:half, :heads]
    lt_ref[...] = lt[:half, :heads]


def merge(messages, heads):
    owners, message_rows, _ = messages.shape
    half = message_rows // (heads + 1) // 2
    vmem = pl.BlockSpec(memory_space=pltpu.VMEM)
    wide = jax.ShapeDtypeStruct((half, heads * HD), jnp.float32)
    small = jax.ShapeDtypeStruct((half, heads), jnp.float32)
    attended, attended_tangent, lse, lse_tangent = pl.pallas_call(
        lambda *refs: merge_kernel(heads, *refs),
        out_shape=(wide, wide, small, small),
        in_specs=[vmem],
        out_specs=(vmem,) * 4,
        compiler_params=pltpu.CompilerParams(vmem_limit_bytes=24 * 1024 * 1024),
    )(messages)
    return attended, attended_tangent, lse.T, lse_tangent.T


def per_device(query, query_tangent, keys, values, key_tangent, value_tangent):
    own = (keys, values, key_tangent, value_tangent)
    other = tuple(lax.ppermute(array, "core", [(0, 1), (1, 0)]) for array in own)
    owners = lax.axis_size("chip")
    groups = lax.axis_size("x")
    heads = keys.shape[1] // HD
    row = jnp.stack(
        [query.reshape(groups, heads * HD), query_tangent.reshape(groups, heads * HD)], axis=1
    )
    row = jnp.broadcast_to(row[None], (owners, *row.shape)).reshape(-1, 2, heads * HD)
    window = lax.all_to_all(row, ("chip", "x"), split_axis=0, concat_axis=0, tiled=True)
    window = jnp.transpose(window, (1, 0, 2))
    messages = attend(window, own, other, owners)
    messages = lax.all_to_all(messages, "chip", split_axis=0, concat_axis=0, tiled=True)
    return merge(messages, heads)


def solution(mesh):
    seq, head = mesh.devices.shape
    grid = Mesh(mesh.devices.reshape(seq // 2, 2, head), ("chip", "core", "x"))
    return jax.shard_map(
        per_device,
        mesh=grid,
        in_specs=(P(("chip", "core", "x"), None),) * 2 + (P(("chip", "core"), "x"),) * 4,
        out_specs=(P(("chip", "core"), "x"),) * 2 + (P("x", ("chip", "core")),) * 2,
        check_vma=False,
    )
```

time: 726 us -> 74.8 us (0.10)
  blocking collectives: 598 us -> 23.6 us
  matrix products: 70.3 us -> 0 us
  waiting for transfers between devices: 1.84 us -> 21.4 us
  between operations: 14.8 us -> 0.77 us
  local copies, waits for them, and re-layouts: 11.3 us -> 2.41 us
  Pallas kernels: 0 us -> 7.67 us
  other arithmetic: 8.46 us -> 0.87 us
    pmax x1 -> x0, blocking collectives: 249 us -> none  [per_device(): top_all = lax.pmax(maxima, 'seq')]
    unnamed x1 -> x0, blocking collectives: 247 us -> none
    all_gather x2 -> x0, blocking collectives: 103 us -> none  [the longest x1 53.3 us: per_device(): lax.all_gather(window_tangent, 'seq', axis=0, tiled=True)]
    dot_general x60 -> x0, matrix products: 70.3 us -> none  [the longest x10 17.3 us: block_terms(): jnp.dot(rounded, value_tangent_block, preferred_element_type=jnp.float32)]
    all_to_all x0 -> x1, blocking collectives: none -> 23.6 us  [per_device(): lax.all_to_all(messages, 'chip', split_axis=0, concat_axis=0, tiled=True)]
    all_to_all x2 -> x1, waiting for transfers between devices: 1.82 us -> 21.4 us  [per_device(): lax.all_to_all(row, ('chip', 'x'), split_axis=0, concat_axis=0, tiled=True)]
    pallas_call x0 -> x2, Pallas kernels: none -> 7.67 us  [the longest x1 6.14 us: attend(): pl.pallas_call(lambda *refs: attend_kernel(owners, *refs), grid=(heads //...]
    all_to_all x2 -> x1, starting transfers between devices: 10.2 us -> 16 us  [per_device(): lax.all_to_all(row, ('chip', 'x'), split_axis=0, concat_axis=0, tiled=True)]
  transfers between devices with their start and end apart: 3 -> 5, of which waited for: 1 -> 1; matrix products, arithmetic and copies ran while one was open for 1% -> 2% of each run, Pallas kernels for 0% -> 0%
where the time goes in v1:
time: 74.8 us; the launch traced here: 73.8 us
  blocking collectives  23.6 us (32%)
  waiting for transfers between devices  21.4 us (29%)
  starting transfers between devices  17.1 us (23%)
  Pallas kernels  7.67 us (10%)
  local copies, waits for them, and re-layouts  2.41 us (3%)
  other arithmetic  0.87 us (1%)
  between operations  0.77 us (1%)
    all_to_all x1, blocking collectives, per_device(): lax.all_to_all(messages, 'chip', split_axis=0, concat_axis=0, tiled=True)  23.6 us
    all_to_all x1, waiting for transfers between devices, per_device(): lax.all_to_all(row, ('chip', 'x'), split_axis=0, concat_axis=0, tiled=True)  21.4 us
    all_to_all x1, starting transfers between devices, per_device(): lax.all_to_all(row, ('chip', 'x'), split_axis=0, concat_axis=0, tiled=True)  16 us
    pallas_call x1, Pallas kernels, attend(): pl.pallas_call(lambda *refs: attend_kernel(owners, *refs), grid=(heads //...  6.14 us
    pallas_call x1, Pallas kernels, merge(): pl.pallas_call(lambda *refs: merge_kernel(heads, *refs), out_shape=(wide,...  1.53 us
  transfers between devices with their start and end apart: 5, of which 1 were waited for; matrix products, arithmetic and copies ran while one was open for 2% of the time, Pallas kernels for 0%

profile of v1, /device:TPU:2, one launch (start us, length us, event | category | flops | bytes accessed | tf_op | source)
XLA Modules:
  0.0 73.8 jit_solution(14870050919934109208)
XLA Ops:
  0.6 0.0 copy-start.4
  0.6 0.8 %reduce = bf16[5120]{0:T(1024)(128)(2,1)S(1)} reduce(bf16[1,5120]{1,0:T(2,128)(2,1)} %param.6, bf16[]{:T(256)} %constant.2), dimensions={0}, to_apply=%param.6.reduce_sub_computation | reduce | bytes 20482 | tf_op args[0]
  1.4 0.0 copy-done.4
  1.5 0.1 reduce.1
  1.6 0.0 copy-start.2
  1.6 1.2 %broadcast_in_dim.2 = bf16[32,4,2,1280]{3,2,1,0:T(2,128)(2,1)} broadcast(bf16[4,2,1280]{2,1,0:T(2,128)(2,1)S(1)} %copy.10), dimensions={1,2,3} | broadcast | bytes 675840 | tf_op jit(solution)/shard_map/broadcast_in_dim | solution.py:178
  2.8 0.0 copy-start
  2.8 0.0 copy-start.1
  2.8 16.0 %all-to-all-start = ((bf16[128,2,1280]{2,1,0:T(2,128)(2,1)}), bf16[128,2,1280]{2,1,0:T(2,128)(2,1)}, u32[]{:S(2)}, u32[]{:S(2)}) async-start(bf16[128,2,1280]{2,1,0:T(2,128)(2,1)} %bitcast), calls=%async_computation | async-start | bytes 1310720 | tf_op jit(solution)/shard_map/all_to_all | solution.py:179
  18.8 0.0 copy-done
  18.8 0.0 copy-start.3
  18.8 0.1 collective-permute-start
  18.9 0.0 copy-done.1
  18.9 0.5 collective-permute-start.1
  19.4 0.0 copy-done.2
  19.4 0.1 collective-permute-start.2
  19.5 0.4 collective-permute-start.3
  19.9 21.4 %all-to-all-done = bf16[128,2,1280]{2,1,0:T(2,128)(2,1)} async-done(((bf16[128,2,1280]{2,1,0:T(2,128)(2,1)}), bf16[128,2,1280]{2,1,0:T(2,128)(2,1)}, u32[]{:S(2)}, u32[]{:S(2)}) %all-to-all-start) | async-done | bytes 655392 | tf_op jit(solution)/shard_map/all_to_all | solution.py:179
  41.3 1.2 %copy.13 = bf16[128,2,1280]{2,0,1:T(8,128)(2,1)S(1)} copy(bf16[128,2,1280]{2,1,0:T(2,128)(2,1)} %all-to-all-done) | data formatting | bytes 1310720 | tf_op jit(solution)/shard_map/all_to_all | solution.py:179
  42.4 0.0 collective-permute-done.refs_5_
  42.4 0.0 collective-permute-done.1.refs_6_
  42.4 0.0 collective-permute-done.2.refs_7_
  42.4 0.0 collective-permute-done.3.refs_8_
  42.5 0.0 copy-done.3
  42.5 6.1 %shard_map.93 = bf16[32,88,128]{2,1,0:T(8,128)(2,1)S(1)} custom-call(bf16[2,128,1280]{2,1,0:T(8,128)(2,1)S(1)} %bitcast.6, bf16[256,1280]{1,0:T(8,128)(2,1)S(1)} %copy-done, bf16[256,1280]{1,0:T(8,128)(2,1)S(1)} %copy-done.1, bf16[256,1280]{1,0:T(8,128)(2,1)S(1)} %copy-done.2, bf16[256,1280]{1,0:T(8,128)(2,1)S(1)} %copy-done.3, ...), custom_call_target="tpu_custom_call" | custom-call | flops 1006632960 | bytes 5242880 | tf_op jit(solution)/shard_map/pallas_call | solution.py:103
  48.6 23.6 %all_to_all.10.refs_0_ = bf16[32,88,128]{2,1,0:T(8,128)(2,1)S(1)} all-to-all(bf16[32,88,128]{2,1,0:T(8,128)(2,1)S(1)} %shard_map.93), channel_id=1, replica_groups=mesh['chip'=32,'core'=2,'x'=4] {'chip'}, dimensions={0} | all-to-all | bytes 1441792 | tf_op jit(solution)/shard_map/all_to_all | solution.py:182
  72.2 1.5 %shard_map.94 = (f32[4,1280]{1,0:T(4,128)}, f32[4,1280]{1,0:T(4,128)}, f32[4,10]{1,0:T(4,128)}, f32[4,10]{1,0:T(4,128)}) custom-call(bf16[32,88,128]{2,1,0:T(8,128)(2,1)S(1)} %all_to_all.10.refs_0_), custom_call_target="tpu_custom_call" | custom-call | tf_op jit(solution)/shard_map/pallas_call | solution.py:159
  (4 shorter events, 0.1 us)
Async XLA Ops:
  0.6 0.8 %copy-start.4 = (bf16[1,5120]{1,0:T(2,128)(2,1)S(1)}, bf16[1,5120]{1,0:T(2,128)(2,1)}, u32[]{:S(2)}) copy-start(bf16[1,5120]{1,0:T(2,128)(2,1)} %param.7) | copy-start | bytes 30724
  1.6 17.8 %copy-start.2 = (bf16[256,1280]{1,0:T(8,128)(2,1)S(1)}, bf16[256,1280]{1,0:T(8,128)(2,1)}, u32[]{:S(2)}) copy-start(bf16[256,1280]{1,0:T(8,128)(2,1)} %refs_3_.1) | copy-start | bytes 1966084
  2.8 16.0 %copy-start = (bf16[256,1280]{1,0:T(8,128)(2,1)S(1)}, bf16[256,1280]{1,0:T(8,128)(2,1)}, u32[]{:S(2)}) copy-start(bf16[256,1280]{1,0:T(8,128)(2,1)} %refs_1_.1) | copy-start | bytes 1966084
  2.8 16.1 %copy-start.1 = (bf16[256,1280]{1,0:T(8,128)(2,1)S(1)}, bf16[256,1280]{1,0:T(8,128)(2,1)}, u32[]{:S(2)}) copy-start(bf16[256,1280]{1,0:T(8,128)(2,1)} %refs_2_.1) | copy-start | bytes 1966084
  2.8 38.5 %all-to-all-start = ((bf16[128,2,1280]{2,1,0:T(2,128)(2,1)}), bf16[128,2,1280]{2,1,0:T(2,128)(2,1)}, u32[]{:S(2)}, u32[]{:S(2)}) async-start(bf16[128,2,1280]{2,1,0:T(2,128)(2,1)} %bitcast), calls=%async_computation | async-start | bytes 1310720 | tf_op jit(solution)/shard_map/all_to_all | solution.py:179
  18.8 23.7 %copy-start.3 = (bf16[256,1280]{1,0:T(8,128)(2,1)S(1)}, bf16[256,1280]{1,0:T(8,128)(2,1)}, u32[]{:S(2)}) copy-start(bf16[256,1280]{1,0:T(8,128)(2,1)} %refs_4_.1) | copy-start | bytes 1966084
  18.8 23.6 %collective-permute-start = (bf16[256,1280]{1,0:T(8,128)(2,1)S(1)}, bf16[256,1280]{1,0:T(8,128)(2,1)S(1)}, u32[]{:S(2)}, u32[]{:S(2)}) collective-permute-start(bf16[256,1280]{1,0:T(8,128)(2,1)S(1)} %copy-done), channel_id=1, source_target_pairs={{0,4},{4,0},{1,5},{5,1},{2,6},{6,2},{3,7},{7,3},{8,12},{12,8},{9,1... | collective-permute-start | bytes 1966088 | tf_op jit(solution)/shard_map/ppermute | solution.py:171
  18.9 23.5 %collective-permute-start.1 = (bf16[256,1280]{1,0:T(8,128)(2,1)S(1)}, bf16[256,1280]{1,0:T(8,128)(2,1)}, u32[]{:S(2)}, u32[]{:S(2)}) collective-permute-start(bf16[256,1280]{1,0:T(8,128)(2,1)S(1)} %copy-done.1), channel_id=1, source_target_pairs={{0,4},{4,0},{1,5},{5,1},{2,6},{6,2},{3,7},{7,3},{8,12},{12,8},{9,1... | collective-permute-start | bytes 1966088 | tf_op jit(solution)/shard_map/ppermute | solution.py:171
  19.4 23.0 %collective-permute-start.2 = (bf16[256,1280]{1,0:T(8,128)(2,1)S(1)}, bf16[256,1280]{1,0:T(8,128)(2,1)}, u32[]{:S(2)}, u32[]{:S(2)}) collective-permute-start(bf16[256,1280]{1,0:T(8,128)(2,1)S(1)} %copy-done.2), channel_id=1, source_target_pairs={{0,4},{4,0},{1,5},{5,1},{2,6},{6,2},{3,7},{7,3},{8,12},{12,8},{9,1... | collective-permute-start | bytes 1966088 | tf_op jit(solution)/shard_map/ppermute | solution.py:171
  19.5 22.9 %collective-permute-start.3 = (bf16[256,1280]{1,0:T(8,128)(2,1)}, bf16[256,1280]{1,0:T(8,128)(2,1)}, u32[]{:S(2)}, u32[]{:S(2)}) collective-permute-start(bf16[256,1280]{1,0:T(8,128)(2,1)} %refs_4_.1), channel_id=1, source_target_pairs={{0,4},{4,0},{1,5},{5,1},{2,6},{6,2},{3,7},{7,3},{8,12},{12,8},{9,1... | collective-permute-start | bytes 1966088 | tf_op jit(solution)/shard_map/ppermute | solution.py:171

commit v2 on v1

v2 whole, which is shorter than its diff:
```python
import math

import jax
import jax.numpy as jnp
from jax import lax
from jax.experimental import pallas as pl
from jax.experimental.pallas import tpu as pltpu
from jax.sharding import Mesh, PartitionSpec as P

HD = 128
LANES = 128
CORES = 2
Y = 4
NT = (((1,), (1,)), ((), ()))
VMEM_LIMIT = 32 * 1024 * 1024


def nt(a, b):
    return lax.dot_general(a, b, NT, preferred_element_type=jnp.float32)


def nn(a, b):
    return jnp.dot(a, b, preferred_element_type=jnp.float32)


def split3(x):
    hi = x.astype(jnp.bfloat16).astype(jnp.float32)
    mid = (x - hi).astype(jnp.bfloat16).astype(jnp.float32)
    return hi, mid, x - hi - mid


def encode(lse, lt, heads):
    total = None
    for i, part in enumerate((*split3(lse), *split3(lt))):
        part = pltpu.roll(part, i * heads, part.ndim - 1) if i else part
        total = part if total is None else total + part
    return total


def decode(stats, heads):
    parts = [
        pltpu.roll(stats, LANES - i * heads, stats.ndim - 1) if i else stats for i in range(6)
    ]
    return parts[2] + parts[1] + parts[0], parts[5] + parts[4] + parts[3]


def twice(x):
    return jnp.concatenate([x, x], axis=1)


def attend_kernel(owners, groups, *refs):
    windows, keys, outs = refs[:groups], refs[groups : groups + 8], refs[groups + 8 :]
    rows = windows[0].shape[1]
    total_rows = rows * groups
    heads = windows[0].shape[2] // HD
    per_owner = rows // owners
    factor = 1.0 / math.sqrt(HD)
    lane = lax.broadcasted_iota(jnp.int32, (total_rows, LANES), 1)
    lses = jnp.zeros((total_rows, LANES), jnp.float32)
    lts = jnp.zeros((total_rows, LANES), jnp.float32)
    pending = None
    for head in range(heads):
        cols = slice(head * HD, (head + 1) * HD)
        q = jnp.concatenate([w[0, :, cols] for w in windows], axis=0)
        qt = jnp.concatenate([w[1, :, cols] for w in windows], axis=0)
        blocks = [tuple(ref[:, cols] for ref in keys[i : i + 4]) for i in (0, 4)]
        scores = [nt(q, k) * factor for k, v, kt, vt in blocks]
        tangents = [(nt(qt, k) + nt(q, kt)) * factor for k, v, kt, vt in blocks]
        top = jnp.max(jnp.maximum(scores[0], scores[1]), axis=1, keepdims=True)
        weights = [jnp.exp(s - top) for s in scores]
        products = [w * t for w, t in zip(weights, tangents)]
        total = jnp.sum(weights[0] + weights[1], axis=1, keepdims=True)
        slope = jnp.sum(products[0] + products[1], axis=1, keepdims=True)
        out = jnp.zeros((total_rows, HD), jnp.float32)
        out_tangent = jnp.zeros((total_rows, HD), jnp.float32)
        for w, p, (k, v, kt, vt) in zip(weights, products, blocks):
            rounded = w.astype(jnp.bfloat16)
            out += nn(rounded, v)
            out_tangent += nn(p.astype(jnp.bfloat16), v) + nn(rounded, vt)
        inverse = 1.0 / total
        lt = slope * inverse
        out = out * inverse
        out_tangent = out_tangent * inverse - lt * out
        lses = jnp.where(lane == head, top + jnp.log(total), lses)
        lts = jnp.where(lane == head, lt, lts)
        tile = jnp.concatenate(
            [
                out.reshape(groups * owners, per_owner, HD),
                out_tangent.reshape(groups * owners, per_owner, HD),
            ],
            axis=1,
        )
        if pending is None:
            pending = tile
            continue
        tile = jnp.concatenate([pending, tile], axis=1).astype(jnp.bfloat16)
        pending = None
        span = tile.shape[1]
        start = (head // 2) * span
        for i, ref in enumerate(outs):
            ref[:, start : start + span, :] = tile[i * owners : (i + 1) * owners]
    stats = twice(encode(lses, lts, heads).reshape(groups * owners, per_owner, LANES))
    span = stats.shape[1]
    for i, ref in enumerate(outs):
        part = stats[i * owners : (i + 1) * owners]
        ref[:, heads * span : (heads + 1) * span, :] = part.astype(jnp.bfloat16)


def attend(windows, own, other, owners):
    arrays, rows, width = windows[0].shape
    groups = len(windows)
    heads = width // HD
    message_rows = (heads + 1) * 2 * (rows // owners)
    vmem = pl.BlockSpec(memory_space=pltpu.VMEM)
    keys = own[0].shape[0] * 2
    return pl.pallas_call(
        lambda *refs: attend_kernel(owners, groups, *refs),
        out_shape=[jax.ShapeDtypeStruct((owners, message_rows, HD), jnp.bfloat16)] * groups,
        in_specs=[vmem] * (groups + 8),
        out_specs=[vmem] * groups,
        compiler_params=pltpu.CompilerParams(vmem_limit_bytes=VMEM_LIMIT),
        cost_estimate=pl.CostEstimate(
            flops=12 * rows * groups * keys * width,
            bytes_accessed=8 * keys * width,
            transcendentals=rows * groups * keys * heads,
        ),
    )(*windows, *own, *other)


def merge_weights(stats, heads):
    decoded = [decode(s.astype(jnp.float32), heads) for s in stats]
    top = decoded[0][0]
    for lse, _ in decoded[1:]:
        top = jnp.maximum(top, lse)
    scales = [jnp.exp(lse - top) for lse, _ in decoded]
    total = sum(scales[1:], scales[0])
    inverse = 1.0 / total
    scales = [scale * inverse for scale in scales]
    lt = sum(scale * part for scale, (_, part) in zip(scales, decoded))
    shifts = [scale * (part - lt) for scale, (_, part) in zip(scales, decoded)]
    return scales, shifts, top + jnp.log(total), lt


def merge_group_kernel(heads, *refs):
    sources, out_ref = refs[:-1], refs[-1]
    owners, message_rows, _ = out_ref.shape
    span = message_rows // (heads + 1)
    half = span // 2
    scales, shifts, lse, lt = merge_weights(
        [ref[:, heads * span : (heads + 1) * span, :] for ref in sources], heads
    )
    tangent_row = lax.broadcasted_iota(jnp.int32, (owners, span, HD), 1) >= half
    for pair in range(heads // 2):
        tiles = []
        for head in (2 * pair, 2 * pair + 1):
            rows = slice(head * span, (head + 1) * span)
            merged = moved = 0.0
            for ref, scale, shift in zip(sources, scales, shifts):
                values = ref[:, rows, :].astype(jnp.float32)
                merged += values * scale[:, :, head : head + 1]
                moved += values * shift[:, :, head : head + 1]
            moved = pltpu.roll(moved, half, 1)
            tiles.append(jnp.where(tangent_row, merged + moved, merged))
        start = pair * 2 * span
        tile = jnp.concatenate(tiles, axis=1).astype(jnp.bfloat16)
        out_ref[:, start : start + 2 * span, :] = tile
    lane = lax.broadcasted_iota(jnp.int32, lse.shape, 2)
    stats = encode(jnp.where(lane < heads, lse, 0.0), jnp.where(lane < heads, lt, 0.0), heads)
    out_ref[:, heads * span : (heads + 1) * span, :] = stats.astype(jnp.bfloat16)


def merge_group(messages, heads):
    vmem = pl.BlockSpec(memory_space=pltpu.VMEM)
    return pl.pallas_call(
        lambda *refs: merge_group_kernel(heads, *refs),
        out_shape=jax.ShapeDtypeStruct(messages[0].shape, jnp.bfloat16),
        in_specs=[vmem] * len(messages),
        out_specs=vmem,
        compiler_params=pltpu.CompilerParams(vmem_limit_bytes=VMEM_LIMIT),
    )(*messages)


def merge_kernel(heads, msg_ref, out_ref, out_tangent_ref, lse_ref, lt_ref):
    half = out_ref.shape[0]
    span = 2 * half
    stats = msg_ref[:, heads * span : (heads + 1) * span, :]
    count = msg_ref.shape[0]
    scales, shifts, lse, lt = merge_weights([stats[i] for i in range(count)], heads)
    for head in range(heads):
        rows = slice(head * span, (head + 1) * span)
        merged = moved = 0.0
        for i, (scale, shift) in enumerate(zip(scales, shifts)):
            values = msg_ref[i, rows, :].astype(jnp.float32)
            merged += values * scale[:, head : head + 1]
            moved += values * shift[:, head : head + 1]
        cols = slice(head * HD, (head + 1) * HD)
        out_ref[:, cols] = merged[:half]
        out_tangent_ref[:, cols] = merged[half:] + moved[:half]
    lse_ref[...] = lse[:half, :heads]
    lt_ref[...] = lt[:half, :heads]


def merge(messages, heads):
    half = messages.shape[1] // (heads + 1) // 2
    vmem = pl.BlockSpec(memory_space=pltpu.VMEM)
    wide = jax.ShapeDtypeStruct((half, heads * HD), jnp.float32)
    small = jax.ShapeDtypeStruct((half, heads), jnp.float32)
    attended, attended_tangent, lse, lse_tangent = pl.pallas_call(
        lambda *refs: merge_kernel(heads, *refs),
        out_shape=(wide, wide, small, small),
        in_specs=[vmem],
        out_specs=(vmem,) * 4,
        compiler_params=pltpu.CompilerParams(vmem_limit_bytes=VMEM_LIMIT),
    )(messages)
    return attended, attended_tangent, lse.T, lse_tangent.T


def shift(array, step):
    count = lax.axis_size("y")
    return lax.ppermute(array, "y", [(i, (i + step) % count) for i in range(count)])


def per_device(query, query_tangent, keys, values, key_tangent, value_tangent):
    own = (keys, values, key_tangent, value_tangent)
    other = tuple(lax.ppermute(array, "core", [(0, 1), (1, 0)]) for array in own)
    owners = lax.axis_size("z")
    heads = keys.shape[1] // HD
    row = jnp.stack(
        [array.reshape(lax.axis_size("x"), heads * HD) for array in (query, query_tangent)], axis=1
    )
    row = jnp.broadcast_to(row[None], (owners, *row.shape)).reshape(-1, 2, heads * HD)
    window = lax.all_to_all(row, ("z", "x"), split_axis=0, concat_axis=0, tiled=True)
    window = jnp.transpose(window, (1, 0, 2))
    steps = (1, 3, 2)
    windows = [window] + [shift(window, step) for step in steps]
    messages = attend(windows, own, other, owners)
    messages = [messages[0]] + [shift(m, -step) for m, step in zip(messages[1:], steps)]
    message = merge_group(messages, heads)
    message = lax.all_to_all(message, "z", split_axis=0, concat_axis=0, tiled=True)
    return merge(message, heads)


def solution(mesh):
    seq, head = mesh.devices.shape
    devices = mesh.devices.reshape(seq // (Y * CORES), Y, CORES, head)
    seq_axes = ("z", "y", "core")
    return jax.shard_map(
        per_device,
        mesh=Mesh(devices, (*seq_axes, "x")),
        in_specs=(P((*seq_axes, "x"), None),) * 2 + (P(seq_axes, "x"),) * 4,
        out_specs=(P(seq_axes, "x"),) * 2 + (P("x", seq_axes),) * 2,
        check_vma=False,
    )
```

time: 74.8 us -> 76.2 us (1.019)
  blocking collectives: 23.6 us -> 12.4 us
  waiting for transfers between devices: 21.4 us -> 28.2 us
  starting transfers between devices: 17.1 us -> 23.7 us
  Pallas kernels: 7.67 us -> 5.77 us
  local copies, waits for them, and re-layouts: 2.41 us -> 4.09 us
    ppermute x0 -> x6, waiting for transfers between devices: none -> 20.1 us  [shift(): lax.ppermute(array, 'y', [(i, (i + step) % count) for i in range(count)])]
    all_to_all x1, waiting for transfers between devices: 21.4 us -> 8.08 us  [per_device(): lax.all_to_all(row, ('z', 'x'), split_axis=0, concat_axis=0, tiled=True)]
    all_to_all x1, blocking collectives: 23.6 us -> 12.4 us  [per_device(): lax.all_to_all(message, 'z', split_axis=0, concat_axis=0, tiled=True)]
    ppermute x0 -> x6, starting transfers between devices: none -> 11 us  [shift(): lax.ppermute(array, 'y', [(i, (i + step) % count) for i in range(count)])]
    all_to_all x1, starting transfers between devices: 16 us -> 11.6 us  [per_device(): lax.all_to_all(row, ('z', 'x'), split_axis=0, concat_axis=0, tiled=True)]
    unnamed x10, local copies, waits for them, and re-layouts: 0.02 us -> 3.26 us
    pallas_call x1 -> x2, Pallas kernels: 6.14 us -> 4.78 us  [the longest x1 3.8 us: attend(): pl.pallas_call(lambda *refs: attend_kernel(owners, groups, *refs), out_sh...]
    all_to_all x1, local copies, waits for them, and re-layouts: 1.15 us -> 0.02 us  [per_device(): lax.all_to_all(row, ('z', 'x'), split_axis=0, concat_axis=0, tiled=True)]
  transfers between devices with their start and end apart: 5 -> 11, of which waited for: 1 -> 6; matrix products, arithmetic and copies ran while one was open for 2% -> 0% of each run, Pallas kernels for 0% -> 0%
where the time goes in v2:
time: 76.2 us; the launch traced here: 75.9 us
  waiting for transfers between devices  28.2 us (37%)
  starting transfers between devices  23.7 us (31%)
  blocking collectives  12.4 us (16%)
  Pallas kernels  5.77 us (8%)
  local copies, waits for them, and re-layouts  4.09 us (5%)
  other arithmetic  0.94 us (1%)
    ppermute x6, waiting for transfers between devices, shift(): lax.ppermute(array, 'y', [(i, (i + step) % count) for i in range(count)])  20.1 us
    all_to_all x1, blocking collectives, per_device(): lax.all_to_all(message, 'z', split_axis=0, concat_axis=0, tiled=True)  12.4 us
    all_to_all x1, starting transfers between devices, per_device(): lax.all_to_all(row, ('z', 'x'), split_axis=0, concat_axis=0, tiled=True)  11.6 us
    ppermute x6, starting transfers between devices, shift(): lax.ppermute(array, 'y', [(i, (i + step) % count) for i in range(count)])  11 us
    all_to_all x1, waiting for transfers between devices, per_device(): lax.all_to_all(row, ('z', 'x'), split_axis=0, concat_axis=0, tiled=True)  8.08 us
    pallas_call x1, Pallas kernels, attend(): pl.pallas_call(lambda *refs: attend_kernel(owners, groups, *refs), out_sh...  3.8 us
    unnamed x10, local copies, waits for them, and re-layouts  3.26 us
  transfers between devices with their start and end apart: 11, of which 6 were waited for; matrix products, arithmetic and copies ran while one was open for 0% of the time, Pallas kernels for 0%

profile of v2, /device:TPU:2, one launch (start us, length us, event | category | flops | bytes accessed | tf_op | source)
XLA Modules:
  0.0 75.9 jit_solution(3728796817541208948)
XLA Ops:
  0.6 0.0 copy-start.4
  0.6 0.0 copy-start
  0.7 0.9 %reduce = bf16[5120]{0:T(1024)(128)(2,1)S(1)} reduce(bf16[1,5120]{1,0:T(2,128)(2,1)} %param.6, bf16[]{:T(256)} %constant.2), dimensions={0}, to_apply=%param.6.reduce_sub_computation | reduce | bytes 20482 | tf_op args[0]
  1.5 0.0 copy-done.4
  1.5 0.1 reduce.1
  1.7 0.8 broadcast_in_dim.2
  2.4 11.6 %all-to-all-start = ((bf16[32,2,1280]{2,1,0:T(2,128)(2,1)}), bf16[32,2,1280]{2,1,0:T(2,128)(2,1)S(1)}, u32[]{:S(2)}, u32[]{:S(2)}) async-start(bf16[32,2,1280]{2,1,0:T(2,128)(2,1)} %bitcast), calls=%async_computation | async-start | bytes 327680 | tf_op jit(solution)/shard_map/all_to_all | solution.py:232
  14.0 0.0 copy-done
  14.1 0.1 collective-permute-start.3
  14.2 0.5 collective-permute-start.4
  14.6 0.1 collective-permute-start.5
  14.7 0.4 collective-permute-start.6
  15.2 8.1 %all-to-all-done = bf16[32,2,1280]{2,1,0:T(2,128)(2,1)S(1)} async-done(((bf16[32,2,1280]{2,1,0:T(2,128)(2,1)}), bf16[32,2,1280]{2,1,0:T(2,128)(2,1)S(1)}, u32[]{:S(2)}, u32[]{:S(2)}) %all-to-all-start) | async-done | bytes 163872 | tf_op jit(solution)/shard_map/all_to_all | solution.py:232
  23.3 3.3 %collective-permute-start.2 = (bf16[2,32,1280]{2,1,0:T(8,128)(2,1)S(1)}, bf16[2,32,1280]{2,1,0:T(8,128)(2,1)S(1)}, u32[]{:S(2)}, u32[]{:S(2)}) collective-permute-start(bf16[2,32,1280]{2,1,0:T(8,128)(2,1)S(1)} %bitcast.6), channel_id=1, source_target_pairs={{0,16},{8,24},{16,0},{24,8},{1,17},{9,25},{17,1},{25,9},{2,18},{10... | collective-permute-start | bytes 491528 | tf_op jit(solution)/shard_map/ppermute | solution.py:220
  26.5 3.6 %collective-permute-done.2.refs_3_ = bf16[2,32,1280]{2,1,0:T(8,128)(2,1)S(1)} collective-permute-done((bf16[2,32,1280]{2,1,0:T(8,128)(2,1)S(1)}, bf16[2,32,1280]{2,1,0:T(8,128)(2,1)S(1)}, u32[]{:S(2)}, u32[]{:S(2)}) %collective-permute-start.2) | collective-permute-done | bytes 163872 | tf_op jit(solution)/shard_map/ppermute | solution.py:220
  30.2 3.6 %collective-permute-start.1 = (bf16[2,32,1280]{2,1,0:T(8,128)(2,1)S(1)}, bf16[2,32,1280]{2,1,0:T(8,128)(2,1)S(1)}, u32[]{:S(2)}, u32[]{:S(2)}) collective-permute-start(bf16[2,32,1280]{2,1,0:T(8,128)(2,1)S(1)} %bitcast.7), channel_id=1, source_target_pairs={{0,24},{8,0},{16,8},{24,16},{1,25},{9,1},{17,9},{25,17},{2,26},{10... | collective-permute-start | bytes 491528 | tf_op jit(solution)/shard_map/ppermute | solution.py:220
  33.8 2.8 %collective-permute-done.1.refs_2_ = bf16[2,32,1280]{2,1,0:T(8,128)(2,1)S(1)} collective-permute-done((bf16[2,32,1280]{2,1,0:T(8,128)(2,1)S(1)}, bf16[2,32,1280]{2,1,0:T(8,128)(2,1)S(1)}, u32[]{:S(2)}, u32[]{:S(2)}) %collective-permute-start.1) | collective-permute-done | bytes 163872 | tf_op jit(solution)/shard_map/ppermute | solution.py:220
  36.6 0.5 collective-permute-start
  37.1 6.5 %collective-permute-done.refs_1_ = bf16[2,32,1280]{2,1,0:T(8,128)(2,1)S(1)} collective-permute-done((bf16[2,32,1280]{2,1,0:T(8,128)(2,1)S(1)}, bf16[2,32,1280]{2,1,0:T(8,128)(2,1)S(1)}, u32[]{:S(2)}, u32[]{:S(2)}) %collective-permute-start) | collective-permute-done | bytes 163872 | tf_op jit(solution)/shard_map/ppermute | solution.py:220
  43.6 0.0 collective-permute-done.3.refs_8_
  43.6 0.0 collective-permute-done.4.refs_9_
  43.6 0.0 collective-permute-done.5.refs_10_
  43.6 0.0 collective-permute-done.6.refs_11_
  43.7 0.0 copy-start.1
  43.7 1.1 %copy-done.1 = bf16[256,1280]{1,0:T(8,128)(2,1)S(1)} copy-done((bf16[256,1280]{1,0:T(8,128)(2,1)S(1)}, bf16[256,1280]{1,0:T(8,128)(2,1)}, u32[]{:S(2)}) %copy-start.1) | copy-done | bytes 655384
  44.7 0.0 copy-start.2
  44.7 1.1 %copy-done.2 = bf16[256,1280]{1,0:T(8,128)(2,1)S(1)} copy-done((bf16[256,1280]{1,0:T(8,128)(2,1)S(1)}, bf16[256,1280]{1,0:T(8,128)(2,1)}, u32[]{:S(2)}) %copy-start.2) | copy-done | bytes 655384
  45.8 0.0 copy-start.3
  45.8 1.1 %copy-done.3 = bf16[256,1280]{1,0:T(8,128)(2,1)S(1)} copy-done((bf16[256,1280]{1,0:T(8,128)(2,1)S(1)}, bf16[256,1280]{1,0:T(8,128)(2,1)}, u32[]{:S(2)}) %copy-start.3) | copy-done | bytes 655384
  46.9 3.8 %shard_map.93 = (bf16[8,88,128]{2,1,0:T(8,128)(2,1)S(1)}, bf16[8,88,128]{2,1,0:T(8,128)(2,1)S(1)}, bf16[8,88,128]{2,1,0:T(8,128)(2,1)S(1)}, bf16[8,88,128]{2,1,0:T(8,128)(2,1)S(1)}) custom-call(bf16[2,32,1280]{2,1,0:T(8,128)(2,1)S(1)} %bitcast.9, bf16[2,32,1280]{2,1,0:T(8,128)(2,1)S(1)} %collective-permute-done.refs_1_, ...), custom_call_target="tpu_custom_call" | custom-call | flops 1006632960 | bytes 5242880 | tf_op jit(solution)/shard_map/pallas_call | solution.py:116
  50.7 2.1 %collective-permute-start.7 = (bf16[8,88,128]{2,1,0:T(8,128)(2,1)S(1)}, bf16[8,88,128]{2,1,0:T(8,128)(2,1)S(1)}, u32[]{:S(2)}, u32[]{:S(2)}) collective-permute-start(bf16[8,88,128]{2,1,0:T(8,128)(2,1)S(1)} %get-tuple-element.13), channel_id=1, source_target_pairs={{0,24},{8,0},{16,8},{24,16},{1,25},{9,1},{17,9},{25,17},{2,26},{10... | collective-permute-start | bytes 540680 | tf_op jit(solution)/shard_map/ppermute | solution.py:220
  52.8 0.0 collective-permute-start.8
  52.8 1.6 %collective-permute-start.9 = (bf16[8,88,128]{2,1,0:T(8,128)(2,1)S(1)}, bf16[8,88,128]{2,1,0:T(8,128)(2,1)S(1)}, u32[]{:S(2)}, u32[]{:S(2)}) collective-permute-start(bf16[8,88,128]{2,1,0:T(8,128)(2,1)S(1)} %get-tuple-element.15), channel_id=1, source_target_pairs={{0,16},{8,24},{16,0},{24,8},{1,17},{9,25},{17,1},{25,9},{2,18},{10... | collective-permute-start | bytes 540680 | tf_op jit(solution)/shard_map/ppermute | solution.py:220
  54.4 1.9 %collective-permute-done.7.refs_1_ = bf16[8,88,128]{2,1,0:T(8,128)(2,1)S(1)} collective-permute-done((bf16[8,88,128]{2,1,0:T(8,128)(2,1)S(1)}, bf16[8,88,128]{2,1,0:T(8,128)(2,1)S(1)}, u32[]{:S(2)}, u32[]{:S(2)}) %collective-permute-start.7) | collective-permute-done | bytes 180256 | tf_op jit(solution)/shard_map/ppermute | solution.py:220
  56.3 5.2 %collective-permute-done.8.refs_2_ = bf16[8,88,128]{2,1,0:T(8,128)(2,1)S(1)} collective-permute-done((bf16[8,88,128]{2,1,0:T(8,128)(2,1)S(1)}, bf16[8,88,128]{2,1,0:T(8,128)(2,1)S(1)}, u32[]{:S(2)}, u32[]{:S(2)}) %collective-permute-start.8) | collective-permute-done | bytes 180256 | tf_op jit(solution)/shard_map/ppermute | solution.py:220
  61.5 0.0 collective-permute-done.9.refs_3_
  61.5 1.0 %shard_map.94 = bf16[8,88,128]{2,1,0:T(8,128)(2,1)S(1)} custom-call(bf16[8,88,128]{2,1,0:T(8,128)(2,1)S(1)} %get-tuple-element.12.refs_0_, bf16[8,88,128]{2,1,0:T(8,128)(2,1)S(1)} %collective-permute-done.7.refs_1_, bf16[8,88,128]{2,1,0:T(8,128)(2,1)S(1)} %collective-permute-done.8.refs_2_, bf16[8,88,128]{2,1,0:T(8,128)(2,1)S(1)} %collective-permute-done.9.refs_3_), custom_call_target="tpu_custom_call" | custom-call | tf_op jit(solution)/shard_map/pallas_call | solution.py:174
  62.4 12.4 %all_to_all.10.refs_0_ = bf16[8,88,128]{2,1,0:T(8,128)(2,1)S(1)} all-to-all(bf16[8,88,128]{2,1,0:T(8,128)(2,1)S(1)} %shard_map.94), channel_id=1, replica_groups=mesh['z'=8,'y'=4,'core'=2,'x'=4] {'z'}, dimensions={0} | all-to-all | bytes 360448 | tf_op jit(solution)/shard_map/all_to_all | solution.py:239
  74.9 1.0 %shard_map.95 = (f32[4,1280]{1,0:T(4,128)}, f32[4,1280]{1,0:T(4,128)}, f32[4,10]{1,0:T(4,128)}, f32[4,10]{1,0:T(4,128)}) custom-call(bf16[8,88,128]{2,1,0:T(8,128)(2,1)S(1)} %all_to_all.10.refs_0_), custom_call_target="tpu_custom_call" | custom-call | tf_op jit(solution)/shard_map/pallas_call | solution.py:208
  (5 shorter events, 0.1 us)
Async XLA Ops:
  0.6 0.9 %copy-start.4 = (bf16[1,5120]{1,0:T(2,128)(2,1)S(1)}, bf16[1,5120]{1,0:T(2,128)(2,1)}, u32[]{:S(2)}) copy-start(bf16[1,5120]{1,0:T(2,128)(2,1)} %param.7) | copy-start | bytes 30724
  0.6 13.4 %copy-start = (bf16[256,1280]{1,0:T(8,128)(2,1)S(1)}, bf16[256,1280]{1,0:T(8,128)(2,1)}, u32[]{:S(2)}) copy-start(bf16[256,1280]{1,0:T(8,128)(2,1)} %refs_4_.1) | copy-start | bytes 1966084
  2.4 20.8 %all-to-all-start = ((bf16[32,2,1280]{2,1,0:T(2,128)(2,1)}), bf16[32,2,1280]{2,1,0:T(2,128)(2,1)S(1)}, u32[]{:S(2)}, u32[]{:S(2)}) async-start(bf16[32,2,1280]{2,1,0:T(2,128)(2,1)} %bitcast), calls=%async_computation | async-start | bytes 327680 | tf_op jit(solution)/shard_map/all_to_all | solution.py:232
  14.1 29.6 %collective-permute-start.3 = (bf16[256,1280]{1,0:T(8,128)(2,1)S(1)}, bf16[256,1280]{1,0:T(8,128)(2,1)S(1)}, u32[]{:S(2)}, u32[]{:S(2)}) collective-permute-start(bf16[256,1280]{1,0:T(8,128)(2,1)S(1)} %copy-done), channel_id=1, source_target_pairs={{0,4},{4,0},{1,5},{5,1},{2,6},{6,2},{3,7},{7,3},{8,12},{12,8},{9,1... | collective-permute-start | bytes 1966088 | tf_op jit(solution)/shard_map/ppermute | solution.py:225
  14.2 29.5 %collective-permute-start.4 = (bf16[256,1280]{1,0:T(8,128)(2,1)}, bf16[256,1280]{1,0:T(8,128)(2,1)S(1)}, u32[]{:S(2)}, u32[]{:S(2)}) collective-permute-start(bf16[256,1280]{1,0:T(8,128)(2,1)} %refs_5_.1), channel_id=1, source_target_pairs={{0,4},{4,0},{1,5},{5,1},{2,6},{6,2},{3,7},{7,3},{8,12},{12,8},{9,1... | collective-permute-start | bytes 1966088 | tf_op jit(solution)/shard_map/ppermute | solution.py:225
  14.6 29.0 %collective-permute-start.5 = (bf16[256,1280]{1,0:T(8,128)(2,1)}, bf16[256,1280]{1,0:T(8,128)(2,1)S(1)}, u32[]{:S(2)}, u32[]{:S(2)}) collective-permute-start(bf16[256,1280]{1,0:T(8,128)(2,1)} %refs_6_.1), channel_id=1, source_target_pairs={{0,4},{4,0},{1,5},{5,1},{2,6},{6,2},{3,7},{7,3},{8,12},{12,8},{9,1... | collective-permute-start | bytes 1966088 | tf_op jit(solution)/shard_map/ppermute | solution.py:225
  14.7 28.9 %collective-permute-start.6 = (bf16[256,1280]{1,0:T(8,128)(2,1)}, bf16[256,1280]{1,0:T(8,128)(2,1)S(1)}, u32[]{:S(2)}, u32[]{:S(2)}) collective-permute-start(bf16[256,1280]{1,0:T(8,128)(2,1)} %refs_7_.1), channel_id=1, source_target_pairs={{0,4},{4,0},{1,5},{5,1},{2,6},{6,2},{3,7},{7,3},{8,12},{12,8},{9,1... | collective-permute-start | bytes 1966088 | tf_op jit(solution)/shard_map/ppermute | solution.py:225
  23.3 6.9 %collective-permute-start.2 = (bf16[2,32,1280]{2,1,0:T(8,128)(2,1)S(1)}, bf16[2,32,1280]{2,1,0:T(8,128)(2,1)S(1)}, u32[]{:S(2)}, u32[]{:S(2)}) collective-permute-start(bf16[2,32,1280]{2,1,0:T(8,128)(2,1)S(1)} %bitcast.6), channel_id=1, source_target_pairs={{0,16},{8,24},{16,0},{24,8},{1,17},{9,25},{17,1},{25,9},{2,18},{10... | collective-permute-start | bytes 491528 | tf_op jit(solution)/shard_map/ppermute | solution.py:220
  30.2 6.5 %collective-permute-start.1 = (bf16[2,32,1280]{2,1,0:T(8,128)(2,1)S(1)}, bf16[2,32,1280]{2,1,0:T(8,128)(2,1)S(1)}, u32[]{:S(2)}, u32[]{:S(2)}) collective-permute-start(bf16[2,32,1280]{2,1,0:T(8,128)(2,1)S(1)} %bitcast.7), channel_id=1, source_target_pairs={{0,24},{8,0},{16,8},{24,16},{1,25},{9,1},{17,9},{25,17},{2,26},{10... | collective-permute-start | bytes 491528 | tf_op jit(solution)/shard_map/ppermute | solution.py:220
  36.6 7.0 %collective-permute-start = (bf16[2,32,1280]{2,1,0:T(8,128)(2,1)S(1)}, bf16[2,32,1280]{2,1,0:T(8,128)(2,1)S(1)}, u32[]{:S(2)}, u32[]{:S(2)}) collective-permute-start(bf16[2,32,1280]{2,1,0:T(8,128)(2,1)S(1)} %bitcast.8), channel_id=1, source_target_pairs={{0,8},{8,16},{16,24},{24,0},{1,9},{9,17},{17,25},{25,1},{2,10},{10... | collective-permute-start | bytes 491528 | tf_op jit(solution)/shard_map/ppermute | solution.py:220
  43.7 1.1 %copy-start.1 = (bf16[256,1280]{1,0:T(8,128)(2,1)S(1)}, bf16[256,1280]{1,0:T(8,128)(2,1)}, u32[]{:S(2)}) copy-start(bf16[256,1280]{1,0:T(8,128)(2,1)} %refs_5_.1) | copy-start | bytes 1966084
  44.7 1.1 %copy-start.2 = (bf16[256,1280]{1,0:T(8,128)(2,1)S(1)}, bf16[256,1280]{1,0:T(8,128)(2,1)}, u32[]{:S(2)}) copy-start(bf16[256,1280]{1,0:T(8,128)(2,1)} %refs_6_.1) | copy-start | bytes 1966084
  45.8 1.1 %copy-start.3 = (bf16[256,1280]{1,0:T(8,128)(2,1)S(1)}, bf16[256,1280]{1,0:T(8,128)(2,1)}, u32[]{:S(2)}) copy-start(bf16[256,1280]{1,0:T(8,128)(2,1)} %refs_7_.1) | copy-start | bytes 1966084
  50.7 5.6 %collective-permute-start.7 = (bf16[8,88,128]{2,1,0:T(8,128)(2,1)S(1)}, bf16[8,88,128]{2,1,0:T(8,128)(2,1)S(1)}, u32[]{:S(2)}, u32[]{:S(2)}) collective-permute-start(bf16[8,88,128]{2,1,0:T(8,128)(2,1)S(1)} %get-tuple-element.13), channel_id=1, source_target_pairs={{0,24},{8,0},{16,8},{24,16},{1,25},{9,1},{17,9},{25,17},{2,26},{10... | collective-permute-start | bytes 540680 | tf_op jit(solution)/shard_map/ppermute | solution.py:220
  52.8 8.6 %collective-permute-start.8 = (bf16[8,88,128]{2,1,0:T(8,128)(2,1)S(1)}, bf16[8,88,128]{2,1,0:T(8,128)(2,1)S(1)}, u32[]{:S(2)}, u32[]{:S(2)}) collective-permute-start(bf16[8,88,128]{2,1,0:T(8,128)(2,1)S(1)} %get-tuple-element.14), channel_id=1, source_target_pairs={{0,8},{8,16},{16,24},{24,0},{1,9},{9,17},{17,25},{25,1},{2,10},{10... | collective-permute-start | bytes 540680 | tf_op jit(solution)/shard_map/ppermute | solution.py:220
  52.8 8.6 %collective-permute-start.9 = (bf16[8,88,128]{2,1,0:T(8,128)(2,1)S(1)}, bf16[8,88,128]{2,1,0:T(8,128)(2,1)S(1)}, u32[]{:S(2)}, u32[]{:S(2)}) collective-permute-start(bf16[8,88,128]{2,1,0:T(8,128)(2,1)S(1)} %get-tuple-element.15), channel_id=1, source_target_pairs={{0,16},{8,24},{16,0},{24,8},{1,17},{9,25},{17,1},{25,9},{2,18},{10... | collective-permute-start | bytes 540680 | tf_op jit(solution)/shard_map/ppermute | solution.py:220

commit v3 on v2

--- a/solution.py
+++ b/solution.py
@@ -46,6 +46,61 @@
 
 def twice(x):
     return jnp.concatenate([x, x], axis=1)
+
+
+LOADS = 2
+
+
+def spread_kernel(copies, groups, q_ref, qt_ref, out_ref):
+    width = q_ref.shape[1] // groups
+    for group in range(groups):
+        cols = slice(group * width, (group + 1) * width)
+        pair = jnp.concatenate([q_ref[:, cols], qt_ref[:, cols]], axis=0)
+        for copy in range(copies):
+            out_ref[copy * groups + group] = pair
+
+
+def spread(query, query_tangent, copies, groups):
+    width = query.shape[1] // groups
+    vmem = pl.BlockSpec(memory_space=pltpu.VMEM)
+    return pl.pallas_call(
+        lambda *refs: spread_kernel(copies, groups, *refs),
+        out_shape=jax.ShapeDtypeStruct((copies * groups, 2, width), query.dtype),
+        in_specs=[vmem] * 2,
+        out_specs=vmem,
+        compiler_params=pltpu.CompilerParams(vmem_limit_bytes=VMEM_LIMIT),
+    )(query, query_tangent)
+
+
+def load_kernel(*refs):
+    count = (len(refs) - 1) // 2
+    sources, targets, sems = refs[:count], refs[count : 2 * count], refs[-1]
+    copies = []
+    for i, (source, target) in enumerate(zip(sources, targets)):
+        rows = source.shape[0] // LOADS
+        for j in range(LOADS):
+            part = pl.ds(j * rows, rows)
+            copies.append(
+                pltpu.make_async_copy(source.at[part], target.at[part], sems.at[i * LOADS + j])
+            )
+    for copy in copies:
+        copy.start()
+    for copy in copies:
+        copy.wait()
+
+
+def load(arrays):
+    count = len(arrays)
+    size = sum(array.size for array in arrays)
+    return pl.pallas_call(
+        load_kernel,
+        out_shape=[jax.ShapeDtypeStruct(array.shape, array.dtype) for array in arrays],
+        in_specs=[pl.BlockSpec(memory_space=pltpu.HBM)] * count,
+        out_specs=[pl.BlockSpec(memory_space=pltpu.VMEM)] * count,
+        scratch_shapes=[pltpu.SemaphoreType.DMA((count * LOADS,))],
+        compiler_params=pltpu.CompilerParams(vmem_limit_bytes=VMEM_LIMIT),
+        cost_estimate=pl.CostEstimate(flops=0, bytes_accessed=4 * size, transcendentals=0),
+    )(*arrays)
 
 
 def attend_kernel(owners, groups, *refs):
@@ -225,12 +280,11 @@
     other = tuple(lax.ppermute(array, "core", [(0, 1), (1, 0)]) for array in own)
     owners = lax.axis_size("z")
     heads = keys.shape[1] // HD
-    row = jnp.stack(
-        [array.reshape(lax.axis_size("x"), heads * HD) for array in (query, query_tangent)], axis=1
-    )
-    row = jnp.broadcast_to(row[None], (owners, *row.shape)).reshape(-1, 2, heads * HD)
+    row = spread(query, query_tangent, owners, lax.axis_size("x"))
+    row, own = lax.optimization_barrier((row, own))
     window = lax.all_to_all(row, ("z", "x"), split_axis=0, concat_axis=0, tiled=True)
     window = jnp.transpose(window, (1, 0, 2))
+    window, own, other = lax.optimization_barrier((window, load(own), other))
     steps = (1, 3, 2)
     windows = [window] + [shift(window, step) for step in steps]
     messages = attend(windows, own, other, owners)

time: 76.2 us -> 74.2 us (0.974)
  waiting for transfers between devices: 28.2 us -> 15.2 us
  local copies, waits for them, and re-layouts: 4.09 us -> 11.6 us
  blocking collectives: 12.4 us -> 16.4 us
  Pallas kernels: 5.77 us -> 7.36 us
  starting transfers between devices: 23.7 us -> 22.2 us
  other arithmetic: 0.94 us -> 0 us
    unnamed x10 -> x24, local copies, waits for them, and re-layouts: 3.26 us -> 11.6 us
    all_to_all x1, waiting for transfers between devices: 8.08 us -> 1.53 us  [per_device(): lax.all_to_all(row, ('z', 'x'), split_axis=0, concat_axis=0, tiled=True)]
    ppermute x6, waiting for transfers between devices: 20.1 us -> 13.7 us  [shift(): lax.ppermute(array, 'y', [(i, (i + step) % count) for i in range(count)])]
    all_to_all x1, blocking collectives: 12.4 us -> 16.4 us  [per_device(): lax.all_to_all(message, 'z', split_axis=0, concat_axis=0, tiled=True)]
    pallas_call x0 -> x2, Pallas kernels: none -> 1.6 us  [the longest x1 0.9 us: load(): pl.pallas_call(load_kernel, out_shape=[jax.ShapeDtypeStruct(array.shape,...]
    ppermute x6, starting transfers between devices: 11 us -> 9.49 us  [shift(): lax.ppermute(array, 'y', [(i, (i + step) % count) for i in range(count)])]
    unnamed x2 -> x0, other arithmetic: 0.92 us -> none
  transfers between devices with their start and end apart: 11 -> 11, of which waited for: 6 -> 6; matrix products, arithmetic and copies ran while one was open for 0% -> 0% of each run, Pallas kernels for 0% -> 2%
where the time goes in v3:
time: 74.2 us; the launch traced here: 73.6 us
  starting transfers between devices  22.2 us (30%)
  blocking collectives  16.4 us (22%)
  waiting for transfers between devices  15.2 us (20%)
  local copies, waits for them, and re-layouts  11.6 us (16%)
  Pallas kernels  7.36 us (10%)
    all_to_all x1, blocking collectives, per_device(): lax.all_to_all(message, 'z', split_axis=0, concat_axis=0, tiled=True)  16.4 us
    ppermute x6, waiting for transfers between devices, shift(): lax.ppermute(array, 'y', [(i, (i + step) % count) for i in range(count)])  13.7 us
    unnamed x24, local copies, waits for them, and re-layouts  11.6 us
    all_to_all x1, starting transfers between devices, per_device(): lax.all_to_all(row, ('z', 'x'), split_axis=0, concat_axis=0, tiled=True)  11.6 us
    ppermute x6, starting transfers between devices, shift(): lax.ppermute(array, 'y', [(i, (i + step) % count) for i in range(count)])  9.49 us
    pallas_call x1, Pallas kernels, attend(): pl.pallas_call(lambda *refs: attend_kernel(owners, groups, *refs), out_sh...  3.8 us
    all_to_all x1, waiting for transfers between devices, per_device(): lax.all_to_all(row, ('z', 'x'), split_axis=0, concat_axis=0, tiled=True)  1.53 us
  transfers between devices with their start and end apart: 11, of which 6 were waited for; matrix products, arithmetic and copies ran while one was open for 0% of the time, Pallas kernels for 2%

profile of v3, /device:TPU:2, one launch (start us, length us, event | category | flops | bytes accessed | tf_op | source)
XLA Modules:
  0.0 73.6 jit_solution(12227989152490854449)
XLA Ops:
  0.6 0.1 collective-permute-start
  0.7 0.5 collective-permute-start.1
  1.2 0.1 collective-permute-start.2
  1.3 0.4 collective-permute-start.3
  1.7 0.0 copy-start.10
  1.7 0.7 copy-done.10
  2.5 0.0 copy-start.11
  2.5 0.7 copy-done.11
  3.2 0.7 shard_map.93
  3.9 11.6 %all-to-all-start = ((bf16[32,2,1280]{2,1,0:T(2,128)(2,1)}), bf16[32,2,1280]{2,1,0:T(2,128)(2,1)S(1)}, u32[]{:S(2)}, u32[]{:S(2)}) async-start(bf16[32,2,1280]{2,1,0:T(2,128)(2,1)} %shard_map.93), calls=%async_computation | async-start | bytes 327680 | tf_op jit(solution)/shard_map/all_to_all | solution.py:285
  15.5 0.0 copy-start
  15.5 1.1 %copy-done = bf16[256,1280]{1,0:T(8,128)(2,1)S(1)} copy-done((bf16[256,1280]{1,0:T(8,128)(2,1)S(1)}, bf16[256,1280]{1,0:T(8,128)(2,1)}, u32[]{:S(2)}) %copy-start) | copy-done | bytes 655384
  16.6 0.0 copy-start.1
  16.6 1.1 %copy-done.1 = bf16[256,1280]{1,0:T(8,128)(2,1)S(1)} copy-done((bf16[256,1280]{1,0:T(8,128)(2,1)S(1)}, bf16[256,1280]{1,0:T(8,128)(2,1)}, u32[]{:S(2)}) %copy-start.1) | copy-done | bytes 655384
  17.7 0.0 copy-start.2
  17.7 1.1 %copy-done.2 = bf16[256,1280]{1,0:T(8,128)(2,1)S(1)} copy-done((bf16[256,1280]{1,0:T(8,128)(2,1)S(1)}, bf16[256,1280]{1,0:T(8,128)(2,1)}, u32[]{:S(2)}) %copy-start.2) | copy-done | bytes 655384
  18.8 0.0 copy-start.3
  18.8 1.1 %copy-done.3 = bf16[256,1280]{1,0:T(8,128)(2,1)S(1)} copy-done((bf16[256,1280]{1,0:T(8,128)(2,1)S(1)}, bf16[256,1280]{1,0:T(8,128)(2,1)}, u32[]{:S(2)}) %copy-start.3) | copy-done | bytes 655384
  19.9 0.9 %shard_map.94 = (bf16[256,1280]{1,0:T(8,128)(2,1)S(1)}, bf16[256,1280]{1,0:T(8,128)(2,1)S(1)}, bf16[256,1280]{1,0:T(8,128)(2,1)S(1)}, bf16[256,1280]{1,0:T(8,128)(2,1)S(1)}) custom-call(bf16[256,1280]{1,0:T(8,128)(2,1)S(1)} %copy-done, bf16[256,1280]{1,0:T(8,128)(2,1)S(1)} %copy-done.1, bf16[256,1280]{1,0:T(8,128)(2,1)S(1)} %copy-done.2, ...), custom_call_target="tpu_custom_call" | custom-call | bytes 5242880 | tf_op jit(solution)/shard_map/pallas_call | solution.py:95
  20.8 0.0 copy-start.4
  20.8 0.8 %copy-done.4 = bf16[256,1280]{1,0:T(8,128)(2,1)} copy-done((bf16[256,1280]{1,0:T(8,128)(2,1)}, bf16[256,1280]{1,0:T(8,128)(2,1)S(1)}, u32[]{:S(2)}) %copy-start.4) | copy-done | bytes 655384
  21.6 0.0 copy-start.6
  21.6 0.9 %copy-done.6 = bf16[256,1280]{1,0:T(8,128)(2,1)} copy-done((bf16[256,1280]{1,0:T(8,128)(2,1)}, bf16[256,1280]{1,0:T(8,128)(2,1)S(1)}, u32[]{:S(2)}) %copy-start.6) | copy-done | bytes 655384
  22.5 0.0 copy-start.8
  22.5 0.9 %copy-done.8 = bf16[256,1280]{1,0:T(8,128)(2,1)} copy-done((bf16[256,1280]{1,0:T(8,128)(2,1)}, bf16[256,1280]{1,0:T(8,128)(2,1)S(1)}, u32[]{:S(2)}) %copy-start.8) | copy-done | bytes 655384
  23.4 1.5 %all-to-all-done = bf16[32,2,1280]{2,1,0:T(2,128)(2,1)S(1)} async-done(((bf16[32,2,1280]{2,1,0:T(2,128)(2,1)}), bf16[32,2,1280]{2,1,0:T(2,128)(2,1)S(1)}, u32[]{:S(2)}, u32[]{:S(2)}) %all-to-all-start) | async-done | bytes 163872 | tf_op jit(solution)/shard_map/all_to_all | solution.py:285
  24.9 0.0 collective-permute-done.refs_8_
  24.9 0.0 collective-permute-done.1.refs_9_
  24.9 0.0 collective-permute-done.2.refs_10_
  24.9 0.0 collective-permute-done.3.refs_11_
  25.0 3.3 %collective-permute-start.6 = (bf16[2,32,1280]{2,1,0:T(8,128)(2,1)S(1)}, bf16[2,32,1280]{2,1,0:T(8,128)(2,1)S(1)}, u32[]{:S(2)}, u32[]{:S(2)}) collective-permute-start(bf16[2,32,1280]{2,1,0:T(8,128)(2,1)S(1)} %bitcast.5), channel_id=1, source_target_pairs={{0,16},{8,24},{16,0},{24,8},{1,17},{9,25},{17,1},{25,9},{2,18},{10... | collective-permute-start | bytes 491528 | tf_op jit(solution)/shard_map/ppermute | solution.py:275
  28.2 1.1 %collective-permute-start.5 = (bf16[2,32,1280]{2,1,0:T(8,128)(2,1)S(1)}, bf16[2,32,1280]{2,1,0:T(8,128)(2,1)S(1)}, u32[]{:S(2)}, u32[]{:S(2)}) collective-permute-start(bf16[2,32,1280]{2,1,0:T(8,128)(2,1)S(1)} %bitcast.6), channel_id=1, source_target_pairs={{0,24},{8,0},{16,8},{24,16},{1,25},{9,1},{17,9},{25,17},{2,26},{10... | collective-permute-start | bytes 491528 | tf_op jit(solution)/shard_map/ppermute | solution.py:275
  29.3 1.0 %collective-permute-start.4 = (bf16[2,32,1280]{2,1,0:T(8,128)(2,1)S(1)}, bf16[2,32,1280]{2,1,0:T(8,128)(2,1)S(1)}, u32[]{:S(2)}, u32[]{:S(2)}) collective-permute-start(bf16[2,32,1280]{2,1,0:T(8,128)(2,1)S(1)} %bitcast.7), channel_id=1, source_target_pairs={{0,8},{8,16},{16,24},{24,0},{1,9},{9,17},{17,25},{25,1},{2,10},{10... | collective-permute-start | bytes 491528 | tf_op jit(solution)/shard_map/ppermute | solution.py:275
  30.3 3.3 %collective-permute-done.6.refs_3_ = bf16[2,32,1280]{2,1,0:T(8,128)(2,1)S(1)} collective-permute-done((bf16[2,32,1280]{2,1,0:T(8,128)(2,1)S(1)}, bf16[2,32,1280]{2,1,0:T(8,128)(2,1)S(1)}, u32[]{:S(2)}, u32[]{:S(2)}) %collective-permute-start.6) | collective-permute-done | bytes 163872 | tf_op jit(solution)/shard_map/ppermute | solution.py:275
  33.5 1.6 %collective-permute-done.5.refs_2_ = bf16[2,32,1280]{2,1,0:T(8,128)(2,1)S(1)} collective-permute-done((bf16[2,32,1280]{2,1,0:T(8,128)(2,1)S(1)}, bf16[2,32,1280]{2,1,0:T(8,128)(2,1)S(1)}, u32[]{:S(2)}, u32[]{:S(2)}) %collective-permute-start.5) | collective-permute-done | bytes 163872 | tf_op jit(solution)/shard_map/ppermute | solution.py:275
  35.1 0.8 %collective-permute-done.4.refs_1_ = bf16[2,32,1280]{2,1,0:T(8,128)(2,1)S(1)} collective-permute-done((bf16[2,32,1280]{2,1,0:T(8,128)(2,1)S(1)}, bf16[2,32,1280]{2,1,0:T(8,128)(2,1)S(1)}, u32[]{:S(2)}, u32[]{:S(2)}) %collective-permute-start.4) | collective-permute-done | bytes 163872 | tf_op jit(solution)/shard_map/ppermute | solution.py:275
  35.9 0.0 copy-start.5
  35.9 1.1 %copy-done.5 = bf16[256,1280]{1,0:T(8,128)(2,1)S(1)} copy-done((bf16[256,1280]{1,0:T(8,128)(2,1)S(1)}, bf16[256,1280]{1,0:T(8,128)(2,1)}, u32[]{:S(2)}) %copy-start.5) | copy-done | bytes 655384
  37.0 0.0 copy-start.7
  37.0 1.1 %copy-done.7 = bf16[256,1280]{1,0:T(8,128)(2,1)S(1)} copy-done((bf16[256,1280]{1,0:T(8,128)(2,1)S(1)}, bf16[256,1280]{1,0:T(8,128)(2,1)}, u32[]{:S(2)}) %copy-start.7) | copy-done | bytes 655384
  38.1 0.0 copy-start.9
  38.1 1.1 %copy-done.9 = bf16[256,1280]{1,0:T(8,128)(2,1)S(1)} copy-done((bf16[256,1280]{1,0:T(8,128)(2,1)S(1)}, bf16[256,1280]{1,0:T(8,128)(2,1)}, u32[]{:S(2)}) %copy-start.9) | copy-done | bytes 655384
  39.2 3.8 %shard_map.95 = (bf16[8,88,128]{2,1,0:T(8,128)(2,1)S(1)}, bf16[8,88,128]{2,1,0:T(8,128)(2,1)S(1)}, bf16[8,88,128]{2,1,0:T(8,128)(2,1)S(1)}, bf16[8,88,128]{2,1,0:T(8,128)(2,1)S(1)}) custom-call(bf16[2,32,1280]{2,1,0:T(8,128)(2,1)S(1)} %bitcast.8, bf16[2,32,1280]{2,1,0:T(8,128)(2,1)S(1)} %collective-permute-done.4.refs_1_, ...), custom_call_target="tpu_custom_call" | custom-call | flops 1006632960 | bytes 5242880 | tf_op jit(solution)/shard_map/pallas_call | solution.py:171
  43.0 2.0 %collective-permute-start.7 = (bf16[8,88,128]{2,1,0:T(8,128)(2,1)S(1)}, bf16[8,88,128]{2,1,0:T(8,128)(2,1)S(1)}, u32[]{:S(2)}, u32[]{:S(2)}) collective-permute-start(bf16[8,88,128]{2,1,0:T(8,128)(2,1)S(1)} %get-tuple-element.49), channel_id=1, source_target_pairs={{0,24},{8,0},{16,8},{24,16},{1,25},{9,1},{17,9},{25,17},{2,26},{10... | collective-permute-start | bytes 540680 | tf_op jit(solution)/shard_map/ppermute | solution.py:275
  45.0 0.1 collective-permute-start.8
  45.1 2.1 %collective-permute-start.9 = (bf16[8,88,128]{2,1,0:T(8,128)(2,1)S(1)}, bf16[8,88,128]{2,1,0:T(8,128)(2,1)S(1)}, u32[]{:S(2)}, u32[]{:S(2)}) collective-permute-start(bf16[8,88,128]{2,1,0:T(8,128)(2,1)S(1)} %get-tuple-element.51), channel_id=1, source_target_pairs={{0,16},{8,24},{16,0},{24,8},{1,17},{9,25},{17,1},{25,9},{2,18},{10... | collective-permute-start | bytes 540680 | tf_op jit(solution)/shard_map/ppermute | solution.py:275
  47.2 4.7 %collective-permute-done.7.refs_1_ = bf16[8,88,128]{2,1,0:T(8,128)(2,1)S(1)} collective-permute-done((bf16[8,88,128]{2,1,0:T(8,128)(2,1)S(1)}, bf16[8,88,128]{2,1,0:T(8,128)(2,1)S(1)}, u32[]{:S(2)}, u32[]{:S(2)}) %collective-permute-start.7) | collective-permute-done | bytes 180256 | tf_op jit(solution)/shard_map/ppermute | solution.py:275
  51.9 3.3 %collective-permute-done.8.refs_2_ = bf16[8,88,128]{2,1,0:T(8,128)(2,1)S(1)} collective-permute-done((bf16[8,88,128]{2,1,0:T(8,128)(2,1)S(1)}, bf16[8,88,128]{2,1,0:T(8,128)(2,1)S(1)}, u32[]{:S(2)}, u32[]{:S(2)}) %collective-permute-start.8) | collective-permute-done | bytes 180256 | tf_op jit(solution)/shard_map/ppermute | solution.py:275
  55.2 0.0 collective-permute-done.9.refs_3_
  55.2 1.0 %shard_map.96 = bf16[8,88,128]{2,1,0:T(8,128)(2,1)S(1)} custom-call(bf16[8,88,128]{2,1,0:T(8,128)(2,1)S(1)} %get-tuple-element.48.refs_0_, bf16[8,88,128]{2,1,0:T(8,128)(2,1)S(1)} %collective-permute-done.7.refs_1_, bf16[8,88,128]{2,1,0:T(8,128)(2,1)S(1)} %collective-permute-done.8.refs_2_, bf16[8,88,128]{2,1,0:T(8,128)(2,1)S(1)} %collective-permute-done.9.refs_3_), custom_call_target="tpu_custom_call" | custom-call | tf_op jit(solution)/shard_map/pallas_call | solution.py:229
  56.2 16.4 %all_to_all.10.refs_0_ = bf16[8,88,128]{2,1,0:T(8,128)(2,1)S(1)} all-to-all(bf16[8,88,128]{2,1,0:T(8,128)(2,1)S(1)} %shard_map.96), channel_id=1, replica_groups=mesh['z'=8,'y'=4,'core'=2,'x'=4] {'z'}, dimensions={0} | all-to-all | bytes 360448 | tf_op jit(solution)/shard_map/all_to_all | solution.py:293
  72.6 1.0 %shard_map.97 = (f32[4,1280]{1,0:T(4,128)}, f32[4,1280]{1,0:T(4,128)}, f32[4,10]{1,0:T(4,128)}, f32[4,10]{1,0:T(4,128)}) custom-call(bf16[8,88,128]{2,1,0:T(8,128)(2,1)S(1)} %all_to_all.10.refs_0_), custom_call_target="tpu_custom_call" | custom-call | tf_op jit(solution)/shard_map/pallas_call | solution.py:263
  (1 shorter events, 0.0 us)
Async XLA Ops:
  0.6 24.3 %collective-permute-start = (bf16[256,1280]{1,0:T(8,128)(2,1)}, bf16[256,1280]{1,0:T(8,128)(2,1)S(1)}, u32[]{:S(2)}, u32[]{:S(2)}) collective-permute-start(bf16[256,1280]{1,0:T(8,128)(2,1)} %refs_0_.2), channel_id=1, source_target_pairs={{0,4},{4,0},{1,5},{5,1},{2,6},{6,2},{3,7},{7,3},{8,12},{12,8},{9,1... | collective-permute-start | bytes 1966088 | tf_op jit(solution)/shard_map/ppermute | solution.py:280
  0.7 24.2 %collective-permute-start.1 = (bf16[256,1280]{1,0:T(8,128)(2,1)}, bf16[256,1280]{1,0:T(8,128)(2,1)S(1)}, u32[]{:S(2)}, u32[]{:S(2)}) collective-permute-start(bf16[256,1280]{1,0:T(8,128)(2,1)} %refs_1_.2), channel_id=1, source_target_pairs={{0,4},{4,0},{1,5},{5,1},{2,6},{6,2},{3,7},{7,3},{8,12},{12,8},{9,1... | collective-permute-start | bytes 1966088 | tf_op jit(solution)/shard_map/ppermute | solution.py:280
  1.2 23.7 %collective-permute-start.2 = (bf16[256,1280]{1,0:T(8,128)(2,1)}, bf16[256,1280]{1,0:T(8,128)(2,1)S(1)}, u32[]{:S(2)}, u32[]{:S(2)}) collective-permute-start(bf16[256,1280]{1,0:T(8,128)(2,1)} %refs_2_), channel_id=1, source_target_pairs={{0,4},{4,0},{1,5},{5,1},{2,6},{6,2},{3,7},{7,3},{8,12},{12,8},{9,1... | collective-permute-start | bytes 1966088 | tf_op jit(solution)/shard_map/ppermute | solution.py:280
  1.3 23.6 %collective-permute-start.3 = (bf16[256,1280]{1,0:T(8,128)(2,1)}, bf16[256,1280]{1,0:T(8,128)(2,1)S(1)}, u32[]{:S(2)}, u32[]{:S(2)}) collective-permute-start(bf16[256,1280]{1,0:T(8,128)(2,1)} %refs_3_), channel_id=1, source_target_pairs={{0,4},{4,0},{1,5},{5,1},{2,6},{6,2},{3,7},{7,3},{8,12},{12,8},{9,1... | collective-permute-start | bytes 1966088 | tf_op jit(solution)/shard_map/ppermute | solution.py:280
  1.7 0.7 copy-start.10
  2.5 0.7 copy-start.11
  3.9 21.0 %all-to-all-start = ((bf16[32,2,1280]{2,1,0:T(2,128)(2,1)}), bf16[32,2,1280]{2,1,0:T(2,128)(2,1)S(1)}, u32[]{:S(2)}, u32[]{:S(2)}) async-start(bf16[32,2,1280]{2,1,0:T(2,128)(2,1)} %shard_map.93), calls=%async_computation | async-start | bytes 327680 | tf_op jit(solution)/shard_map/all_to_all | solution.py:285
  15.5 1.1 %copy-start = (bf16[256,1280]{1,0:T(8,128)(2,1)S(1)}, bf16[256,1280]{1,0:T(8,128)(2,1)}, u32[]{:S(2)}) copy-start(bf16[256,1280]{1,0:T(8,128)(2,1)} %refs_0_.2) | copy-start | bytes 1966084
  16.6 1.1 %copy-start.1 = (bf16[256,1280]{1,0:T(8,128)(2,1)S(1)}, bf16[256,1280]{1,0:T(8,128)(2,1)}, u32[]{:S(2)}) copy-start(bf16[256,1280]{1,0:T(8,128)(2,1)} %refs_1_.2) | copy-start | bytes 1966084
  17.7 1.1 %copy-start.2 = (bf16[256,1280]{1,0:T(8,128)(2,1)S(1)}, bf16[256,1280]{1,0:T(8,128)(2,1)}, u32[]{:S(2)}) copy-start(bf16[256,1280]{1,0:T(8,128)(2,1)} %refs_2_) | copy-start | bytes 1966084
  18.8 1.1 %copy-start.3 = (bf16[256,1280]{1,0:T(8,128)(2,1)S(1)}, bf16[256,1280]{1,0:T(8,128)(2,1)}, u32[]{:S(2)}) copy-start(bf16[256,1280]{1,0:T(8,128)(2,1)} %refs_3_) | copy-start | bytes 1966084
  20.8 0.9 %copy-start.4 = (bf16[256,1280]{1,0:T(8,128)(2,1)}, bf16[256,1280]{1,0:T(8,128)(2,1)S(1)}, u32[]{:S(2)}) copy-start(bf16[256,1280]{1,0:T(8,128)(2,1)S(1)} %get-tuple-element.41.refs_5_) | copy-start | bytes 1966084
  21.6 0.9 %copy-start.6 = (bf16[256,1280]{1,0:T(8,128)(2,1)}, bf16[256,1280]{1,0:T(8,128)(2,1)S(1)}, u32[]{:S(2)}) copy-start(bf16[256,1280]{1,0:T(8,128)(2,1)S(1)} %get-tuple-element.42.refs_6_) | copy-start | bytes 1966084
  22.5 0.9 %copy-start.8 = (bf16[256,1280]{1,0:T(8,128)(2,1)}, bf16[256,1280]{1,0:T(8,128)(2,1)S(1)}, u32[]{:S(2)}) copy-start(bf16[256,1280]{1,0:T(8,128)(2,1)S(1)} %get-tuple-element.43.refs_7_) | copy-start | bytes 1966084
  25.0 8.6 %collective-permute-start.6 = (bf16[2,32,1280]{2,1,0:T(8,128)(2,1)S(1)}, bf16[2,32,1280]{2,1,0:T(8,128)(2,1)S(1)}, u32[]{:S(2)}, u32[]{:S(2)}) collective-permute-start(bf16[2,32,1280]{2,1,0:T(8,128)(2,1)S(1)} %bitcast.5), channel_id=1, source_target_pairs={{0,16},{8,24},{16,0},{24,8},{1,17},{9,25},{17,1},{25,9},{2,18},{10... | collective-permute-start | bytes 491528 | tf_op jit(solution)/shard_map/ppermute | solution.py:275
  28.2 6.9 %collective-permute-start.5 = (bf16[2,32,1280]{2,1,0:T(8,128)(2,1)S(1)}, bf16[2,32,1280]{2,1,0:T(8,128)(2,1)S(1)}, u32[]{:S(2)}, u32[]{:S(2)}) collective-permute-start(bf16[2,32,1280]{2,1,0:T(8,128)(2,1)S(1)} %bitcast.6), channel_id=1, source_target_pairs={{0,24},{8,0},{16,8},{24,16},{1,25},{9,1},{17,9},{25,17},{2,26},{10... | collective-permute-start | bytes 491528 | tf_op jit(solution)/shard_map/ppermute | solution.py:275
  29.3 6.6 %collective-permute-start.4 = (bf16[2,32,1280]{2,1,0:T(8,128)(2,1)S(1)}, bf16[2,32,1280]{2,1,0:T(8,128)(2,1)S(1)}, u32[]{:S(2)}, u32[]{:S(2)}) collective-permute-start(bf16[2,32,1280]{2,1,0:T(8,128)(2,1)S(1)} %bitcast.7), channel_id=1, source_target_pairs={{0,8},{8,16},{16,24},{24,0},{1,9},{9,17},{17,25},{25,1},{2,10},{10... | collective-permute-start | bytes 491528 | tf_op jit(solution)/shard_map/ppermute | solution.py:275
  35.9 1.1 %copy-start.5 = (bf16[256,1280]{1,0:T(8,128)(2,1)S(1)}, bf16[256,1280]{1,0:T(8,128)(2,1)}, u32[]{:S(2)}) copy-start(bf16[256,1280]{1,0:T(8,128)(2,1)} %copy-done.4) | copy-start | bytes 1966084
  37.0 1.1 %copy-start.7 = (bf16[256,1280]{1,0:T(8,128)(2,1)S(1)}, bf16[256,1280]{1,0:T(8,128)(2,1)}, u32[]{:S(2)}) copy-start(bf16[256,1280]{1,0:T(8,128)(2,1)} %copy-done.6) | copy-start | bytes 1966084
  38.1 1.1 %copy-start.9 = (bf16[256,1280]{1,0:T(8,128)(2,1)S(1)}, bf16[256,1280]{1,0:T(8,128)(2,1)}, u32[]{:S(2)}) copy-start(bf16[256,1280]{1,0:T(8,128)(2,1)} %copy-done.8) | copy-start | bytes 1966084
  43.0 8.9 %collective-permute-start.7 = (bf16[8,88,128]{2,1,0:T(8,128)(2,1)S(1)}, bf16[8,88,128]{2,1,0:T(8,128)(2,1)S(1)}, u32[]{:S(2)}, u32[]{:S(2)}) collective-permute-start(bf16[8,88,128]{2,1,0:T(8,128)(2,1)S(1)} %get-tuple-element.49), channel_id=1, source_target_pairs={{0,24},{8,0},{16,8},{24,16},{1,25},{9,1},{17,9},{25,17},{2,26},{10... | collective-permute-start | bytes 540680 | tf_op jit(solution)/shard_map/ppermute | solution.py:275
  45.0 10.2 %collective-permute-start.8 = (bf16[8,88,128]{2,1,0:T(8,128)(2,1)S(1)}, bf16[8,88,128]{2,1,0:T(8,128)(2,1)S(1)}, u32[]{:S(2)}, u32[]{:S(2)}) collective-permute-start(bf16[8,88,128]{2,1,0:T(8,128)(2,1)S(1)} %get-tuple-element.50), channel_id=1, source_target_pairs={{0,8},{8,16},{16,24},{24,0},{1,9},{9,17},{17,25},{25,1},{2,10},{10... | collective-permute-start | bytes 540680 | tf_op jit(solution)/shard_map/ppermute | solution.py:275
  45.1 10.1 %collective-permute-start.9 = (bf16[8,88,128]{2,1,0:T(8,128)(2,1)S(1)}, bf16[8,88,128]{2,1,0:T(8,128)(2,1)S(1)}, u32[]{:S(2)}, u32[]{:S(2)}) collective-permute-start(bf16[8,88,128]{2,1,0:T(8,128)(2,1)S(1)} %get-tuple-element.51), channel_id=1, source_target_pairs={{0,16},{8,24},{16,0},{24,8},{1,17},{9,25},{17,1},{25,9},{2,18},{10... | collective-permute-start | bytes 540680 | tf_op jit(solution)/shard_map/ppermute | solution.py:275

commit v4 on v2

--- a/solution.py
+++ b/solution.py
@@ -11,6 +11,7 @@
 LANES = 128
 CORES = 2
 Y = 4
+FIRST_HEADS = 4
 NT = (((1,), (1,)), ((), ()))
 VMEM_LIMIT = 32 * 1024 * 1024
 
@@ -48,22 +49,70 @@
     return jnp.concatenate([x, x], axis=1)
 
 
-def attend_kernel(owners, groups, *refs):
-    windows, keys, outs = refs[:groups], refs[groups : groups + 8], refs[groups + 8 :]
+def spread_kernel(copies, groups, row_ref, out_ref):
+    width = row_ref.shape[1] // groups
+    for group in range(groups):
+        pair = row_ref[:, group * width : (group + 1) * width]
+        for copy in range(copies):
+            out_ref[copy * groups + group] = pair
+
+
+def spread(row, copies, groups):
+    arrays, width = row.shape
+    vmem = pl.BlockSpec(memory_space=pltpu.VMEM)
+    return pl.pallas_call(
+        lambda *refs: spread_kernel(copies, groups, *refs),
+        out_shape=jax.ShapeDtypeStruct((copies * groups, arrays, width // groups), row.dtype),
+        in_specs=[vmem],
+        out_specs=vmem,
+        compiler_params=pltpu.CompilerParams(vmem_limit_bytes=VMEM_LIMIT),
+    )(row)
+
+
+def attend_kernel(owners, groups, first, last, *refs):
+    windows, sources = refs[:groups], refs[groups : groups + 8]
+    rest = refs[groups + 8 :]
+    if first == 0:
+        carried = None
+    else:
+        carried, rest = rest[:2], rest[2:]
+    outs, rest = rest[:groups], rest[groups:]
+    stats_out, (buffers, sems) = rest[:-2], rest[-2:]
     rows = windows[0].shape[1]
     total_rows = rows * groups
     heads = windows[0].shape[2] // HD
     per_owner = rows // owners
     factor = 1.0 / math.sqrt(HD)
+    width = 2 * HD
+    copies = []
+    for pair in range(heads // 2):
+        copies.append(
+            [
+                pltpu.make_async_copy(
+                    source.at[:, pl.ds(first * HD + pair * width, width)],
+                    buffers.at[i, :, pl.ds(pair * width, width)],
+                    sems.at[i, pair],
+                )
+                for i, source in enumerate(sources)
+            ]
+        )
+        for copy in copies[-1]:
+            copy.start()
     lane = lax.broadcasted_iota(jnp.int32, (total_rows, LANES), 1)
-    lses = jnp.zeros((total_rows, LANES), jnp.float32)
-    lts = jnp.zeros((total_rows, LANES), jnp.float32)
+    if carried is None:
+        lses = jnp.zeros((total_rows, LANES), jnp.float32)
+        lts = jnp.zeros((total_rows, LANES), jnp.float32)
+    else:
+        lses, lts = carried[0][...], carried[1][...]
     pending = None
     for head in range(heads):
         cols = slice(head * HD, (head + 1) * HD)
+        if head % 2 == 0:
+            for copy in copies[head // 2]:
+                copy.wait()
         q = jnp.concatenate([w[0, :, cols] for w in windows], axis=0)
         qt = jnp.concatenate([w[1, :, cols] for w in windows], axis=0)
-        blocks = [tuple(ref[:, cols] for ref in keys[i : i + 4]) for i in (0, 4)]
+        blocks = [tuple(buffers[j, :, cols] for j in range(i, i + 4)) for i in (0, 4)]
         scores = [nt(q, k) * factor for k, v, kt, vt in blocks]
         tangents = [(nt(qt, k) + nt(q, kt)) * factor for k, v, kt, vt in blocks]
         top = jnp.max(jnp.maximum(scores[0], scores[1]), axis=1, keepdims=True)
@@ -81,8 +130,8 @@
         lt = slope * inverse
         out = out * inverse
         out_tangent = out_tangent * inverse - lt * out
-        lses = jnp.where(lane == head, top + jnp.log(total), lses)
-        lts = jnp.where(lane == head, lt, lts)
+        lses = jnp.where(lane == first + head, top + jnp.log(total), lses)
+        lts = jnp.where(lane == first + head, lt, lts)
         tile = jnp.concatenate(
             [
                 out.reshape(groups * owners, per_owner, HD),
@@ -99,32 +148,47 @@
         start = (head // 2) * span
         for i, ref in enumerate(outs):
             ref[:, start : start + span, :] = tile[i * owners : (i + 1) * owners]
-    stats = twice(encode(lses, lts, heads).reshape(groups * owners, per_owner, LANES))
+    if not last:
+        stats_out[0][...] = lses
+        stats_out[1][...] = lts
+        return
+    stats = encode(lses, lts, first + heads)
+    stats = twice(stats.reshape(groups * owners, per_owner, LANES))
     span = stats.shape[1]
     for i, ref in enumerate(outs):
         part = stats[i * owners : (i + 1) * owners]
         ref[:, heads * span : (heads + 1) * span, :] = part.astype(jnp.bfloat16)
 
 
-def attend(windows, own, other, owners):
+def attend(windows, own, other, owners, first, last, carried):
     arrays, rows, width = windows[0].shape
     groups = len(windows)
     heads = width // HD
-    message_rows = (heads + 1) * 2 * (rows // owners)
+    total_rows = rows * groups
+    message_rows = (heads + last) * 2 * (rows // owners)
     vmem = pl.BlockSpec(memory_space=pltpu.VMEM)
-    keys = own[0].shape[0] * 2
-    return pl.pallas_call(
-        lambda *refs: attend_kernel(owners, groups, *refs),
-        out_shape=[jax.ShapeDtypeStruct((owners, message_rows, HD), jnp.bfloat16)] * groups,
-        in_specs=[vmem] * (groups + 8),
-        out_specs=[vmem] * groups,
-        compiler_params=pltpu.CompilerParams(vmem_limit_bytes=VMEM_LIMIT),
+    keys = own[0].shape[0]
+    outs = [jax.ShapeDtypeStruct((owners, message_rows, HD), jnp.bfloat16)] * groups
+    if not last:
+        outs += [jax.ShapeDtypeStruct((total_rows, LANES), jnp.float32)] * 2
+    result = pl.pallas_call(
+        lambda *refs: attend_kernel(owners, groups, first, last, *refs),
+        out_shape=outs,
+        in_specs=[vmem] * groups
+        + [pl.BlockSpec(memory_space=pl.ANY)] * 8
+        + [vmem] * len(carried),
+        out_specs=[vmem] * len(outs),
+        scratch_shapes=[
+            pltpu.VMEM((8, keys, width), jnp.bfloat16),
+            pltpu.SemaphoreType.DMA((8, heads // 2)),
+        ],
         cost_estimate=pl.CostEstimate(
-            flops=12 * rows * groups * keys * width,
-            bytes_accessed=8 * keys * width,
-            transcendentals=rows * groups * keys * heads,
+            flops=24 * total_rows * keys * width,
+            bytes_accessed=16 * keys * width,
+            transcendentals=2 * total_rows * keys * heads,
         ),
-    )(*windows, *own, *other)
+    )(*windows, *own, *other, *carried)
+    return result[:groups], result[groups:]
 
 
 def merge_weights(stats, heads):
@@ -141,19 +205,24 @@
     return scales, shifts, top + jnp.log(total), lt
 
 
-def merge_group_kernel(heads, *refs):
-    sources, out_ref = refs[:-1], refs[-1]
+def merge_group_kernel(splits, groups, *refs):
+    parts, out_ref = refs[:-1], refs[-1]
+    parts = [parts[i * groups : (i + 1) * groups] for i in range(len(splits))]
+    heads = sum(splits)
     owners, message_rows, _ = out_ref.shape
     span = message_rows // (heads + 1)
     half = span // 2
+    last = splits[-1]
     scales, shifts, lse, lt = merge_weights(
-        [ref[:, heads * span : (heads + 1) * span, :] for ref in sources], heads
+        [ref[:, last * span : (last + 1) * span, :] for ref in parts[-1]], heads
     )
     tangent_row = lax.broadcasted_iota(jnp.int32, (owners, span, HD), 1) >= half
+    places = [(part, head) for part, count in zip(parts, splits) for head in range(count)]
     for pair in range(heads // 2):
         tiles = []
         for head in (2 * pair, 2 * pair + 1):
-            rows = slice(head * span, (head + 1) * span)
+            sources, place = places[head]
+            rows = slice(place * span, (place + 1) * span)
             merged = moved = 0.0
             for ref, scale, shift in zip(sources, scales, shifts):
                 values = ref[:, rows, :].astype(jnp.float32)
@@ -169,11 +238,15 @@
     out_ref[:, heads * span : (heads + 1) * span, :] = stats.astype(jnp.bfloat16)
 
 
-def merge_group(messages, heads):
+def merge_group(parts, splits):
     vmem = pl.BlockSpec(memory_space=pltpu.VMEM)
+    groups = len(parts[0])
+    owners, rows, lanes = parts[0][0].shape
+    rows = rows // splits[0] * (sum(splits) + 1)
+    messages = [message for part in parts for message in part]
     return pl.pallas_call(
-        lambda *refs: merge_group_kernel(heads, *refs),
-        out_shape=jax.ShapeDtypeStruct(messages[0].shape, jnp.bfloat16),
+        lambda *refs: merge_group_kernel(splits, groups, *refs),
+        out_shape=jax.ShapeDtypeStruct((owners, rows, lanes), jnp.bfloat16),
         in_specs=[vmem] * len(messages),
         out_specs=vmem,
         compiler_params=pltpu.CompilerParams(vmem_limit_bytes=VMEM_LIMIT),
@@ -222,20 +295,32 @@
 
 def per_device(query, query_tangent, keys, values, key_tangent, value_tangent):
     own = (keys, values, key_tangent, value_tangent)
-    other = tuple(lax.ppermute(array, "core", [(0, 1), (1, 0)]) for array in own)
     owners = lax.axis_size("z")
     heads = keys.shape[1] // HD
-    row = jnp.stack(
-        [array.reshape(lax.axis_size("x"), heads * HD) for array in (query, query_tangent)], axis=1
-    )
-    row = jnp.broadcast_to(row[None], (owners, *row.shape)).reshape(-1, 2, heads * HD)
+    row = jnp.concatenate([query, query_tangent], axis=0)
+    row = spread(row, owners, lax.axis_size("x"))
+    row, own = lax.optimization_barrier((row, own))
+    other = tuple(lax.ppermute(array, "core", [(0, 1), (1, 0)]) for array in own)
     window = lax.all_to_all(row, ("z", "x"), split_axis=0, concat_axis=0, tiled=True)
     window = jnp.transpose(window, (1, 0, 2))
+    window, other = lax.optimization_barrier((window, other))
+    splits = (FIRST_HEADS, heads - FIRST_HEADS)
     steps = (1, 3, 2)
-    windows = [window] + [shift(window, step) for step in steps]
-    messages = attend(windows, own, other, owners)
-    messages = [messages[0]] + [shift(m, -step) for m, step in zip(messages[1:], steps)]
-    message = merge_group(messages, heads)
+    windows = []
+    first = 0
+    for count in splits:
+        part = window[:, :, first * HD : (first + count) * HD]
+        windows.append([part] + [shift(part, step) for step in steps])
+        first += count
+    parts = []
+    carried = ()
+    first = 0
+    for i, count in enumerate(splits):
+        last = i == len(splits) - 1
+        messages, carried = attend(windows[i], own, other, owners, first, last, carried)
+        parts.append([messages[0]] + [shift(m, -step) for m, step in zip(messages[1:], steps)])
+        first += count
+    message = merge_group(parts, splits)
     message = lax.all_to_all(message, "z", split_axis=0, concat_axis=0, tiled=True)
     return merge(message, heads)
 

time: 76.2 us -> 75 us (0.984)
  waiting for transfers between devices: 28.2 us -> 5.3 us
  blocking collectives: 12.4 us -> 33.4 us
  Pallas kernels: 5.77 us -> 12.7 us
  starting transfers between devices: 23.7 us -> 18.8 us
  local copies, waits for them, and re-layouts: 4.09 us -> 2.75 us
    all_to_all x0 -> x1, blocking collectives: none -> 20.8 us  [per_device(): lax.all_to_all(row, ('z', 'x'), split_axis=0, concat_axis=0, tiled=True)]
    ppermute x6 -> x12, waiting for transfers between devices: 20.1 us -> 5.28 us  [shift(): lax.ppermute(array, 'y', [(i, (i + step) % count) for i in range(count)])]
    all_to_all x1 -> x0, starting transfers between devices: 11.6 us -> none  [per_device(): lax.all_to_all(row, ('z', 'x'), split_axis=0, concat_axis=0, tiled=True)]
    all_to_all x1 -> x0, waiting for transfers between devices: 8.08 us -> none  [per_device(): lax.all_to_all(row, ('z', 'x'), split_axis=0, concat_axis=0, tiled=True)]
    pallas_call x2 -> x4, Pallas kernels: 4.78 us -> 11.8 us  [the longest x2 10.8 us: attend(): pl.pallas_call(lambda *refs: attend_kernel(owners, groups, first, last, *...]
    ppermute x6 -> x12, starting transfers between devices: 11 us -> 17.7 us  [shift(): lax.ppermute(array, 'y', [(i, (i + step) % count) for i in range(count)])]
    unnamed x2 -> x0, other arithmetic: 0.92 us -> none
    concatenate x0 -> x1, other arithmetic: none -> 0.8 us  [per_device(): row = jnp.concatenate([query, query_tangent], axis=0)]
  transfers between devices with their start and end apart: 11 -> 16, of which waited for: 6 -> 3; matrix products, arithmetic and copies ran while one was open for 0% -> 0% of each run, Pallas kernels for 0% -> 14%
where the time goes in v4:
time: 75 us; the launch traced here: 74.7 us
  blocking collectives  33.4 us (45%)
  starting transfers between devices  18.8 us (25%)
  Pallas kernels  12.7 us (17%)
  waiting for transfers between devices  5.3 us (7%)
  local copies, waits for them, and re-layouts  2.75 us (4%)
  between operations  0.85 us (1%)
  other arithmetic  0.8 us (1%)
    all_to_all x1, blocking collectives, per_device(): lax.all_to_all(row, ('z', 'x'), split_axis=0, concat_axis=0, tiled=True)  20.8 us
    ppermute x12, starting transfers between devices, shift(): lax.ppermute(array, 'y', [(i, (i + step) % count) for i in range(count)])  17.7 us
    all_to_all x1, blocking collectives, per_device(): lax.all_to_all(message, 'z', split_axis=0, concat_axis=0, tiled=True)  12.6 us
    pallas_call x2, Pallas kernels, attend(): pl.pallas_call(lambda *refs: attend_kernel(owners, groups, first, last, *...  10.8 us
    ppermute x12, waiting for transfers between devices, shift(): lax.ppermute(array, 'y', [(i, (i + step) % count) for i in range(count)])  5.28 us
    unnamed x32, local copies, waits for them, and re-layouts  2.72 us
  transfers between devices with their start and end apart: 16, of which 3 were waited for; matrix products, arithmetic and copies ran while one was open for 0% of the time, Pallas kernels for 14%

profile of v4, /device:TPU:2, one launch (start us, length us, event | category | flops | bytes accessed | tf_op | source)
XLA Modules:
  0.0 74.7 jit_solution(1683856148470576641)
XLA Ops:
  0.6 0.8 %pad_maximum_fusion.refs_0_ = bf16[2,5120]{1,0:T(2,128)(2,1)S(1)} fusion(bf16[1,5120]{1,0:T(2,128)(2,1)} %param.7, bf16[1,5120]{1,0:T(2,128)(2,1)} %param.6), kind=kLoop, calls=%fused_computation.1 | loop fusion | flops 40960 | bytes 40960 | tf_op jit(solution)/shard_map/concatenate | solution.py:300
  1.5 0.1 collective-permute-start
  1.6 0.5 collective-permute-start.1
  2.1 0.1 collective-permute-start.2
  2.2 0.4 collective-permute-start.3
  2.6 20.8 %all_to_all.10 = bf16[32,2,1280]{2,1,0:T(2,128)(2,1)S(1)} all-to-all(bf16[32,2,1280]{2,1,0:T(2,128)(2,1)S(1)} %shard_map.93), channel_id=1, replica_groups=mesh['z'=8,'y'=4,'core'=2,'x'=4] {'z','x'}, dimensions={0} | all-to-all | bytes 327680 | tf_op jit(solution)/shard_map/all_to_all | solution.py:304
  23.4 0.0 collective-permute-done.refs_8_
  23.4 0.0 copy-start.2
  23.4 0.0 collective-permute-done.1.refs_9_
  23.4 0.0 copy-start.3
  23.4 0.0 collective-permute-done.2.refs_10_
  23.4 0.0 copy-start.4
  23.4 0.0 collective-permute-done.3.refs_11_
  23.4 0.0 copy-start.5
  23.5 0.0 copy-start.7
  23.5 1.7 %collective-permute-start.4 = (bf16[2,32,512]{2,1,0:T(8,128)(2,1)S(1)}, bf16[2,32,512]{2,1,0:T(8,128)(2,1)S(1)}, u32[]{:S(2)}, u32[]{:S(2)}) collective-permute-start(bf16[2,32,512]{2,1,0:T(8,128)(2,1)S(1)} %slice.6.refs_0_), channel_id=1, source_target_pairs={{0,8},{8,16},{16,24},{24,0},{1,9},{9,17},{17,25},{25,1},{2,10},{10... | collective-permute-start | bytes 196616 | tf_op jit(solution)/shard_map/ppermute | solution.py:293
  25.1 1.7 %collective-permute-start.5 = (bf16[2,32,512]{2,1,0:T(8,128)(2,1)S(1)}, bf16[2,32,512]{2,1,0:T(8,128)(2,1)S(1)}, u32[]{:S(2)}, u32[]{:S(2)}) collective-permute-start(bf16[2,32,512]{2,1,0:T(8,128)(2,1)S(1)} %slice.6.refs_0_), channel_id=1, source_target_pairs={{0,24},{8,0},{16,8},{24,16},{1,25},{9,1},{17,9},{25,17},{2,26},{10... | collective-permute-start | bytes 196616 | tf_op jit(solution)/shard_map/ppermute | solution.py:293
  26.8 2.0 %collective-permute-start.6 = (bf16[2,32,512]{2,1,0:T(8,128)(2,1)S(1)}, bf16[2,32,512]{2,1,0:T(8,128)(2,1)S(1)}, u32[]{:S(2)}, u32[]{:S(2)}) collective-permute-start(bf16[2,32,512]{2,1,0:T(8,128)(2,1)S(1)} %slice.6.refs_0_), channel_id=1, source_target_pairs={{0,16},{8,24},{16,0},{24,8},{1,17},{9,25},{17,1},{25,9},{2,18},{10... | collective-permute-start | bytes 196616 | tf_op jit(solution)/shard_map/ppermute | solution.py:293
  28.8 0.0 copy-done.7
  28.8 0.0 copy-start.6
  28.8 0.8 %collective-permute-start.10 = (bf16[2,32,768]{2,1,0:T(8,128)(2,1)S(1)}, bf16[2,32,768]{2,1,0:T(8,128)(2,1)S(1)}, u32[]{:S(2)}, u32[]{:S(2)}) collective-permute-start(bf16[2,32,768]{2,1,0:T(8,128)(2,1)S(1)} %slice.7.refs_0_), channel_id=1, source_target_pairs={{0,8},{8,16},{16,24},{24,0},{1,9},{9,17},{17,25},{25,1},{2,10},{10... | collective-permute-start | bytes 294920 | tf_op jit(solution)/shard_map/ppermute | solution.py:293
  29.5 2.6 %collective-permute-start.11 = (bf16[2,32,768]{2,1,0:T(8,128)(2,1)S(1)}, bf16[2,32,768]{2,1,0:T(8,128)(2,1)S(1)}, u32[]{:S(2)}, u32[]{:S(2)}) collective-permute-start(bf16[2,32,768]{2,1,0:T(8,128)(2,1)S(1)} %slice.7.refs_0_), channel_id=1, source_target_pairs={{0,24},{8,0},{16,8},{24,16},{1,25},{9,1},{17,9},{25,17},{2,26},{10... | collective-permute-start | bytes 294920 | tf_op jit(solution)/shard_map/ppermute | solution.py:293
  32.1 0.0 collective-permute-done.4.refs_1_
  32.1 0.3 collective-permute-start.12
  32.5 0.0 collective-permute-done.5.refs_2_
  32.5 0.1 collective-permute-done.6.refs_3_
  32.6 0.0 copy-done.2
  32.6 0.0 copy-done.3
  32.6 0.0 copy-done.4
  32.6 0.0 copy-done.5
  32.6 0.2 copy-done.11
  32.7 0.3 copy-done.12
  33.1 0.6 copy-done.13
  33.7 4.8 %shard_map.94 = (bf16[8,32,128]{2,1,0:T(8,128)(2,1)}, bf16[8,32,128]{2,1,0:T(8,128)(2,1)}, bf16[8,32,128]{2,1,0:T(8,128)(2,1)}, bf16[8,32,128]{2,1,0:T(8,128)(2,...) custom-call(bf16[2,32,512]{2,1,0:T(8,128)(2,1)} %copy-done.7, bf16[2,32,512]{2,1,0:T(8,128)(2,1)} %copy-done.11, ...), custom_call_target="tpu_custom_call" | custom-call | flops 402653184 | bytes 2097152 | tf_op jit(solution)/shard_map/pallas_call | solution.py:174
  38.5 0.0 copy-done.6
  38.5 2.0 %collective-permute-start.7 = (bf16[8,32,128]{2,1,0:T(8,128)(2,1)}, bf16[8,32,128]{2,1,0:T(8,128)(2,1)S(1)}, u32[]{:S(2)}, u32[]{:S(2)}) collective-permute-start(bf16[8,32,128]{2,1,0:T(8,128)(2,1)} %get-tuple-element.39), channel_id=1, source_target_pairs={{0,24},{8,0},{16,8},{24,16},{1,25},{9,1},{17,9},{25,17},{2,26},{10... | collective-permute-start | bytes 196616 | tf_op jit(solution)/shard_map/ppermute | solution.py:293
  40.6 0.0 collective-permute-done.10.refs_1_
  40.6 0.0 collective-permute-done.11.refs_2_
  40.6 0.0 copy-start.9
  40.6 0.0 collective-permute-done.12.refs_3_
  40.6 0.0 copy-start.10
  40.6 0.6 copy-done.8
  41.2 0.0 copy-done.9
  41.2 0.0 copy-done.10
  41.3 5.9 %shard_map.95 = (bf16[8,56,128]{2,1,0:T(8,128)(2,1)}, bf16[8,56,128]{2,1,0:T(8,128)(2,1)}, bf16[8,56,128]{2,1,0:T(8,128)(2,1)}, bf16[8,56,128]{2,1,0:T(8,128)(2,1)}) custom-call(bf16[2,32,768]{2,1,0:T(8,128)(2,1)} %copy-done.6, bf16[2,32,768]{2,1,0:T(8,128)(2,1)} %copy-done.8, bf16[2,32,768]{2,1,0:T(8,128)(2,1)} %copy-done.9, ...), custom_call_target="tpu_custom_call" | custom-call | flops 603979776 | bytes 3145728 | tf_op jit(solution)/shard_map/pallas_call | solution.py:174
  47.2 2.0 %collective-permute-start.13 = (bf16[8,56,128]{2,1,0:T(8,128)(2,1)}, bf16[8,56,128]{2,1,0:T(8,128)(2,1)S(1)}, u32[]{:S(2)}, u32[]{:S(2)}) collective-permute-start(bf16[8,56,128]{2,1,0:T(8,128)(2,1)} %get-tuple-element.45), channel_id=1, source_target_pairs={{0,24},{8,0},{16,8},{24,16},{1,25},{9,1},{17,9},{25,17},{2,26},{10... | collective-permute-start | bytes 344072 | tf_op jit(solution)/shard_map/ppermute | solution.py:293
  49.3 0.2 collective-permute-start.14
  49.5 1.3 %collective-permute-start.15 = (bf16[8,56,128]{2,1,0:T(8,128)(2,1)}, bf16[8,56,128]{2,1,0:T(8,128)(2,1)S(1)}, u32[]{:S(2)}, u32[]{:S(2)}) collective-permute-start(bf16[8,56,128]{2,1,0:T(8,128)(2,1)} %get-tuple-element.47), channel_id=1, source_target_pairs={{0,16},{8,24},{16,0},{24,8},{1,17},{9,25},{17,1},{25,9},{2,18},{10... | collective-permute-start | bytes 344072 | tf_op jit(solution)/shard_map/ppermute | solution.py:293
  50.8 0.0 copy-done.15
  50.9 2.5 %collective-permute-start.8 = (bf16[8,32,128]{2,1,0:T(8,128)(2,1)S(1)}, bf16[8,32,128]{2,1,0:T(8,128)(2,1)S(1)}, u32[]{:S(2)}, u32[]{:S(2)}) collective-permute-start(bf16[8,32,128]{2,1,0:T(8,128)(2,1)S(1)} %copy-done.15), channel_id=1, source_target_pairs={{0,8},{8,16},{16,24},{24,0},{1,9},{9,17},{17,25},{25,1},{2,10},{10... | collective-permute-start | bytes 196616 | tf_op jit(solution)/shard_map/ppermute | solution.py:293
  53.4 0.0 collective-permute-done.7.refs_1_
  53.4 0.0 copy-done.14
  53.4 0.6 collective-permute-start.9
  54.0 3.5 %collective-permute-done.8.refs_2_ = bf16[8,32,128]{2,1,0:T(8,128)(2,1)S(1)} collective-permute-done((bf16[8,32,128]{2,1,0:T(8,128)(2,1)S(1)}, bf16[8,32,128]{2,1,0:T(8,128)(2,1)S(1)}, u32[]{:S(2)}, u32[]{:S(2)}) %collective-permute-start.8) | collective-permute-done | bytes 65568 | tf_op jit(solution)/shard_map/ppermute | solution.py:293
  57.5 1.7 %collective-permute-done.9.refs_3_ = bf16[8,32,128]{2,1,0:T(8,128)(2,1)S(1)} collective-permute-done((bf16[8,32,128]{2,1,0:T(8,128)(2,1)S(1)}, bf16[8,32,128]{2,1,0:T(8,128)(2,1)S(1)}, u32[]{:S(2)}, u32[]{:S(2)}) %collective-permute-start.9) | collective-permute-done | bytes 65568 | tf_op jit(solution)/shard_map/ppermute | solution.py:293
  59.2 0.0 collective-permute-done.13.refs_5_
  59.2 0.0 collective-permute-done.14.refs_6_
  59.2 0.0 collective-permute-done.15.refs_7_
  59.2 0.0 copy-done.1
  59.2 0.0 copy-start
  59.2 0.9 %copy-done = bf16[8,56,128]{2,1,0:T(8,128)(2,1)S(1)} copy-done((bf16[8,56,128]{2,1,0:T(8,128)(2,1)S(1)}, bf16[8,56,128]{2,1,0:T(8,128)(2,1)}, u32[]{:S(2)}) %copy-start) | copy-done | bytes 114712
  60.1 1.0 %shard_map.96 = bf16[8,88,128]{2,1,0:T(8,128)(2,1)S(1)} custom-call(bf16[8,32,128]{2,1,0:T(8,128)(2,1)S(1)} %copy-done.1, bf16[8,32,128]{2,1,0:T(8,128)(2,1)S(1)} %collective-permute-done.7.refs_1_, bf16[8,32,128]{2,1,0:T(8,128)(2,1)S(1)} %collective-permute-done.8.refs_2_, bf16[8,32,128]{2,1,0:T(8,128)(2,1)S(1)} %collective-permute-done.9.refs_3_, ...), custom_call_target="tpu_custom_call" | custom-call | tf_op jit(solution)/shard_map/pallas_call | solution.py:247
  61.1 12.6 %all_to_all.11.refs_0_ = bf16[8,88,128]{2,1,0:T(8,128)(2,1)S(1)} all-to-all(bf16[8,88,128]{2,1,0:T(8,128)(2,1)S(1)} %shard_map.96), channel_id=1, replica_groups=mesh['z'=8,'y'=4,'core'=2,'x'=4] {'z'}, dimensions={0} | all-to-all | bytes 360448 | tf_op jit(solution)/shard_map/all_to_all | solution.py:324
  73.7 1.0 %shard_map.97 = (f32[4,1280]{1,0:T(4,128)}, f32[4,1280]{1,0:T(4,128)}, f32[4,10]{1,0:T(4,128)}, f32[4,10]{1,0:T(4,128)}) custom-call(bf16[8,88,128]{2,1,0:T(8,128)(2,1)S(1)} %all_to_all.11.refs_0_), custom_call_target="tpu_custom_call" | custom-call | tf_op jit(solution)/shard_map/pallas_call | solution.py:281
  (11 shorter events, 0.1 us)
Async XLA Ops:
  1.5 21.9 %collective-permute-start = (bf16[256,1280]{1,0:T(8,128)(2,1)}, bf16[256,1280]{1,0:T(8,128)(2,1)S(1)}, u32[]{:S(2)}, u32[]{:S(2)}) collective-permute-start(bf16[256,1280]{1,0:T(8,128)(2,1)} %refs_4_.1), channel_id=1, source_target_pairs={{0,4},{4,0},{1,5},{5,1},{2,6},{6,2},{3,7},{7,3},{8,12},{12,8},{9,1... | collective-permute-start | bytes 1966088 | tf_op jit(solution)/shard_map/ppermute | solution.py:303
  1.6 21.8 %collective-permute-start.1 = (bf16[256,1280]{1,0:T(8,128)(2,1)}, bf16[256,1280]{1,0:T(8,128)(2,1)S(1)}, u32[]{:S(2)}, u32[]{:S(2)}) collective-permute-start(bf16[256,1280]{1,0:T(8,128)(2,1)} %refs_5_.1), channel_id=1, source_target_pairs={{0,4},{4,0},{1,5},{5,1},{2,6},{6,2},{3,7},{7,3},{8,12},{12,8},{9,1... | collective-permute-start | bytes 1966088 | tf_op jit(solution)/shard_map/ppermute | solution.py:303
  2.1 21.4 %collective-permute-start.2 = (bf16[256,1280]{1,0:T(8,128)(2,1)}, bf16[256,1280]{1,0:T(8,128)(2,1)S(1)}, u32[]{:S(2)}, u32[]{:S(2)}) collective-permute-start(bf16[256,1280]{1,0:T(8,128)(2,1)} %refs_6_.1), channel_id=1, source_target_pairs={{0,4},{4,0},{1,5},{5,1},{2,6},{6,2},{3,7},{7,3},{8,12},{12,8},{9,1... | collective-permute-start | bytes 1966088 | tf_op jit(solution)/shard_map/ppermute | solution.py:303
  2.2 21.3 %collective-permute-start.3 = (bf16[256,1280]{1,0:T(8,128)(2,1)}, bf16[256,1280]{1,0:T(8,128)(2,1)S(1)}, u32[]{:S(2)}, u32[]{:S(2)}) collective-permute-start(bf16[256,1280]{1,0:T(8,128)(2,1)} %refs_7_.1), channel_id=1, source_target_pairs={{0,4},{4,0},{1,5},{5,1},{2,6},{6,2},{3,7},{7,3},{8,12},{12,8},{9,1... | collective-permute-start | bytes 1966088 | tf_op jit(solution)/shard_map/ppermute | solution.py:303
  23.4 9.2 %copy-start.2 = (bf16[256,1280]{1,0:T(8,128)(2,1)}, bf16[256,1280]{1,0:T(8,128)(2,1)S(1)}, u32[]{:S(2)}) copy-start(bf16[256,1280]{1,0:T(8,128)(2,1)S(1)} %collective-permute-done.refs_8_) | copy-start | bytes 1966084
  23.4 9.2 %copy-start.3 = (bf16[256,1280]{1,0:T(8,128)(2,1)}, bf16[256,1280]{1,0:T(8,128)(2,1)S(1)}, u32[]{:S(2)}) copy-start(bf16[256,1280]{1,0:T(8,128)(2,1)S(1)} %collective-permute-done.1.refs_9_) | copy-start | bytes 1966084
  23.4 9.1 %copy-start.4 = (bf16[256,1280]{1,0:T(8,128)(2,1)}, bf16[256,1280]{1,0:T(8,128)(2,1)S(1)}, u32[]{:S(2)}) copy-start(bf16[256,1280]{1,0:T(8,128)(2,1)S(1)} %collective-permute-done.2.refs_10_) | copy-start | bytes 1966084
  23.4 9.1 %copy-start.5 = (bf16[256,1280]{1,0:T(8,128)(2,1)}, bf16[256,1280]{1,0:T(8,128)(2,1)S(1)}, u32[]{:S(2)}) copy-start(bf16[256,1280]{1,0:T(8,128)(2,1)S(1)} %collective-permute-done.3.refs_11_) | copy-start | bytes 1966084
  23.5 5.3 %copy-start.7 = (bf16[2,32,512]{2,1,0:T(8,128)(2,1)}, bf16[2,32,512]{2,1,0:T(8,128)(2,1)S(1)}, u32[]{:S(2)}) copy-start(bf16[2,32,512]{2,1,0:T(8,128)(2,1)S(1)} %slice.6.refs_0_) | copy-start | bytes 196612
  23.5 8.6 %collective-permute-start.4 = (bf16[2,32,512]{2,1,0:T(8,128)(2,1)S(1)}, bf16[2,32,512]{2,1,0:T(8,128)(2,1)S(1)}, u32[]{:S(2)}, u32[]{:S(2)}) collective-permute-start(bf16[2,32,512]{2,1,0:T(8,128)(2,1)S(1)} %slice.6.refs_0_), channel_id=1, source_target_pairs={{0,8},{8,16},{16,24},{24,0},{1,9},{9,17},{17,25},{25,1},{2,10},{10... | collective-permute-start | bytes 196616 | tf_op jit(solution)/shard_map/ppermute | solution.py:293
  25.1 7.3 %collective-permute-start.5 = (bf16[2,32,512]{2,1,0:T(8,128)(2,1)S(1)}, bf16[2,32,512]{2,1,0:T(8,128)(2,1)S(1)}, u32[]{:S(2)}, u32[]{:S(2)}) collective-permute-start(bf16[2,32,512]{2,1,0:T(8,128)(2,1)S(1)} %slice.6.refs_0_), channel_id=1, source_target_pairs={{0,24},{8,0},{16,8},{24,16},{1,25},{9,1},{17,9},{25,17},{2,26},{10... | collective-permute-start | bytes 196616 | tf_op jit(solution)/shard_map/ppermute | solution.py:293
  26.8 5.8 %collective-permute-start.6 = (bf16[2,32,512]{2,1,0:T(8,128)(2,1)S(1)}, bf16[2,32,512]{2,1,0:T(8,128)(2,1)S(1)}, u32[]{:S(2)}, u32[]{:S(2)}) collective-permute-start(bf16[2,32,512]{2,1,0:T(8,128)(2,1)S(1)} %slice.6.refs_0_), channel_id=1, source_target_pairs={{0,16},{8,24},{16,0},{24,8},{1,17},{9,25},{17,1},{25,9},{2,18},{10... | collective-permute-start | bytes 196616 | tf_op jit(solution)/shard_map/ppermute | solution.py:293
  28.8 9.7 %copy-start.6 = (bf16[2,32,768]{2,1,0:T(8,128)(2,1)}, bf16[2,32,768]{2,1,0:T(8,128)(2,1)S(1)}, u32[]{:S(2)}) copy-start(bf16[2,32,768]{2,1,0:T(8,128)(2,1)S(1)} %slice.7.refs_0_) | copy-start | bytes 294916
  28.8 11.8 %collective-permute-start.10 = (bf16[2,32,768]{2,1,0:T(8,128)(2,1)S(1)}, bf16[2,32,768]{2,1,0:T(8,128)(2,1)S(1)}, u32[]{:S(2)}, u32[]{:S(2)}) collective-permute-start(bf16[2,32,768]{2,1,0:T(8,128)(2,1)S(1)} %slice.7.refs_0_), channel_id=1, source_target_pairs={{0,8},{8,16},{16,24},{24,0},{1,9},{9,17},{17,25},{25,1},{2,10},{10... | collective-permute-start | bytes 294920 | tf_op jit(solution)/shard_map/ppermute | solution.py:293
  29.5 11.0 %collective-permute-start.11 = (bf16[2,32,768]{2,1,0:T(8,128)(2,1)S(1)}, bf16[2,32,768]{2,1,0:T(8,128)(2,1)S(1)}, u32[]{:S(2)}, u32[]{:S(2)}) collective-permute-start(bf16[2,32,768]{2,1,0:T(8,128)(2,1)S(1)} %slice.7.refs_0_), channel_id=1, source_target_pairs={{0,24},{8,0},{16,8},{24,16},{1,25},{9,1},{17,9},{25,17},{2,26},{10... | collective-permute-start | bytes 294920 | tf_op jit(solution)/shard_map/ppermute | solution.py:293
  32.1 0.6 copy-start.11
  32.1 8.5 %collective-permute-start.12 = (bf16[2,32,768]{2,1,0:T(8,128)(2,1)S(1)}, bf16[2,32,768]{2,1,0:T(8,128)(2,1)S(1)}, u32[]{:S(2)}, u32[]{:S(2)}) collective-permute-start(bf16[2,32,768]{2,1,0:T(8,128)(2,1)S(1)} %slice.7.refs_0_), channel_id=1, source_target_pairs={{0,16},{8,24},{16,0},{24,8},{1,17},{9,25},{17,1},{25,9},{2,18},{10... | collective-permute-start | bytes 294920 | tf_op jit(solution)/shard_map/ppermute | solution.py:293
  32.5 0.6 copy-start.12
  33.1 0.6 copy-start.13
  38.5 14.9 %collective-permute-start.7 = (bf16[8,32,128]{2,1,0:T(8,128)(2,1)}, bf16[8,32,128]{2,1,0:T(8,128)(2,1)S(1)}, u32[]{:S(2)}, u32[]{:S(2)}) collective-permute-start(bf16[8,32,128]{2,1,0:T(8,128)(2,1)} %get-tuple-element.39), channel_id=1, source_target_pairs={{0,24},{8,0},{16,8},{24,16},{1,25},{9,1},{17,9},{25,17},{2,26},{10... | collective-permute-start | bytes 196616 | tf_op jit(solution)/shard_map/ppermute | solution.py:293
  40.6 0.6 copy-start.8
  40.6 0.7 copy-start.9
  40.6 0.7 copy-start.10
  41.3 9.6 %copy-start.15 = (bf16[8,32,128]{2,1,0:T(8,128)(2,1)S(1)}, bf16[8,32,128]{2,1,0:T(8,128)(2,1)}, u32[]{:S(2)}) copy-start(bf16[8,32,128]{2,1,0:T(8,128)(2,1)} %get-tuple-element.40) | copy-start | bytes 196612
  41.3 12.1 %copy-start.14 = (bf16[8,32,128]{2,1,0:T(8,128)(2,1)S(1)}, bf16[8,32,128]{2,1,0:T(8,128)(2,1)}, u32[]{:S(2)}) copy-start(bf16[8,32,128]{2,1,0:T(8,128)(2,1)} %get-tuple-element.41) | copy-start | bytes 196612
  41.3 17.9 %copy-start.1 = (bf16[8,32,128]{2,1,0:T(8,128)(2,1)S(1)}, bf16[8,32,128]{2,1,0:T(8,128)(2,1)}, u32[]{:S(2)}) copy-start(bf16[8,32,128]{2,1,0:T(8,128)(2,1)} %get-tuple-element.38.refs_0_) | copy-start | bytes 196612
  47.2 11.9 %collective-permute-start.13 = (bf16[8,56,128]{2,1,0:T(8,128)(2,1)}, bf16[8,56,128]{2,1,0:T(8,128)(2,1)S(1)}, u32[]{:S(2)}, u32[]{:S(2)}) collective-permute-start(bf16[8,56,128]{2,1,0:T(8,128)(2,1)} %get-tuple-element.45), channel_id=1, source_target_pairs={{0,24},{8,0},{16,8},{24,16},{1,25},{9,1},{17,9},{25,17},{2,26},{10... | collective-permute-start | bytes 344072 | tf_op jit(solution)/shard_map/ppermute | solution.py:293
  49.3 9.9 %collective-permute-start.14 = (bf16[8,56,128]{2,1,0:T(8,128)(2,1)}, bf16[8,56,128]{2,1,0:T(8,128)(2,1)S(1)}, u32[]{:S(2)}, u32[]{:S(2)}) collective-permute-start(bf16[8,56,128]{2,1,0:T(8,128)(2,1)} %get-tuple-element.46), channel_id=1, source_target_pairs={{0,8},{8,16},{16,24},{24,0},{1,9},{9,17},{17,25},{25,1},{2,10},{10... | collective-permute-start | bytes 344072 | tf_op jit(solution)/shard_map/ppermute | solution.py:293
  49.5 9.6 %collective-permute-start.15 = (bf16[8,56,128]{2,1,0:T(8,128)(2,1)}, bf16[8,56,128]{2,1,0:T(8,128)(2,1)S(1)}, u32[]{:S(2)}, u32[]{:S(2)}) collective-permute-start(bf16[8,56,128]{2,1,0:T(8,128)(2,1)} %get-tuple-element.47), channel_id=1, source_target_pairs={{0,16},{8,24},{16,0},{24,8},{1,17},{9,25},{17,1},{25,9},{2,18},{10... | collective-permute-start | bytes 344072 | tf_op jit(solution)/shard_map/ppermute | solution.py:293
  50.9 6.6 %collective-permute-start.8 = (bf16[8,32,128]{2,1,0:T(8,128)(2,1)S(1)}, bf16[8,32,128]{2,1,0:T(8,128)(2,1)S(1)}, u32[]{:S(2)}, u32[]{:S(2)}) collective-permute-start(bf16[8,32,128]{2,1,0:T(8,128)(2,1)S(1)} %copy-done.15), channel_id=1, source_target_pairs={{0,8},{8,16},{16,24},{24,0},{1,9},{9,17},{17,25},{25,1},{2,10},{10... | collective-permute-start | bytes 196616 | tf_op jit(solution)/shard_map/ppermute | solution.py:293
  53.4 5.8 %collective-permute-start.9 = (bf16[8,32,128]{2,1,0:T(8,128)(2,1)S(1)}, bf16[8,32,128]{2,1,0:T(8,128)(2,1)S(1)}, u32[]{:S(2)}, u32[]{:S(2)}) collective-permute-start(bf16[8,32,128]{2,1,0:T(8,128)(2,1)S(1)} %copy-done.14), channel_id=1, source_target_pairs={{0,16},{8,24},{16,0},{24,8},{1,17},{9,25},{17,1},{25,9},{2,18},{10... | collective-permute-start | bytes 196616 | tf_op jit(solution)/shard_map/ppermute | solution.py:293
  59.2 0.9 %copy-start = (bf16[8,56,128]{2,1,0:T(8,128)(2,1)S(1)}, bf16[8,56,128]{2,1,0:T(8,128)(2,1)}, u32[]{:S(2)}) copy-start(bf16[8,56,128]{2,1,0:T(8,128)(2,1)} %get-tuple-element.44.refs_4_) | copy-start | bytes 344068

commit v5 on v3

--- a/solution.py
+++ b/solution.py
@@ -11,6 +11,7 @@
 LANES = 128
 CORES = 2
 Y = 4
+ORDER = (4, 5, 6, 7, 0, 1, 2, 3)
 NT = (((1,), (1,)), ((), ()))
 VMEM_LIMIT = 32 * 1024 * 1024
 
@@ -48,28 +49,27 @@
     return jnp.concatenate([x, x], axis=1)
 
 
-LOADS = 2
-
-
-def spread_kernel(copies, groups, q_ref, qt_ref, out_ref):
-    width = q_ref.shape[1] // groups
+def spread_kernel(copies, groups, row_ref, out_ref):
+    width = row_ref.shape[1] // groups
     for group in range(groups):
-        cols = slice(group * width, (group + 1) * width)
-        pair = jnp.concatenate([q_ref[:, cols], qt_ref[:, cols]], axis=0)
+        pair = row_ref[:, group * width : (group + 1) * width]
         for copy in range(copies):
             out_ref[copy * groups + group] = pair
 
 
-def spread(query, query_tangent, copies, groups):
-    width = query.shape[1] // groups
+def spread(row, copies, groups):
+    arrays, width = row.shape
     vmem = pl.BlockSpec(memory_space=pltpu.VMEM)
     return pl.pallas_call(
         lambda *refs: spread_kernel(copies, groups, *refs),
-        out_shape=jax.ShapeDtypeStruct((copies * groups, 2, width), query.dtype),
-        in_specs=[vmem] * 2,
+        out_shape=jax.ShapeDtypeStruct((copies * groups, arrays, width // groups), row.dtype),
+        in_specs=[vmem],
         out_specs=vmem,
         compiler_params=pltpu.CompilerParams(vmem_limit_bytes=VMEM_LIMIT),
-    )(query, query_tangent)
+    )(row)
+
+
+LOADS = 2
 
 
 def load_kernel(*refs):
@@ -95,12 +95,16 @@
     return pl.pallas_call(
         load_kernel,
         out_shape=[jax.ShapeDtypeStruct(array.shape, array.dtype) for array in arrays],
-        in_specs=[pl.BlockSpec(memory_space=pltpu.HBM)] * count,
+        in_specs=[pl.BlockSpec(memory_space=pl.ANY)] * count,
         out_specs=[pl.BlockSpec(memory_space=pltpu.VMEM)] * count,
         scratch_shapes=[pltpu.SemaphoreType.DMA((count * LOADS,))],
         compiler_params=pltpu.CompilerParams(vmem_limit_bytes=VMEM_LIMIT),
         cost_estimate=pl.CostEstimate(flops=0, bytes_accessed=4 * size, transcendentals=0),
     )(*arrays)
+
+
+def blocks_of(refs):
+    return refs[:4], refs[4:]
 
 
 def attend_kernel(owners, groups, *refs):
@@ -110,45 +114,46 @@
     heads = windows[0].shape[2] // HD
     per_owner = rows // owners
     factor = 1.0 / math.sqrt(HD)
+    power = factor * math.log2(math.e)
     lane = lax.broadcasted_iota(jnp.int32, (total_rows, LANES), 1)
     lses = jnp.zeros((total_rows, LANES), jnp.float32)
     lts = jnp.zeros((total_rows, LANES), jnp.float32)
+    zeros = jnp.zeros((total_rows, HD), jnp.bfloat16)
     pending = None
     for head in range(heads):
         cols = slice(head * HD, (head + 1) * HD)
         q = jnp.concatenate([w[0, :, cols] for w in windows], axis=0)
         qt = jnp.concatenate([w[1, :, cols] for w in windows], axis=0)
-        blocks = [tuple(ref[:, cols] for ref in keys[i : i + 4]) for i in (0, 4)]
-        scores = [nt(q, k) * factor for k, v, kt, vt in blocks]
-        tangents = [(nt(qt, k) + nt(q, kt)) * factor for k, v, kt, vt in blocks]
+        lhs = jnp.concatenate(
+            [jnp.concatenate([q, zeros], axis=1), jnp.concatenate([qt, q], axis=1)], axis=0
+        )
+        scores, tangents, acc = [], [], 0.0
+        for k, v, kt, vt in blocks_of(keys):
+            both = nt(lhs, jnp.concatenate([k[:, cols], kt[:, cols]], axis=1))
+            scores.append(both[:total_rows])
+            tangents.append(both[total_rows:] * factor)
         top = jnp.max(jnp.maximum(scores[0], scores[1]), axis=1, keepdims=True)
-        weights = [jnp.exp(s - top) for s in scores]
+        weights = [jnp.exp2((s - top) * power) for s in scores]
         products = [w * t for w, t in zip(weights, tangents)]
         total = jnp.sum(weights[0] + weights[1], axis=1, keepdims=True)
         slope = jnp.sum(products[0] + products[1], axis=1, keepdims=True)
-        out = jnp.zeros((total_rows, HD), jnp.float32)
-        out_tangent = jnp.zeros((total_rows, HD), jnp.float32)
-        for w, p, (k, v, kt, vt) in zip(weights, products, blocks):
-            rounded = w.astype(jnp.bfloat16)
-            out += nn(rounded, v)
-            out_tangent += nn(p.astype(jnp.bfloat16), v) + nn(rounded, vt)
+        for w, p, (k, v, kt, vt) in zip(weights, products, blocks_of(keys)):
+            both = jnp.concatenate([w.astype(jnp.bfloat16), p.astype(jnp.bfloat16)], axis=0)
+            acc += nn(both, jnp.concatenate([v[:, cols], vt[:, cols]], axis=1))
         inverse = 1.0 / total
         lt = slope * inverse
-        out = out * inverse
-        out_tangent = out_tangent * inverse - lt * out
-        lses = jnp.where(lane == head, top + jnp.log(total), lses)
+        out = acc[:total_rows, :HD] * inverse
+        out_tangent = (acc[total_rows:, :HD] + acc[:total_rows, HD:]) * inverse - lt * out
+        lses = jnp.where(lane == head, top * factor + jnp.log(total), lses)
         lts = jnp.where(lane == head, lt, lts)
-        tile = jnp.concatenate(
-            [
-                out.reshape(groups * owners, per_owner, HD),
-                out_tangent.reshape(groups * owners, per_owner, HD),
-            ],
-            axis=1,
-        )
+        tile = [
+            x.reshape(groups * owners, per_owner, HD) for x in (out, out_tangent)
+        ]
         if pending is None:
             pending = tile
             continue
-        tile = jnp.concatenate([pending, tile], axis=1).astype(jnp.bfloat16)
+        tile = [pending[0], tile[0], pending[1], tile[1]]
+        tile = jnp.concatenate(tile, axis=1).astype(jnp.bfloat16)
         pending = None
         span = tile.shape[1]
         start = (head // 2) * span
@@ -182,6 +187,12 @@
     )(*windows, *own, *other)
 
 
+def pairs(x):
+    half = x.shape[-2] // 2
+    row = lax.broadcasted_iota(jnp.int32, x.shape, x.ndim - 2)
+    return jnp.where(row < half, x, pltpu.roll(x, LANES - 1, x.ndim - 1))
+
+
 def merge_weights(stats, heads):
     decoded = [decode(s.astype(jnp.float32), heads) for s in stats]
     top = decoded[0][0]
@@ -193,35 +204,34 @@
     scales = [scale * inverse for scale in scales]
     lt = sum(scale * part for scale, (_, part) in zip(scales, decoded))
     shifts = [scale * (part - lt) for scale, (_, part) in zip(scales, decoded)]
-    return scales, shifts, top + jnp.log(total), lt
+    return [pairs(x) for x in scales], [pairs(x) for x in shifts], top + jnp.log(total), lt
 
 
 def merge_group_kernel(heads, *refs):
     sources, out_ref = refs[:-1], refs[-1]
     owners, message_rows, _ = out_ref.shape
     span = message_rows // (heads + 1)
-    half = span // 2
     scales, shifts, lse, lt = merge_weights(
         [ref[:, heads * span : (heads + 1) * span, :] for ref in sources], heads
     )
-    tangent_row = lax.broadcasted_iota(jnp.int32, (owners, span, HD), 1) >= half
     for pair in range(heads // 2):
-        tiles = []
-        for head in (2 * pair, 2 * pair + 1):
-            rows = slice(head * span, (head + 1) * span)
-            merged = moved = 0.0
-            for ref, scale, shift in zip(sources, scales, shifts):
-                values = ref[:, rows, :].astype(jnp.float32)
-                merged += values * scale[:, :, head : head + 1]
-                moved += values * shift[:, :, head : head + 1]
-            moved = pltpu.roll(moved, half, 1)
-            tiles.append(jnp.where(tangent_row, merged + moved, merged))
-        start = pair * 2 * span
-        tile = jnp.concatenate(tiles, axis=1).astype(jnp.bfloat16)
-        out_ref[:, start : start + 2 * span, :] = tile
+        head = 2 * pair
+        start = head * span
+        out = tangent = 0.0
+        for ref, scale, shift in zip(sources, scales, shifts):
+            values = ref[:, start : start + span, :].astype(jnp.float32)
+            tangents = ref[:, start + span : start + 2 * span, :].astype(jnp.float32)
+            scale = scale[:, :, head : head + 1]
+            out += values * scale
+            tangent += tangents * scale + values * shift[:, :, head : head + 1]
+        tile = jnp.concatenate([out, tangent], axis=1).astype(jnp.bfloat16)
+        for slot, owner in enumerate(ORDER):
+            out_ref[slot, start : start + 2 * span, :] = tile[owner]
     lane = lax.broadcasted_iota(jnp.int32, lse.shape, 2)
     stats = encode(jnp.where(lane < heads, lse, 0.0), jnp.where(lane < heads, lt, 0.0), heads)
-    out_ref[:, heads * span : (heads + 1) * span, :] = stats.astype(jnp.bfloat16)
+    stats = stats.astype(jnp.bfloat16)
+    for slot, owner in enumerate(ORDER):
+        out_ref[slot, heads * span : (heads + 1) * span, :] = stats[owner]
 
 
 def merge_group(messages, heads):
@@ -241,16 +251,20 @@
     stats = msg_ref[:, heads * span : (heads + 1) * span, :]
     count = msg_ref.shape[0]
     scales, shifts, lse, lt = merge_weights([stats[i] for i in range(count)], heads)
-    for head in range(heads):
-        rows = slice(head * span, (head + 1) * span)
-        merged = moved = 0.0
+    for head in range(0, heads, 2):
+        start = head * span
+        out = tangent = 0.0
         for i, (scale, shift) in enumerate(zip(scales, shifts)):
-            values = msg_ref[i, rows, :].astype(jnp.float32)
-            merged += values * scale[:, head : head + 1]
-            moved += values * shift[:, head : head + 1]
-        cols = slice(head * HD, (head + 1) * HD)
-        out_ref[:, cols] = merged[:half]
-        out_tangent_ref[:, cols] = merged[half:] + moved[:half]
+            values = msg_ref[i, start : start + span, :].astype(jnp.float32)
+            tangents = msg_ref[i, start + span : start + 2 * span, :].astype(jnp.float32)
+            scale = scale[:, head : head + 1]
+            out += values * scale
+            tangent += tangents * scale + values * shift[:, head : head + 1]
+        for j in range(2):
+            rows = slice(j * half, (j + 1) * half)
+            cols = slice((head + j) * HD, (head + j + 1) * HD)
+            out_ref[:, cols] = out[rows]
+            out_tangent_ref[:, cols] = tangent[rows]
     lse_ref[...] = lse[:half, :heads]
     lt_ref[...] = lt[:half, :heads]
 
@@ -277,20 +291,23 @@
 
 def per_device(query, query_tangent, keys, values, key_tangent, value_tangent):
     own = (keys, values, key_tangent, value_tangent)
-    other = tuple(lax.ppermute(array, "core", [(0, 1), (1, 0)]) for array in own)
     owners = lax.axis_size("z")
     heads = keys.shape[1] // HD
-    row = spread(query, query_tangent, owners, lax.axis_size("x"))
-    row, own = lax.optimization_barrier((row, own))
+    row = jnp.concatenate([query, query_tangent], axis=0)
+    row = spread(row, owners, lax.axis_size("x"))
+    other = tuple(lax.ppermute(array, "core", [(0, 1), (1, 0)]) for array in own)
     window = lax.all_to_all(row, ("z", "x"), split_axis=0, concat_axis=0, tiled=True)
     window = jnp.transpose(window, (1, 0, 2))
-    window, own, other = lax.optimization_barrier((window, load(own), other))
-    steps = (1, 3, 2)
+    window, own, other = lax.optimization_barrier((window, own, other))
+    own = load(own)
+    steps = (2, 1, 3)
     windows = [window] + [shift(window, step) for step in steps]
     messages = attend(windows, own, other, owners)
     messages = [messages[0]] + [shift(m, -step) for m, step in zip(messages[1:], steps)]
     message = merge_group(messages, heads)
-    message = lax.all_to_all(message, "z", split_axis=0, concat_axis=0, tiled=True)
+    message = lax.all_to_all(
+        message, "z", split_axis=0, concat_axis=0, tiled=True, axis_index_groups=[list(ORDER)]
+    )
     return merge(message, heads)
 
 

time: 74.2 us -> 60.6 us (0.82)
  blocking collectives: 16.4 us -> 32.1 us
  starting transfers between devices: 22.2 us -> 9.08 us
  local copies, waits for them, and re-layouts: 11.6 us -> 3.28 us
  waiting for transfers between devices: 15.2 us -> 9.14 us
  Pallas kernels: 7.36 us -> 4.88 us
  other arithmetic: 0 us -> 0.8 us
    all_to_all x1 -> x2, blocking collectives: 16.4 us -> 32.1 us  [the longest x1 20.8 us: per_device(): lax.all_to_all(row, ('z', 'x'), split_axis=0, concat_axis=0, tiled=True)]
    all_to_all x1 -> x0, starting transfers between devices: 11.6 us -> none  [per_device(): lax.all_to_all(row, ('z', 'x'), split_axis=0, concat_axis=0, tiled=True)]
    unnamed x24 -> x8, local copies, waits for them, and re-layouts: 11.6 us -> 3.27 us
    ppermute x6, waiting for transfers between devices: 13.7 us -> 9.13 us  [shift(): lax.ppermute(array, 'y', [(i, (i + step) % count) for i in range(count)])]
    pallas_call x1, Pallas kernels: 3.8 us -> 2.26 us  [attend(): pl.pallas_call(lambda *refs: attend_kernel(owners, groups, *refs), out_sh...]
    all_to_all x1 -> x0, waiting for transfers between devices: 1.53 us -> none  [per_device(): lax.all_to_all(row, ('z', 'x'), split_axis=0, concat_axis=0, tiled=True)]
    ppermute x6, starting transfers between devices: 9.49 us -> 7.98 us  [shift(): lax.ppermute(array, 'y', [(i, (i + step) % count) for i in range(count)])]
    concatenate x0 -> x1, other arithmetic: none -> 0.8 us  [per_device(): row = jnp.concatenate([query, query_tangent], axis=0)]
  transfers between devices with their start and end apart: 11 -> 10, of which waited for: 6 -> 4; matrix products, arithmetic and copies ran while one was open for 0% -> 1% of each run, Pallas kernels for 2% -> 2%
where the time goes in v5:
time: 60.6 us; the launch traced here: 60 us
  blocking collectives  32.1 us (53%)
  waiting for transfers between devices  9.14 us (15%)
  starting transfers between devices  9.08 us (15%)
  Pallas kernels  4.88 us (8%)
  local copies, waits for them, and re-layouts  3.28 us (5%)
  other arithmetic  0.8 us (1%)
  between operations  0.73 us (1%)
    all_to_all x1, blocking collectives, per_device(): lax.all_to_all(row, ('z', 'x'), split_axis=0, concat_axis=0, tiled=True)  20.8 us
    all_to_all x1, blocking collectives, per_device(): lax.all_to_all(message, 'z', split_axis=0, concat_axis=0, tiled=True, axi...  11.3 us
    ppermute x6, waiting for transfers between devices, shift(): lax.ppermute(array, 'y', [(i, (i + step) % count) for i in range(count)])  9.13 us
    ppermute x6, starting transfers between devices, shift(): lax.ppermute(array, 'y', [(i, (i + step) % count) for i in range(count)])  7.98 us
    unnamed x8, local copies, waits for them, and re-layouts  3.27 us
    pallas_call x1, Pallas kernels, attend(): pl.pallas_call(lambda *refs: attend_kernel(owners, groups, *refs), out_sh...  2.26 us
  transfers between devices with their start and end apart: 10, of which 4 were waited for; matrix products, arithmetic and copies ran while one was open for 1% of the time, Pallas kernels for 2%

profile of v5, /device:TPU:2, one launch (start us, length us, event | category | flops | bytes accessed | tf_op | source)
XLA Modules:
  0.0 60.0 jit_solution(1492276690977506858)
XLA Ops:
  0.6 0.0 copy-start
  0.6 0.1 collective-permute-start
  0.7 0.5 collective-permute-start.1
  1.2 0.1 collective-permute-start.2
  1.3 0.4 collective-permute-start.3
  1.8 0.8 %pad_maximum_fusion.refs_0_ = bf16[2,5120]{1,0:T(2,128)(2,1)S(1)} fusion(bf16[1,5120]{1,0:T(2,128)(2,1)} %param.7, bf16[1,5120]{1,0:T(2,128)(2,1)} %param.6), kind=kLoop, calls=%fused_computation.1 | loop fusion | flops 40960 | bytes 40960 | tf_op jit(solution)/shard_map/concatenate | solution.py:296
  2.6 20.8 %all_to_all.10 = bf16[32,2,1280]{2,1,0:T(2,128)(2,1)S(1)} all-to-all(bf16[32,2,1280]{2,1,0:T(2,128)(2,1)S(1)} %shard_map.93), channel_id=1, replica_groups=mesh['z'=8,'y'=4,'core'=2,'x'=4] {'z','x'}, dimensions={0} | all-to-all | bytes 327680 | tf_op jit(solution)/shard_map/all_to_all | solution.py:299
  23.4 0.0 collective-permute-done.refs_8_
  23.4 0.0 collective-permute-done.1.refs_9_
  23.4 0.0 collective-permute-done.2.refs_10_
  23.4 0.0 collective-permute-done.3.refs_11_
  23.4 3.1 %collective-permute-start.6 = (bf16[2,32,1280]{2,1,0:T(8,128)(2,1)S(1)}, bf16[2,32,1280]{2,1,0:T(8,128)(2,1)S(1)}, u32[]{:S(2)}, u32[]{:S(2)}) collective-permute-start(bf16[2,32,1280]{2,1,0:T(8,128)(2,1)S(1)} %bitcast.5), channel_id=1, source_target_pairs={{0,24},{8,0},{16,8},{24,16},{1,25},{9,1},{17,9},{25,17},{2,26},{10... | collective-permute-start | bytes 491528 | tf_op jit(solution)/shard_map/ppermute | solution.py:289
  26.5 0.0 collective-permute-start.5
  26.5 2.2 %collective-permute-start.4 = (bf16[2,32,1280]{2,1,0:T(8,128)(2,1)S(1)}, bf16[2,32,1280]{2,1,0:T(8,128)(2,1)S(1)}, u32[]{:S(2)}, u32[]{:S(2)}) collective-permute-start(bf16[2,32,1280]{2,1,0:T(8,128)(2,1)S(1)} %bitcast.7), channel_id=1, source_target_pairs={{0,16},{8,24},{16,0},{24,8},{1,17},{9,25},{17,1},{25,9},{2,18},{10... | collective-permute-start | bytes 491528 | tf_op jit(solution)/shard_map/ppermute | solution.py:289
  28.7 0.0 copy-done
  28.7 0.0 copy-start.1
  28.7 1.1 %copy-done.1 = bf16[256,1280]{1,0:T(8,128)(2,1)S(1)} copy-done((bf16[256,1280]{1,0:T(8,128)(2,1)S(1)}, bf16[256,1280]{1,0:T(8,128)(2,1)}, u32[]{:S(2)}) %copy-start.1) | copy-done | bytes 655384
  29.8 0.0 copy-start.2
  29.8 1.1 %copy-done.2 = bf16[256,1280]{1,0:T(8,128)(2,1)S(1)} copy-done((bf16[256,1280]{1,0:T(8,128)(2,1)S(1)}, bf16[256,1280]{1,0:T(8,128)(2,1)}, u32[]{:S(2)}) %copy-start.2) | copy-done | bytes 655384
  30.9 0.0 copy-start.3
  30.9 1.1 %copy-done.3 = bf16[256,1280]{1,0:T(8,128)(2,1)S(1)} copy-done((bf16[256,1280]{1,0:T(8,128)(2,1)S(1)}, bf16[256,1280]{1,0:T(8,128)(2,1)}, u32[]{:S(2)}) %copy-start.3) | copy-done | bytes 655384
  32.0 0.9 %shard_map.94 = (bf16[256,1280]{1,0:T(8,128)(2,1)S(1)}, bf16[256,1280]{1,0:T(8,128)(2,1)S(1)}, bf16[256,1280]{1,0:T(8,128)(2,1)S(1)}, bf16[256,1280]{1,0:T(8,128)(2,1)S(1)}) custom-call(bf16[256,1280]{1,0:T(8,128)(2,1)S(1)} %copy-done, bf16[256,1280]{1,0:T(8,128)(2,1)S(1)} %copy-done.1, bf16[256,1280]{1,0:T(8,128)(2,1)S(1)} %copy-done.2, ...), custom_call_target="tpu_custom_call" | custom-call | bytes 5242880 | tf_op jit(solution)/shard_map/pallas_call | solution.py:95
  32.9 0.0 collective-permute-done.6.refs_3_
  32.9 2.8 %collective-permute-done.5.refs_2_ = bf16[2,32,1280]{2,1,0:T(8,128)(2,1)S(1)} collective-permute-done((bf16[2,32,1280]{2,1,0:T(8,128)(2,1)S(1)}, bf16[2,32,1280]{2,1,0:T(8,128)(2,1)S(1)}, u32[]{:S(2)}, u32[]{:S(2)}) %collective-permute-start.5) | collective-permute-done | bytes 163872 | tf_op jit(solution)/shard_map/ppermute | solution.py:289
  35.7 0.0 collective-permute-done.4.refs_1_
  35.7 2.3 %shard_map.95 = (bf16[8,88,128]{2,1,0:T(8,128)(2,1)S(1)}, bf16[8,88,128]{2,1,0:T(8,128)(2,1)S(1)}, bf16[8,88,128]{2,1,0:T(8,128)(2,1)S(1)}, bf16[8,88,128]{2,1,0:T(8,128)(2,1)S(1)}) custom-call(bf16[2,32,1280]{2,1,0:T(8,128)(2,1)S(1)} %bitcast.8, bf16[2,32,1280]{2,1,0:T(8,128)(2,1)S(1)} %collective-permute-done.4.refs_1_, ...), custom_call_target="tpu_custom_call" | custom-call | flops 1006632960 | bytes 5242880 | tf_op jit(solution)/shard_map/pallas_call | solution.py:176
  38.0 0.7 %collective-permute-start.7 = (bf16[8,88,128]{2,1,0:T(8,128)(2,1)S(1)}, bf16[8,88,128]{2,1,0:T(8,128)(2,1)S(1)}, u32[]{:S(2)}, u32[]{:S(2)}) collective-permute-start(bf16[8,88,128]{2,1,0:T(8,128)(2,1)S(1)} %get-tuple-element.39), channel_id=1, source_target_pairs={{0,16},{8,24},{16,0},{24,8},{1,17},{9,25},{17,1},{25,9},{2,18},{10... | collective-permute-start | bytes 540680 | tf_op jit(solution)/shard_map/ppermute | solution.py:289
  38.6 1.2 %collective-permute-start.8 = (bf16[8,88,128]{2,1,0:T(8,128)(2,1)S(1)}, bf16[8,88,128]{2,1,0:T(8,128)(2,1)S(1)}, u32[]{:S(2)}, u32[]{:S(2)}) collective-permute-start(bf16[8,88,128]{2,1,0:T(8,128)(2,1)S(1)} %get-tuple-element.40), channel_id=1, source_target_pairs={{0,24},{8,0},{16,8},{24,16},{1,25},{9,1},{17,9},{25,17},{2,26},{10... | collective-permute-start | bytes 540680 | tf_op jit(solution)/shard_map/ppermute | solution.py:289
  39.8 0.8 %collective-permute-start.9 = (bf16[8,88,128]{2,1,0:T(8,128)(2,1)S(1)}, bf16[8,88,128]{2,1,0:T(8,128)(2,1)S(1)}, u32[]{:S(2)}, u32[]{:S(2)}) collective-permute-start(bf16[8,88,128]{2,1,0:T(8,128)(2,1)S(1)} %get-tuple-element.41), channel_id=1, source_target_pairs={{0,8},{8,16},{16,24},{24,0},{1,9},{9,17},{17,25},{25,1},{2,10},{10... | collective-permute-start | bytes 540680 | tf_op jit(solution)/shard_map/ppermute | solution.py:289
  40.7 4.4 %collective-permute-done.7.refs_1_ = bf16[8,88,128]{2,1,0:T(8,128)(2,1)S(1)} collective-permute-done((bf16[8,88,128]{2,1,0:T(8,128)(2,1)S(1)}, bf16[8,88,128]{2,1,0:T(8,128)(2,1)S(1)}, u32[]{:S(2)}, u32[]{:S(2)}) %collective-permute-start.7) | collective-permute-done | bytes 180256 | tf_op jit(solution)/shard_map/ppermute | solution.py:289
  45.1 0.1 collective-permute-done.8.refs_2_
  45.2 1.8 %collective-permute-done.9.refs_3_ = bf16[8,88,128]{2,1,0:T(8,128)(2,1)S(1)} collective-permute-done((bf16[8,88,128]{2,1,0:T(8,128)(2,1)S(1)}, bf16[8,88,128]{2,1,0:T(8,128)(2,1)S(1)}, u32[]{:S(2)}, u32[]{:S(2)}) %collective-permute-start.9) | collective-permute-done | bytes 180256 | tf_op jit(solution)/shard_map/ppermute | solution.py:289
  47.0 0.7 %shard_map.96 = bf16[8,88,128]{2,1,0:T(8,128)(2,1)S(1)} custom-call(bf16[8,88,128]{2,1,0:T(8,128)(2,1)S(1)} %get-tuple-element.38.refs_0_, bf16[8,88,128]{2,1,0:T(8,128)(2,1)S(1)} %collective-permute-done.7.refs_1_, bf16[8,88,128]{2,1,0:T(8,128)(2,1)S(1)} %collective-permute-done.8.refs_2_, bf16[8,88,128]{2,1,0:T(8,128)(2,1)S(1)} %collective-permute-done.9.refs_3_), custom_call_target="tpu_custom_call" | custom-call | tf_op jit(solution)/shard_map/pallas_call | solution.py:239
  47.7 11.3 %all_to_all.11.refs_0_ = bf16[8,88,128]{2,1,0:T(8,128)(2,1)S(1)} all-to-all(bf16[8,88,128]{2,1,0:T(8,128)(2,1)S(1)} %shard_map.96), channel_id=1, replica_groups={{128,160,192,224,0,32,64,96},{129,161,193,225,1,33,65,97},{130,162,194,..., dimensions={0} | all-to-all | bytes 360448 | tf_op jit(solution)/shard_map/all_to_all | solution.py:308
  59.0 1.0 %shard_map.97 = (f32[4,1280]{1,0:T(4,128)}, f32[4,1280]{1,0:T(4,128)}, f32[4,10]{1,0:T(4,128)}, f32[4,10]{1,0:T(4,128)}) custom-call(bf16[8,88,128]{2,1,0:T(8,128)(2,1)S(1)} %all_to_all.11.refs_0_), custom_call_target="tpu_custom_call" | custom-call | tf_op jit(solution)/shard_map/pallas_call | solution.py:277
  (2 shorter events, 0.0 us)
Async XLA Ops:
  0.6 28.1 %copy-start = (bf16[256,1280]{1,0:T(8,128)(2,1)S(1)}, bf16[256,1280]{1,0:T(8,128)(2,1)}, u32[]{:S(2)}) copy-start(bf16[256,1280]{1,0:T(8,128)(2,1)} %refs_0_) | copy-start | bytes 1966084
  0.6 22.7 %collective-permute-start = (bf16[256,1280]{1,0:T(8,128)(2,1)}, bf16[256,1280]{1,0:T(8,128)(2,1)S(1)}, u32[]{:S(2)}, u32[]{:S(2)}) collective-permute-start(bf16[256,1280]{1,0:T(8,128)(2,1)} %refs_0_), channel_id=1, source_target_pairs={{0,4},{4,0},{1,5},{5,1},{2,6},{6,2},{3,7},{7,3},{8,12},{12,8},{9,1... | collective-permute-start | bytes 1966088 | tf_op jit(solution)/shard_map/ppermute | solution.py:298
  0.7 22.7 %collective-permute-start.1 = (bf16[256,1280]{1,0:T(8,128)(2,1)}, bf16[256,1280]{1,0:T(8,128)(2,1)S(1)}, u32[]{:S(2)}, u32[]{:S(2)}) collective-permute-start(bf16[256,1280]{1,0:T(8,128)(2,1)} %refs_1_), channel_id=1, source_target_pairs={{0,4},{4,0},{1,5},{5,1},{2,6},{6,2},{3,7},{7,3},{8,12},{12,8},{9,1... | collective-permute-start | bytes 1966088 | tf_op jit(solution)/shard_map/ppermute | solution.py:298
  1.2 22.2 %collective-permute-start.2 = (bf16[256,1280]{1,0:T(8,128)(2,1)}, bf16[256,1280]{1,0:T(8,128)(2,1)S(1)}, u32[]{:S(2)}, u32[]{:S(2)}) collective-permute-start(bf16[256,1280]{1,0:T(8,128)(2,1)} %refs_2_), channel_id=1, source_target_pairs={{0,4},{4,0},{1,5},{5,1},{2,6},{6,2},{3,7},{7,3},{8,12},{12,8},{9,1... | collective-permute-start | bytes 1966088 | tf_op jit(solution)/shard_map/ppermute | solution.py:298
  1.3 22.1 %collective-permute-start.3 = (bf16[256,1280]{1,0:T(8,128)(2,1)}, bf16[256,1280]{1,0:T(8,128)(2,1)S(1)}, u32[]{:S(2)}, u32[]{:S(2)}) collective-permute-start(bf16[256,1280]{1,0:T(8,128)(2,1)} %refs_3_), channel_id=1, source_target_pairs={{0,4},{4,0},{1,5},{5,1},{2,6},{6,2},{3,7},{7,3},{8,12},{12,8},{9,1... | collective-permute-start | bytes 1966088 | tf_op jit(solution)/shard_map/ppermute | solution.py:298
  23.4 9.5 %collective-permute-start.6 = (bf16[2,32,1280]{2,1,0:T(8,128)(2,1)S(1)}, bf16[2,32,1280]{2,1,0:T(8,128)(2,1)S(1)}, u32[]{:S(2)}, u32[]{:S(2)}) collective-permute-start(bf16[2,32,1280]{2,1,0:T(8,128)(2,1)S(1)} %bitcast.5), channel_id=1, source_target_pairs={{0,24},{8,0},{16,8},{24,16},{1,25},{9,1},{17,9},{25,17},{2,26},{10... | collective-permute-start | bytes 491528 | tf_op jit(solution)/shard_map/ppermute | solution.py:289
  26.5 9.2 %collective-permute-start.5 = (bf16[2,32,1280]{2,1,0:T(8,128)(2,1)S(1)}, bf16[2,32,1280]{2,1,0:T(8,128)(2,1)S(1)}, u32[]{:S(2)}, u32[]{:S(2)}) collective-permute-start(bf16[2,32,1280]{2,1,0:T(8,128)(2,1)S(1)} %bitcast.6), channel_id=1, source_target_pairs={{0,8},{8,16},{16,24},{24,0},{1,9},{9,17},{17,25},{25,1},{2,10},{10... | collective-permute-start | bytes 491528 | tf_op jit(solution)/shard_map/ppermute | solution.py:289
  26.5 9.2 %collective-permute-start.4 = (bf16[2,32,1280]{2,1,0:T(8,128)(2,1)S(1)}, bf16[2,32,1280]{2,1,0:T(8,128)(2,1)S(1)}, u32[]{:S(2)}, u32[]{:S(2)}) collective-permute-start(bf16[2,32,1280]{2,1,0:T(8,128)(2,1)S(1)} %bitcast.7), channel_id=1, source_target_pairs={{0,16},{8,24},{16,0},{24,8},{1,17},{9,25},{17,1},{25,9},{2,18},{10... | collective-permute-start | bytes 491528 | tf_op jit(solution)/shard_map/ppermute | solution.py:289
  28.7 1.1 %copy-start.1 = (bf16[256,1280]{1,0:T(8,128)(2,1)S(1)}, bf16[256,1280]{1,0:T(8,128)(2,1)}, u32[]{:S(2)}) copy-start(bf16[256,1280]{1,0:T(8,128)(2,1)} %refs_1_) | copy-start | bytes 1966084
  29.8 1.1 %copy-start.2 = (bf16[256,1280]{1,0:T(8,128)(2,1)S(1)}, bf16[256,1280]{1,0:T(8,128)(2,1)}, u32[]{:S(2)}) copy-start(bf16[256,1280]{1,0:T(8,128)(2,1)} %refs_2_) | copy-start | bytes 1966084
  30.9 1.1 %copy-start.3 = (bf16[256,1280]{1,0:T(8,128)(2,1)S(1)}, bf16[256,1280]{1,0:T(8,128)(2,1)}, u32[]{:S(2)}) copy-start(bf16[256,1280]{1,0:T(8,128)(2,1)} %refs_3_) | copy-start | bytes 1966084
  38.0 7.1 %collective-permute-start.7 = (bf16[8,88,128]{2,1,0:T(8,128)(2,1)S(1)}, bf16[8,88,128]{2,1,0:T(8,128)(2,1)S(1)}, u32[]{:S(2)}, u32[]{:S(2)}) collective-permute-start(bf16[8,88,128]{2,1,0:T(8,128)(2,1)S(1)} %get-tuple-element.39), channel_id=1, source_target_pairs={{0,16},{8,24},{16,0},{24,8},{1,17},{9,25},{17,1},{25,9},{2,18},{10... | collective-permute-start | bytes 540680 | tf_op jit(solution)/shard_map/ppermute | solution.py:289
  38.6 6.6 %collective-permute-start.8 = (bf16[8,88,128]{2,1,0:T(8,128)(2,1)S(1)}, bf16[8,88,128]{2,1,0:T(8,128)(2,1)S(1)}, u32[]{:S(2)}, u32[]{:S(2)}) collective-permute-start(bf16[8,88,128]{2,1,0:T(8,128)(2,1)S(1)} %get-tuple-element.40), channel_id=1, source_target_pairs={{0,24},{8,0},{16,8},{24,16},{1,25},{9,1},{17,9},{25,17},{2,26},{10... | collective-permute-start | bytes 540680 | tf_op jit(solution)/shard_map/ppermute | solution.py:289
  39.8 7.1 %collective-permute-start.9 = (bf16[8,88,128]{2,1,0:T(8,128)(2,1)S(1)}, bf16[8,88,128]{2,1,0:T(8,128)(2,1)S(1)}, u32[]{:S(2)}, u32[]{:S(2)}) collective-permute-start(bf16[8,88,128]{2,1,0:T(8,128)(2,1)S(1)} %get-tuple-element.41), channel_id=1, source_target_pairs={{0,8},{8,16},{16,24},{24,0},{1,9},{9,17},{17,25},{25,1},{2,10},{10... | collective-permute-start | bytes 540680 | tf_op jit(solution)/shard_map/ppermute | solution.py:289

commit v6 on v5

--- a/solution.py
+++ b/solution.py
@@ -219,8 +219,8 @@
         start = head * span
         out = tangent = 0.0
         for ref, scale, shift in zip(sources, scales, shifts):
-            values = ref[:, start : start + span, :].astype(jnp.float32)
-            tangents = ref[:, start + span : start + 2 * span, :].astype(jnp.float32)
+            block = ref[:, start : start + 2 * span, :].astype(jnp.float32)
+            values, tangents = block[:, :span], block[:, span:]
             scale = scale[:, :, head : head + 1]
             out += values * scale
             tangent += tangents * scale + values * shift[:, :, head : head + 1]
@@ -255,8 +255,8 @@
         start = head * span
         out = tangent = 0.0
         for i, (scale, shift) in enumerate(zip(scales, shifts)):
-            values = msg_ref[i, start : start + span, :].astype(jnp.float32)
-            tangents = msg_ref[i, start + span : start + 2 * span, :].astype(jnp.float32)
+            block = msg_ref[i, start : start + 2 * span, :].astype(jnp.float32)
+            values, tangents = block[:span], block[span:]
             scale = scale[:, head : head + 1]
             out += values * scale
             tangent += tangents * scale + values * shift[:, head : head + 1]

time: 60.6 us -> 60.6 us (level)
  no operation moved by 1% of the time
where the time goes in v6:
time: 60.6 us; the launch traced here: 60 us
  blocking collectives  32.1 us (53%)
  waiting for transfers between devices  9.14 us (15%)
  starting transfers between devices  9.08 us (15%)
  Pallas kernels  4.88 us (8%)
  local copies, waits for them, and re-layouts  3.28 us (5%)
  other arithmetic  0.8 us (1%)
  between operations  0.73 us (1%)
    all_to_all x1, blocking collectives, per_device(): lax.all_to_all(row, ('z', 'x'), split_axis=0, concat_axis=0, tiled=True)  20.8 us
    all_to_all x1, blocking collectives, per_device(): lax.all_to_all(message, 'z', split_axis=0, concat_axis=0, tiled=True, axi...  11.3 us
    ppermute x6, waiting for transfers between devices, shift(): lax.ppermute(array, 'y', [(i, (i + step) % count) for i in range(count)])  9.13 us
    ppermute x6, starting transfers between devices, shift(): lax.ppermute(array, 'y', [(i, (i + step) % count) for i in range(count)])  7.98 us
    unnamed x8, local copies, waits for them, and re-layouts  3.27 us
    pallas_call x1, Pallas kernels, attend(): pl.pallas_call(lambda *refs: attend_kernel(owners, groups, *refs), out_sh...  2.26 us
  transfers between devices with their start and end apart: 10, of which 4 were waited for; matrix products, arithmetic and copies ran while one was open for 1% of the time, Pallas kernels for 2%

profile of v6, /device:TPU:2, one launch (start us, length us, event | category | flops | bytes accessed | tf_op | source)
XLA Modules:
  0.0 60.0 jit_solution(6118926606784215214)
XLA Ops:
  0.6 0.0 copy-start
  0.6 0.1 collective-permute-start
  0.7 0.5 collective-permute-start.1
  1.2 0.1 collective-permute-start.2
  1.3 0.4 collective-permute-start.3
  1.8 0.8 %pad_maximum_fusion.refs_0_ = bf16[2,5120]{1,0:T(2,128)(2,1)S(1)} fusion(bf16[1,5120]{1,0:T(2,128)(2,1)} %param.7, bf16[1,5120]{1,0:T(2,128)(2,1)} %param.6), kind=kLoop, calls=%fused_computation.1 | loop fusion | flops 40960 | bytes 40960 | tf_op jit(solution)/shard_map/concatenate | solution.py:296
  2.6 20.8 %all_to_all.10 = bf16[32,2,1280]{2,1,0:T(2,128)(2,1)S(1)} all-to-all(bf16[32,2,1280]{2,1,0:T(2,128)(2,1)S(1)} %shard_map.93), channel_id=1, replica_groups=mesh['z'=8,'y'=4,'core'=2,'x'=4] {'z','x'}, dimensions={0} | all-to-all | bytes 327680 | tf_op jit(solution)/shard_map/all_to_all | solution.py:299
  23.4 0.0 collective-permute-done.refs_8_
  23.4 0.0 collective-permute-done.1.refs_9_
  23.4 0.0 collective-permute-done.2.refs_10_
  23.4 0.0 collective-permute-done.3.refs_11_
  23.4 3.1 %collective-permute-start.6 = (bf16[2,32,1280]{2,1,0:T(8,128)(2,1)S(1)}, bf16[2,32,1280]{2,1,0:T(8,128)(2,1)S(1)}, u32[]{:S(2)}, u32[]{:S(2)}) collective-permute-start(bf16[2,32,1280]{2,1,0:T(8,128)(2,1)S(1)} %bitcast.5), channel_id=1, source_target_pairs={{0,24},{8,0},{16,8},{24,16},{1,25},{9,1},{17,9},{25,17},{2,26},{10... | collective-permute-start | bytes 491528 | tf_op jit(solution)/shard_map/ppermute | solution.py:289
  26.5 0.0 collective-permute-start.5
  26.5 2.2 %collective-permute-start.4 = (bf16[2,32,1280]{2,1,0:T(8,128)(2,1)S(1)}, bf16[2,32,1280]{2,1,0:T(8,128)(2,1)S(1)}, u32[]{:S(2)}, u32[]{:S(2)}) collective-permute-start(bf16[2,32,1280]{2,1,0:T(8,128)(2,1)S(1)} %bitcast.7), channel_id=1, source_target_pairs={{0,16},{8,24},{16,0},{24,8},{1,17},{9,25},{17,1},{25,9},{2,18},{10... | collective-permute-start | bytes 491528 | tf_op jit(solution)/shard_map/ppermute | solution.py:289
  28.7 0.0 copy-done
  28.7 0.0 copy-start.1
  28.7 1.1 %copy-done.1 = bf16[256,1280]{1,0:T(8,128)(2,1)S(1)} copy-done((bf16[256,1280]{1,0:T(8,128)(2,1)S(1)}, bf16[256,1280]{1,0:T(8,128)(2,1)}, u32[]{:S(2)}) %copy-start.1) | copy-done | bytes 655384
  29.8 0.0 copy-start.2
  29.8 1.1 %copy-done.2 = bf16[256,1280]{1,0:T(8,128)(2,1)S(1)} copy-done((bf16[256,1280]{1,0:T(8,128)(2,1)S(1)}, bf16[256,1280]{1,0:T(8,128)(2,1)}, u32[]{:S(2)}) %copy-start.2) | copy-done | bytes 655384
  30.9 0.0 copy-start.3
  30.9 1.1 %copy-done.3 = bf16[256,1280]{1,0:T(8,128)(2,1)S(1)} copy-done((bf16[256,1280]{1,0:T(8,128)(2,1)S(1)}, bf16[256,1280]{1,0:T(8,128)(2,1)}, u32[]{:S(2)}) %copy-start.3) | copy-done | bytes 655384
  32.0 0.9 %shard_map.94 = (bf16[256,1280]{1,0:T(8,128)(2,1)S(1)}, bf16[256,1280]{1,0:T(8,128)(2,1)S(1)}, bf16[256,1280]{1,0:T(8,128)(2,1)S(1)}, bf16[256,1280]{1,0:T(8,128)(2,1)S(1)}) custom-call(bf16[256,1280]{1,0:T(8,128)(2,1)S(1)} %copy-done, bf16[256,1280]{1,0:T(8,128)(2,1)S(1)} %copy-done.1, bf16[256,1280]{1,0:T(8,128)(2,1)S(1)} %copy-done.2, ...), custom_call_target="tpu_custom_call" | custom-call | bytes 5242880 | tf_op jit(solution)/shard_map/pallas_call | solution.py:95
  32.9 0.0 collective-permute-done.6.refs_3_
  32.9 2.8 %collective-permute-done.5.refs_2_ = bf16[2,32,1280]{2,1,0:T(8,128)(2,1)S(1)} collective-permute-done((bf16[2,32,1280]{2,1,0:T(8,128)(2,1)S(1)}, bf16[2,32,1280]{2,1,0:T(8,128)(2,1)S(1)}, u32[]{:S(2)}, u32[]{:S(2)}) %collective-permute-start.5) | collective-permute-done | bytes 163872 | tf_op jit(solution)/shard_map/ppermute | solution.py:289
  35.7 0.0 collective-permute-done.4.refs_1_
  35.7 2.3 %shard_map.95 = (bf16[8,88,128]{2,1,0:T(8,128)(2,1)S(1)}, bf16[8,88,128]{2,1,0:T(8,128)(2,1)S(1)}, bf16[8,88,128]{2,1,0:T(8,128)(2,1)S(1)}, bf16[8,88,128]{2,1,0:T(8,128)(2,1)S(1)}) custom-call(bf16[2,32,1280]{2,1,0:T(8,128)(2,1)S(1)} %bitcast.8, bf16[2,32,1280]{2,1,0:T(8,128)(2,1)S(1)} %collective-permute-done.4.refs_1_, ...), custom_call_target="tpu_custom_call" | custom-call | flops 1006632960 | bytes 5242880 | tf_op jit(solution)/shard_map/pallas_call | solution.py:176
  38.0 0.7 %collective-permute-start.7 = (bf16[8,88,128]{2,1,0:T(8,128)(2,1)S(1)}, bf16[8,88,128]{2,1,0:T(8,128)(2,1)S(1)}, u32[]{:S(2)}, u32[]{:S(2)}) collective-permute-start(bf16[8,88,128]{2,1,0:T(8,128)(2,1)S(1)} %get-tuple-element.39), channel_id=1, source_target_pairs={{0,16},{8,24},{16,0},{24,8},{1,17},{9,25},{17,1},{25,9},{2,18},{10... | collective-permute-start | bytes 540680 | tf_op jit(solution)/shard_map/ppermute | solution.py:289
  38.6 1.2 %collective-permute-start.8 = (bf16[8,88,128]{2,1,0:T(8,128)(2,1)S(1)}, bf16[8,88,128]{2,1,0:T(8,128)(2,1)S(1)}, u32[]{:S(2)}, u32[]{:S(2)}) collective-permute-start(bf16[8,88,128]{2,1,0:T(8,128)(2,1)S(1)} %get-tuple-element.40), channel_id=1, source_target_pairs={{0,24},{8,0},{16,8},{24,16},{1,25},{9,1},{17,9},{25,17},{2,26},{10... | collective-permute-start | bytes 540680 | tf_op jit(solution)/shard_map/ppermute | solution.py:289
  39.8 0.8 %collective-permute-start.9 = (bf16[8,88,128]{2,1,0:T(8,128)(2,1)S(1)}, bf16[8,88,128]{2,1,0:T(8,128)(2,1)S(1)}, u32[]{:S(2)}, u32[]{:S(2)}) collective-permute-start(bf16[8,88,128]{2,1,0:T(8,128)(2,1)S(1)} %get-tuple-element.41), channel_id=1, source_target_pairs={{0,8},{8,16},{16,24},{24,0},{1,9},{9,17},{17,25},{25,1},{2,10},{10... | collective-permute-start | bytes 540680 | tf_op jit(solution)/shard_map/ppermute | solution.py:289
  40.7 4.4 %collective-permute-done.7.refs_1_ = bf16[8,88,128]{2,1,0:T(8,128)(2,1)S(1)} collective-permute-done((bf16[8,88,128]{2,1,0:T(8,128)(2,1)S(1)}, bf16[8,88,128]{2,1,0:T(8,128)(2,1)S(1)}, u32[]{:S(2)}, u32[]{:S(2)}) %collective-permute-start.7) | collective-permute-done | bytes 180256 | tf_op jit(solution)/shard_map/ppermute | solution.py:289
  45.1 0.1 collective-permute-done.8.refs_2_
  45.2 1.8 %collective-permute-done.9.refs_3_ = bf16[8,88,128]{2,1,0:T(8,128)(2,1)S(1)} collective-permute-done((bf16[8,88,128]{2,1,0:T(8,128)(2,1)S(1)}, bf16[8,88,128]{2,1,0:T(8,128)(2,1)S(1)}, u32[]{:S(2)}, u32[]{:S(2)}) %collective-permute-start.9) | collective-permute-done | bytes 180256 | tf_op jit(solution)/shard_map/ppermute | solution.py:289
  47.0 0.7 %shard_map.96 = bf16[8,88,128]{2,1,0:T(8,128)(2,1)S(1)} custom-call(bf16[8,88,128]{2,1,0:T(8,128)(2,1)S(1)} %get-tuple-element.38.refs_0_, bf16[8,88,128]{2,1,0:T(8,128)(2,1)S(1)} %collective-permute-done.7.refs_1_, bf16[8,88,128]{2,1,0:T(8,128)(2,1)S(1)} %collective-permute-done.8.refs_2_, bf16[8,88,128]{2,1,0:T(8,128)(2,1)S(1)} %collective-permute-done.9.refs_3_), custom_call_target="tpu_custom_call" | custom-call | tf_op jit(solution)/shard_map/pallas_call | solution.py:239
  47.7 11.3 %all_to_all.11.refs_0_ = bf16[8,88,128]{2,1,0:T(8,128)(2,1)S(1)} all-to-all(bf16[8,88,128]{2,1,0:T(8,128)(2,1)S(1)} %shard_map.96), channel_id=1, replica_groups={{128,160,192,224,0,32,64,96},{129,161,193,225,1,33,65,97},{130,162,194,..., dimensions={0} | all-to-all | bytes 360448 | tf_op jit(solution)/shard_map/all_to_all | solution.py:308
  59.0 1.0 %shard_map.97 = (f32[4,1280]{1,0:T(4,128)}, f32[4,1280]{1,0:T(4,128)}, f32[4,10]{1,0:T(4,128)}, f32[4,10]{1,0:T(4,128)}) custom-call(bf16[8,88,128]{2,1,0:T(8,128)(2,1)S(1)} %all_to_all.11.refs_0_), custom_call_target="tpu_custom_call" | custom-call | tf_op jit(solution)/shard_map/pallas_call | solution.py:277
  (2 shorter events, 0.0 us)
Async XLA Ops:
  0.6 28.1 %copy-start = (bf16[256,1280]{1,0:T(8,128)(2,1)S(1)}, bf16[256,1280]{1,0:T(8,128)(2,1)}, u32[]{:S(2)}) copy-start(bf16[256,1280]{1,0:T(8,128)(2,1)} %refs_0_) | copy-start | bytes 1966084
  0.6 22.7 %collective-permute-start = (bf16[256,1280]{1,0:T(8,128)(2,1)}, bf16[256,1280]{1,0:T(8,128)(2,1)S(1)}, u32[]{:S(2)}, u32[]{:S(2)}) collective-permute-start(bf16[256,1280]{1,0:T(8,128)(2,1)} %refs_0_), channel_id=1, source_target_pairs={{0,4},{4,0},{1,5},{5,1},{2,6},{6,2},{3,7},{7,3},{8,12},{12,8},{9,1... | collective-permute-start | bytes 1966088 | tf_op jit(solution)/shard_map/ppermute | solution.py:298
  0.7 22.7 %collective-permute-start.1 = (bf16[256,1280]{1,0:T(8,128)(2,1)}, bf16[256,1280]{1,0:T(8,128)(2,1)S(1)}, u32[]{:S(2)}, u32[]{:S(2)}) collective-permute-start(bf16[256,1280]{1,0:T(8,128)(2,1)} %refs_1_), channel_id=1, source_target_pairs={{0,4},{4,0},{1,5},{5,1},{2,6},{6,2},{3,7},{7,3},{8,12},{12,8},{9,1... | collective-permute-start | bytes 1966088 | tf_op jit(solution)/shard_map/ppermute | solution.py:298
  1.2 22.2 %collective-permute-start.2 = (bf16[256,1280]{1,0:T(8,128)(2,1)}, bf16[256,1280]{1,0:T(8,128)(2,1)S(1)}, u32[]{:S(2)}, u32[]{:S(2)}) collective-permute-start(bf16[256,1280]{1,0:T(8,128)(2,1)} %refs_2_), channel_id=1, source_target_pairs={{0,4},{4,0},{1,5},{5,1},{2,6},{6,2},{3,7},{7,3},{8,12},{12,8},{9,1... | collective-permute-start | bytes 1966088 | tf_op jit(solution)/shard_map/ppermute | solution.py:298
  1.3 22.1 %collective-permute-start.3 = (bf16[256,1280]{1,0:T(8,128)(2,1)}, bf16[256,1280]{1,0:T(8,128)(2,1)S(1)}, u32[]{:S(2)}, u32[]{:S(2)}) collective-permute-start(bf16[256,1280]{1,0:T(8,128)(2,1)} %refs_3_), channel_id=1, source_target_pairs={{0,4},{4,0},{1,5},{5,1},{2,6},{6,2},{3,7},{7,3},{8,12},{12,8},{9,1... | collective-permute-start | bytes 1966088 | tf_op jit(solution)/shard_map/ppermute | solution.py:298
  23.4 9.5 %collective-permute-start.6 = (bf16[2,32,1280]{2,1,0:T(8,128)(2,1)S(1)}, bf16[2,32,1280]{2,1,0:T(8,128)(2,1)S(1)}, u32[]{:S(2)}, u32[]{:S(2)}) collective-permute-start(bf16[2,32,1280]{2,1,0:T(8,128)(2,1)S(1)} %bitcast.5), channel_id=1, source_target_pairs={{0,24},{8,0},{16,8},{24,16},{1,25},{9,1},{17,9},{25,17},{2,26},{10... | collective-permute-start | bytes 491528 | tf_op jit(solution)/shard_map/ppermute | solution.py:289
  26.5 9.2 %collective-permute-start.5 = (bf16[2,32,1280]{2,1,0:T(8,128)(2,1)S(1)}, bf16[2,32,1280]{2,1,0:T(8,128)(2,1)S(1)}, u32[]{:S(2)}, u32[]{:S(2)}) collective-permute-start(bf16[2,32,1280]{2,1,0:T(8,128)(2,1)S(1)} %bitcast.6), channel_id=1, source_target_pairs={{0,8},{8,16},{16,24},{24,0},{1,9},{9,17},{17,25},{25,1},{2,10},{10... | collective-permute-start | bytes 491528 | tf_op jit(solution)/shard_map/ppermute | solution.py:289
  26.5 9.2 %collective-permute-start.4 = (bf16[2,32,1280]{2,1,0:T(8,128)(2,1)S(1)}, bf16[2,32,1280]{2,1,0:T(8,128)(2,1)S(1)}, u32[]{:S(2)}, u32[]{:S(2)}) collective-permute-start(bf16[2,32,1280]{2,1,0:T(8,128)(2,1)S(1)} %bitcast.7), channel_id=1, source_target_pairs={{0,16},{8,24},{16,0},{24,8},{1,17},{9,25},{17,1},{25,9},{2,18},{10... | collective-permute-start | bytes 491528 | tf_op jit(solution)/shard_map/ppermute | solution.py:289
  28.7 1.1 %copy-start.1 = (bf16[256,1280]{1,0:T(8,128)(2,1)S(1)}, bf16[256,1280]{1,0:T(8,128)(2,1)}, u32[]{:S(2)}) copy-start(bf16[256,1280]{1,0:T(8,128)(2,1)} %refs_1_) | copy-start | bytes 1966084
  29.8 1.1 %copy-start.2 = (bf16[256,1280]{1,0:T(8,128)(2,1)S(1)}, bf16[256,1280]{1,0:T(8,128)(2,1)}, u32[]{:S(2)}) copy-start(bf16[256,1280]{1,0:T(8,128)(2,1)} %refs_2_) | copy-start | bytes 1966084
  30.9 1.1 %copy-start.3 = (bf16[256,1280]{1,0:T(8,128)(2,1)S(1)}, bf16[256,1280]{1,0:T(8,128)(2,1)}, u32[]{:S(2)}) copy-start(bf16[256,1280]{1,0:T(8,128)(2,1)} %refs_3_) | copy-start | bytes 1966084
  38.0 7.1 %collective-permute-start.7 = (bf16[8,88,128]{2,1,0:T(8,128)(2,1)S(1)}, bf16[8,88,128]{2,1,0:T(8,128)(2,1)S(1)}, u32[]{:S(2)}, u32[]{:S(2)}) collective-permute-start(bf16[8,88,128]{2,1,0:T(8,128)(2,1)S(1)} %get-tuple-element.39), channel_id=1, source_target_pairs={{0,16},{8,24},{16,0},{24,8},{1,17},{9,25},{17,1},{25,9},{2,18},{10... | collective-permute-start | bytes 540680 | tf_op jit(solution)/shard_map/ppermute | solution.py:289
  38.6 6.6 %collective-permute-start.8 = (bf16[8,88,128]{2,1,0:T(8,128)(2,1)S(1)}, bf16[8,88,128]{2,1,0:T(8,128)(2,1)S(1)}, u32[]{:S(2)}, u32[]{:S(2)}) collective-permute-start(bf16[8,88,128]{2,1,0:T(8,128)(2,1)S(1)} %get-tuple-element.40), channel_id=1, source_target_pairs={{0,24},{8,0},{16,8},{24,16},{1,25},{9,1},{17,9},{25,17},{2,26},{10... | collective-permute-start | bytes 540680 | tf_op jit(solution)/shard_map/ppermute | solution.py:289
  39.8 7.1 %collective-permute-start.9 = (bf16[8,88,128]{2,1,0:T(8,128)(2,1)S(1)}, bf16[8,88,128]{2,1,0:T(8,128)(2,1)S(1)}, u32[]{:S(2)}, u32[]{:S(2)}) collective-permute-start(bf16[8,88,128]{2,1,0:T(8,128)(2,1)S(1)} %get-tuple-element.41), channel_id=1, source_target_pairs={{0,8},{8,16},{16,24},{24,0},{1,9},{9,17},{17,25},{25,1},{2,10},{10... | collective-permute-start | bytes 540680 | tf_op jit(solution)/shard_map/ppermute | solution.py:289

commit v7 on v6

--- a/solution.py
+++ b/solution.py
@@ -157,25 +157,26 @@
         pending = None
         span = tile.shape[1]
         start = (head // 2) * span
+        rows_each = heads * span // 2
         for i, ref in enumerate(outs):
-            ref[:, start : start + span, :] = tile[i * owners : (i + 1) * owners]
-    stats = twice(encode(lses, lts, heads).reshape(groups * owners, per_owner, LANES))
-    span = stats.shape[1]
+            for owner in range(owners):
+                place = owner * rows_each + start
+                ref[place : place + span, :] = tile[i * owners + owner]
+    stats = encode(lses, lts, heads).astype(jnp.bfloat16)
     for i, ref in enumerate(outs):
-        part = stats[i * owners : (i + 1) * owners]
-        ref[:, heads * span : (heads + 1) * span, :] = part.astype(jnp.bfloat16)
+        ref[ref.shape[0] - rows :, :] = stats[i * rows : (i + 1) * rows]
 
 
 def attend(windows, own, other, owners):
     arrays, rows, width = windows[0].shape
     groups = len(windows)
     heads = width // HD
-    message_rows = (heads + 1) * 2 * (rows // owners)
+    message_rows = (2 * heads + 1) * rows
     vmem = pl.BlockSpec(memory_space=pltpu.VMEM)
     keys = own[0].shape[0] * 2
     return pl.pallas_call(
         lambda *refs: attend_kernel(owners, groups, *refs),
-        out_shape=[jax.ShapeDtypeStruct((owners, message_rows, HD), jnp.bfloat16)] * groups,
+        out_shape=[jax.ShapeDtypeStruct((message_rows, HD), jnp.bfloat16)] * groups,
         in_specs=[vmem] * (groups + 8),
         out_specs=[vmem] * groups,
         compiler_params=pltpu.CompilerParams(vmem_limit_bytes=VMEM_LIMIT),
@@ -211,15 +212,19 @@
     sources, out_ref = refs[:-1], refs[-1]
     owners, message_rows, _ = out_ref.shape
     span = message_rows // (heads + 1)
+    rows_each = heads * span
+    stats = [ref[owners * rows_each :, :].astype(jnp.float32) for ref in sources]
     scales, shifts, lse, lt = merge_weights(
-        [ref[:, heads * span : (heads + 1) * span, :] for ref in sources], heads
+        [twice(x.reshape(owners, span // 2, LANES)) for x in stats], heads
     )
     for pair in range(heads // 2):
         head = 2 * pair
         start = head * span
         out = tangent = 0.0
         for ref, scale, shift in zip(sources, scales, shifts):
-            block = ref[:, start : start + 2 * span, :].astype(jnp.float32)
+            places = [owner * rows_each + start for owner in range(owners)]
+            block = jnp.stack([ref[place : place + 2 * span, :] for place in places])
+            block = block.astype(jnp.float32)
             values, tangents = block[:, :span], block[:, span:]
             scale = scale[:, :, head : head + 1]
             out += values * scale
@@ -234,11 +239,12 @@
         out_ref[slot, heads * span : (heads + 1) * span, :] = stats[owner]
 
 
-def merge_group(messages, heads):
+def merge_group(messages, heads, owners):
     vmem = pl.BlockSpec(memory_space=pltpu.VMEM)
+    rows = messages[0].shape[0] // owners // (2 * heads + 1) * 2 * (heads + 1)
     return pl.pallas_call(
         lambda *refs: merge_group_kernel(heads, *refs),
-        out_shape=jax.ShapeDtypeStruct(messages[0].shape, jnp.bfloat16),
+        out_shape=jax.ShapeDtypeStruct((owners, rows, HD), jnp.bfloat16),
         in_specs=[vmem] * len(messages),
         out_specs=vmem,
         compiler_params=pltpu.CompilerParams(vmem_limit_bytes=VMEM_LIMIT),
@@ -304,7 +310,7 @@
     windows = [window] + [shift(window, step) for step in steps]
     messages = attend(windows, own, other, owners)
     messages = [messages[0]] + [shift(m, -step) for m, step in zip(messages[1:], steps)]
-    message = merge_group(messages, heads)
+    message = merge_group(messages, heads, owners)
     message = lax.all_to_all(
         message, "z", split_axis=0, concat_axis=0, tiled=True, axis_index_groups=[list(ORDER)]
     )

time: 60.6 us -> 60.5 us (level)
  transfers between devices with their start and end apart: 10 -> 10, of which waited for: 4 -> 3; matrix products, arithmetic and copies ran while one was open for 1% -> 1% of each run, Pallas kernels for 2% -> 2%
where the time goes in v7:
time: 60.5 us; the launch traced here: 59.8 us
  blocking collectives  32.1 us (53%)
  starting transfers between devices  9.08 us (15%)
  waiting for transfers between devices  8.96 us (15%)
  Pallas kernels  4.86 us (8%)
  local copies, waits for them, and re-layouts  3.28 us (5%)
  other arithmetic  0.8 us (1%)
  between operations  0.73 us (1%)
    all_to_all x1, blocking collectives, per_device(): lax.all_to_all(row, ('z', 'x'), split_axis=0, concat_axis=0, tiled=True)  20.8 us
    all_to_all x1, blocking collectives, per_device(): lax.all_to_all(message, 'z', split_axis=0, concat_axis=0, tiled=True, axi...  11.3 us
    ppermute x6, waiting for transfers between devices, shift(): lax.ppermute(array, 'y', [(i, (i + step) % count) for i in range(count)])  8.95 us
    ppermute x6, starting transfers between devices, shift(): lax.ppermute(array, 'y', [(i, (i + step) % count) for i in range(count)])  7.98 us
    unnamed x8, local copies, waits for them, and re-layouts  3.27 us
    pallas_call x1, Pallas kernels, attend(): pl.pallas_call(lambda *refs: attend_kernel(owners, groups, *refs), out_sh...  2.24 us
  transfers between devices with their start and end apart: 10, of which 3 were waited for; matrix products, arithmetic and copies ran while one was open for 1% of the time, Pallas kernels for 2%

profile of v7, /device:TPU:2, one launch (start us, length us, event | category | flops | bytes accessed | tf_op | source)
XLA Modules:
  0.0 59.8 jit_solution(2986210283393686445)
XLA Ops:
  0.6 0.0 copy-start
  0.6 0.1 collective-permute-start
  0.7 0.5 collective-permute-start.1
  1.2 0.1 collective-permute-start.2
  1.3 0.4 collective-permute-start.3
  1.8 0.8 %pad_maximum_fusion.refs_0_ = bf16[2,5120]{1,0:T(2,128)(2,1)S(1)} fusion(bf16[1,5120]{1,0:T(2,128)(2,1)} %param.7, bf16[1,5120]{1,0:T(2,128)(2,1)} %param.6), kind=kLoop, calls=%fused_computation.1 | loop fusion | flops 40960 | bytes 40960 | tf_op jit(solution)/shard_map/concatenate | solution.py:302
  2.6 20.8 %all_to_all.10 = bf16[32,2,1280]{2,1,0:T(2,128)(2,1)S(1)} all-to-all(bf16[32,2,1280]{2,1,0:T(2,128)(2,1)S(1)} %shard_map.93), channel_id=1, replica_groups=mesh['z'=8,'y'=4,'core'=2,'x'=4] {'z','x'}, dimensions={0} | all-to-all | bytes 327680 | tf_op jit(solution)/shard_map/all_to_all | solution.py:305
  23.4 0.0 collective-permute-done.refs_8_
  23.4 0.0 collective-permute-done.1.refs_9_
  23.4 0.0 collective-permute-done.2.refs_10_
  23.4 0.0 collective-permute-done.3.refs_11_
  23.4 3.1 %collective-permute-start.6 = (bf16[2,32,1280]{2,1,0:T(8,128)(2,1)S(1)}, bf16[2,32,1280]{2,1,0:T(8,128)(2,1)S(1)}, u32[]{:S(2)}, u32[]{:S(2)}) collective-permute-start(bf16[2,32,1280]{2,1,0:T(8,128)(2,1)S(1)} %bitcast.5), channel_id=1, source_target_pairs={{0,24},{8,0},{16,8},{24,16},{1,25},{9,1},{17,9},{25,17},{2,26},{10... | collective-permute-start | bytes 491528 | tf_op jit(solution)/shard_map/ppermute | solution.py:295
  26.5 0.0 collective-permute-start.5
  26.5 2.2 %collective-permute-start.4 = (bf16[2,32,1280]{2,1,0:T(8,128)(2,1)S(1)}, bf16[2,32,1280]{2,1,0:T(8,128)(2,1)S(1)}, u32[]{:S(2)}, u32[]{:S(2)}) collective-permute-start(bf16[2,32,1280]{2,1,0:T(8,128)(2,1)S(1)} %bitcast.7), channel_id=1, source_target_pairs={{0,16},{8,24},{16,0},{24,8},{1,17},{9,25},{17,1},{25,9},{2,18},{10... | collective-permute-start | bytes 491528 | tf_op jit(solution)/shard_map/ppermute | solution.py:295
  28.7 0.0 copy-done
  28.7 0.0 copy-start.1
  28.7 1.1 %copy-done.1 = bf16[256,1280]{1,0:T(8,128)(2,1)S(1)} copy-done((bf16[256,1280]{1,0:T(8,128)(2,1)S(1)}, bf16[256,1280]{1,0:T(8,128)(2,1)}, u32[]{:S(2)}) %copy-start.1) | copy-done | bytes 655384
  29.8 0.0 copy-start.2
  29.8 1.1 %copy-done.2 = bf16[256,1280]{1,0:T(8,128)(2,1)S(1)} copy-done((bf16[256,1280]{1,0:T(8,128)(2,1)S(1)}, bf16[256,1280]{1,0:T(8,128)(2,1)}, u32[]{:S(2)}) %copy-start.2) | copy-done | bytes 655384
  30.9 0.0 copy-start.3
  30.9 1.1 %copy-done.3 = bf16[256,1280]{1,0:T(8,128)(2,1)S(1)} copy-done((bf16[256,1280]{1,0:T(8,128)(2,1)S(1)}, bf16[256,1280]{1,0:T(8,128)(2,1)}, u32[]{:S(2)}) %copy-start.3) | copy-done | bytes 655384
  32.0 0.9 %shard_map.94 = (bf16[256,1280]{1,0:T(8,128)(2,1)S(1)}, bf16[256,1280]{1,0:T(8,128)(2,1)S(1)}, bf16[256,1280]{1,0:T(8,128)(2,1)S(1)}, bf16[256,1280]{1,0:T(8,128)(2,1)S(1)}) custom-call(bf16[256,1280]{1,0:T(8,128)(2,1)S(1)} %copy-done, bf16[256,1280]{1,0:T(8,128)(2,1)S(1)} %copy-done.1, bf16[256,1280]{1,0:T(8,128)(2,1)S(1)} %copy-done.2, ...), custom_call_target="tpu_custom_call" | custom-call | bytes 5242880 | tf_op jit(solution)/shard_map/pallas_call | solution.py:95
  32.9 0.0 collective-permute-done.6.refs_3_
  32.9 2.8 %collective-permute-done.5.refs_2_ = bf16[2,32,1280]{2,1,0:T(8,128)(2,1)S(1)} collective-permute-done((bf16[2,32,1280]{2,1,0:T(8,128)(2,1)S(1)}, bf16[2,32,1280]{2,1,0:T(8,128)(2,1)S(1)}, u32[]{:S(2)}, u32[]{:S(2)}) %collective-permute-start.5) | collective-permute-done | bytes 163872 | tf_op jit(solution)/shard_map/ppermute | solution.py:295
  35.7 0.0 collective-permute-done.4.refs_1_
  35.7 2.2 %shard_map.95 = (bf16[672,128]{1,0:T(8,128)(2,1)S(1)}, bf16[672,128]{1,0:T(8,128)(2,1)S(1)}, bf16[672,128]{1,0:T(8,128)(2,1)S(1)}, bf16[672,128]{1,0:T(8,128)(2,1)S(1)}) custom-call(bf16[2,32,1280]{2,1,0:T(8,128)(2,1)S(1)} %bitcast.8, bf16[2,32,1280]{2,1,0:T(8,128)(2,1)S(1)} %collective-permute-done.4.refs_1_, ...), custom_call_target="tpu_custom_call" | custom-call | flops 1006632960 | bytes 5242880 | tf_op jit(solution)/shard_map/pallas_call | solution.py:177
  38.0 0.7 %collective-permute-start.7 = (bf16[672,128]{1,0:T(8,128)(2,1)S(1)}, bf16[672,128]{1,0:T(8,128)(2,1)S(1)}, u32[]{:S(2)}, u32[]{:S(2)}) collective-permute-start(bf16[672,128]{1,0:T(8,128)(2,1)S(1)} %get-tuple-element.39), channel_id=1, source_target_pairs={{0,16},{8,24},{16,0},{24,8},{1,17},{9,25},{17,1},{25,9},{2,18},{10... | collective-permute-start | bytes 516104 | tf_op jit(solution)/shard_map/ppermute | solution.py:295
  38.6 1.2 %collective-permute-start.8 = (bf16[672,128]{1,0:T(8,128)(2,1)S(1)}, bf16[672,128]{1,0:T(8,128)(2,1)S(1)}, u32[]{:S(2)}, u32[]{:S(2)}) collective-permute-start(bf16[672,128]{1,0:T(8,128)(2,1)S(1)} %get-tuple-element.40), channel_id=1, source_target_pairs={{0,24},{8,0},{16,8},{24,16},{1,25},{9,1},{17,9},{25,17},{2,26},{10... | collective-permute-start | bytes 516104 | tf_op jit(solution)/shard_map/ppermute | solution.py:295
  39.8 0.8 %collective-permute-start.9 = (bf16[672,128]{1,0:T(8,128)(2,1)S(1)}, bf16[672,128]{1,0:T(8,128)(2,1)S(1)}, u32[]{:S(2)}, u32[]{:S(2)}) collective-permute-start(bf16[672,128]{1,0:T(8,128)(2,1)S(1)} %get-tuple-element.41), channel_id=1, source_target_pairs={{0,8},{8,16},{16,24},{24,0},{1,9},{9,17},{17,25},{25,1},{2,10},{10... | collective-permute-start | bytes 516104 | tf_op jit(solution)/shard_map/ppermute | solution.py:295
  40.6 4.3 %collective-permute-done.7.refs_1_ = bf16[672,128]{1,0:T(8,128)(2,1)S(1)} collective-permute-done((bf16[672,128]{1,0:T(8,128)(2,1)S(1)}, bf16[672,128]{1,0:T(8,128)(2,1)S(1)}, u32[]{:S(2)}, u32[]{:S(2)}) %collective-permute-start.7) | collective-permute-done | bytes 172064 | tf_op jit(solution)/shard_map/ppermute | solution.py:295
  45.0 0.0 collective-permute-done.8.refs_2_
  45.0 1.8 %collective-permute-done.9.refs_3_ = bf16[672,128]{1,0:T(8,128)(2,1)S(1)} collective-permute-done((bf16[672,128]{1,0:T(8,128)(2,1)S(1)}, bf16[672,128]{1,0:T(8,128)(2,1)S(1)}, u32[]{:S(2)}, u32[]{:S(2)}) %collective-permute-start.9) | collective-permute-done | bytes 172064 | tf_op jit(solution)/shard_map/ppermute | solution.py:295
  46.8 0.7 %shard_map.96 = bf16[8,88,128]{2,1,0:T(8,128)(2,1)S(1)} custom-call(bf16[672,128]{1,0:T(8,128)(2,1)S(1)} %get-tuple-element.38.refs_0_, bf16[672,128]{1,0:T(8,128)(2,1)S(1)} %collective-permute-done.7.refs_1_, bf16[672,128]{1,0:T(8,128)(2,1)S(1)} %collective-permute-done.8.refs_2_, bf16[672,128]{1,0:T(8,128)(2,1)S(1)} %collective-permute-done.9.refs_3_), custom_call_target="tpu_custom_call" | custom-call | tf_op jit(solution)/shard_map/pallas_call | solution.py:245
  47.5 11.3 %all_to_all.11.refs_0_ = bf16[8,88,128]{2,1,0:T(8,128)(2,1)S(1)} all-to-all(bf16[8,88,128]{2,1,0:T(8,128)(2,1)S(1)} %shard_map.96), channel_id=1, replica_groups={{128,160,192,224,0,32,64,96},{129,161,193,225,1,33,65,97},{130,162,194,..., dimensions={0} | all-to-all | bytes 360448 | tf_op jit(solution)/shard_map/all_to_all | solution.py:314
  58.8 1.0 %shard_map.97 = (f32[4,1280]{1,0:T(4,128)}, f32[4,1280]{1,0:T(4,128)}, f32[4,10]{1,0:T(4,128)}, f32[4,10]{1,0:T(4,128)}) custom-call(bf16[8,88,128]{2,1,0:T(8,128)(2,1)S(1)} %all_to_all.11.refs_0_), custom_call_target="tpu_custom_call" | custom-call | tf_op jit(solution)/shard_map/pallas_call | solution.py:283
  (2 shorter events, 0.0 us)
Async XLA Ops:
  0.6 28.1 %copy-start = (bf16[256,1280]{1,0:T(8,128)(2,1)S(1)}, bf16[256,1280]{1,0:T(8,128)(2,1)}, u32[]{:S(2)}) copy-start(bf16[256,1280]{1,0:T(8,128)(2,1)} %refs_0_) | copy-start | bytes 1966084
  0.6 22.7 %collective-permute-start = (bf16[256,1280]{1,0:T(8,128)(2,1)}, bf16[256,1280]{1,0:T(8,128)(2,1)S(1)}, u32[]{:S(2)}, u32[]{:S(2)}) collective-permute-start(bf16[256,1280]{1,0:T(8,128)(2,1)} %refs_0_), channel_id=1, source_target_pairs={{0,4},{4,0},{1,5},{5,1},{2,6},{6,2},{3,7},{7,3},{8,12},{12,8},{9,1... | collective-permute-start | bytes 1966088 | tf_op jit(solution)/shard_map/ppermute | solution.py:304
  0.7 22.7 %collective-permute-start.1 = (bf16[256,1280]{1,0:T(8,128)(2,1)}, bf16[256,1280]{1,0:T(8,128)(2,1)S(1)}, u32[]{:S(2)}, u32[]{:S(2)}) collective-permute-start(bf16[256,1280]{1,0:T(8,128)(2,1)} %refs_1_), channel_id=1, source_target_pairs={{0,4},{4,0},{1,5},{5,1},{2,6},{6,2},{3,7},{7,3},{8,12},{12,8},{9,1... | collective-permute-start | bytes 1966088 | tf_op jit(solution)/shard_map/ppermute | solution.py:304
  1.2 22.2 %collective-permute-start.2 = (bf16[256,1280]{1,0:T(8,128)(2,1)}, bf16[256,1280]{1,0:T(8,128)(2,1)S(1)}, u32[]{:S(2)}, u32[]{:S(2)}) collective-permute-start(bf16[256,1280]{1,0:T(8,128)(2,1)} %refs_2_), channel_id=1, source_target_pairs={{0,4},{4,0},{1,5},{5,1},{2,6},{6,2},{3,7},{7,3},{8,12},{12,8},{9,1... | collective-permute-start | bytes 1966088 | tf_op jit(solution)/shard_map/ppermute | solution.py:304
  1.3 22.1 %collective-permute-start.3 = (bf16[256,1280]{1,0:T(8,128)(2,1)}, bf16[256,1280]{1,0:T(8,128)(2,1)S(1)}, u32[]{:S(2)}, u32[]{:S(2)}) collective-permute-start(bf16[256,1280]{1,0:T(8,128)(2,1)} %refs_3_), channel_id=1, source_target_pairs={{0,4},{4,0},{1,5},{5,1},{2,6},{6,2},{3,7},{7,3},{8,12},{12,8},{9,1... | collective-permute-start | bytes 1966088 | tf_op jit(solution)/shard_map/ppermute | solution.py:304
  23.4 9.5 %collective-permute-start.6 = (bf16[2,32,1280]{2,1,0:T(8,128)(2,1)S(1)}, bf16[2,32,1280]{2,1,0:T(8,128)(2,1)S(1)}, u32[]{:S(2)}, u32[]{:S(2)}) collective-permute-start(bf16[2,32,1280]{2,1,0:T(8,128)(2,1)S(1)} %bitcast.5), channel_id=1, source_target_pairs={{0,24},{8,0},{16,8},{24,16},{1,25},{9,1},{17,9},{25,17},{2,26},{10... | collective-permute-start | bytes 491528 | tf_op jit(solution)/shard_map/ppermute | solution.py:295
  26.5 9.2 %collective-permute-start.5 = (bf16[2,32,1280]{2,1,0:T(8,128)(2,1)S(1)}, bf16[2,32,1280]{2,1,0:T(8,128)(2,1)S(1)}, u32[]{:S(2)}, u32[]{:S(2)}) collective-permute-start(bf16[2,32,1280]{2,1,0:T(8,128)(2,1)S(1)} %bitcast.6), channel_id=1, source_target_pairs={{0,8},{8,16},{16,24},{24,0},{1,9},{9,17},{17,25},{25,1},{2,10},{10... | collective-permute-start | bytes 491528 | tf_op jit(solution)/shard_map/ppermute | solution.py:295
  26.5 9.2 %collective-permute-start.4 = (bf16[2,32,1280]{2,1,0:T(8,128)(2,1)S(1)}, bf16[2,32,1280]{2,1,0:T(8,128)(2,1)S(1)}, u32[]{:S(2)}, u32[]{:S(2)}) collective-permute-start(bf16[2,32,1280]{2,1,0:T(8,128)(2,1)S(1)} %bitcast.7), channel_id=1, source_target_pairs={{0,16},{8,24},{16,0},{24,8},{1,17},{9,25},{17,1},{25,9},{2,18},{10... | collective-permute-start | bytes 491528 | tf_op jit(solution)/shard_map/ppermute | solution.py:295
  28.7 1.1 %copy-start.1 = (bf16[256,1280]{1,0:T(8,128)(2,1)S(1)}, bf16[256,1280]{1,0:T(8,128)(2,1)}, u32[]{:S(2)}) copy-start(bf16[256,1280]{1,0:T(8,128)(2,1)} %refs_1_) | copy-start | bytes 1966084
  29.8 1.1 %copy-start.2 = (bf16[256,1280]{1,0:T(8,128)(2,1)S(1)}, bf16[256,1280]{1,0:T(8,128)(2,1)}, u32[]{:S(2)}) copy-start(bf16[256,1280]{1,0:T(8,128)(2,1)} %refs_2_) | copy-start | bytes 1966084
  30.9 1.1 %copy-start.3 = (bf16[256,1280]{1,0:T(8,128)(2,1)S(1)}, bf16[256,1280]{1,0:T(8,128)(2,1)}, u32[]{:S(2)}) copy-start(bf16[256,1280]{1,0:T(8,128)(2,1)} %refs_3_) | copy-start | bytes 1966084
  38.0 7.0 %collective-permute-start.7 = (bf16[672,128]{1,0:T(8,128)(2,1)S(1)}, bf16[672,128]{1,0:T(8,128)(2,1)S(1)}, u32[]{:S(2)}, u32[]{:S(2)}) collective-permute-start(bf16[672,128]{1,0:T(8,128)(2,1)S(1)} %get-tuple-element.39), channel_id=1, source_target_pairs={{0,16},{8,24},{16,0},{24,8},{1,17},{9,25},{17,1},{25,9},{2,18},{10... | collective-permute-start | bytes 516104 | tf_op jit(solution)/shard_map/ppermute | solution.py:295
  38.6 6.4 %collective-permute-start.8 = (bf16[672,128]{1,0:T(8,128)(2,1)S(1)}, bf16[672,128]{1,0:T(8,128)(2,1)S(1)}, u32[]{:S(2)}, u32[]{:S(2)}) collective-permute-start(bf16[672,128]{1,0:T(8,128)(2,1)S(1)} %get-tuple-element.40), channel_id=1, source_target_pairs={{0,24},{8,0},{16,8},{24,16},{1,25},{9,1},{17,9},{25,17},{2,26},{10... | collective-permute-start | bytes 516104 | tf_op jit(solution)/shard_map/ppermute | solution.py:295
  39.8 7.0 %collective-permute-start.9 = (bf16[672,128]{1,0:T(8,128)(2,1)S(1)}, bf16[672,128]{1,0:T(8,128)(2,1)S(1)}, u32[]{:S(2)}, u32[]{:S(2)}) collective-permute-start(bf16[672,128]{1,0:T(8,128)(2,1)S(1)} %get-tuple-element.41), channel_id=1, source_target_pairs={{0,8},{8,16},{16,24},{24,0},{1,9},{9,17},{17,25},{25,1},{2,10},{10... | collective-permute-start | bytes 516104 | tf_op jit(solution)/shard_map/ppermute | solution.py:295
